TPU v7x, 256 devices: a whole 4x4x8 slice. The times are simulated.
256 devices in a mesh: row: 32 (over z, y), col: 8 (over x, core).
Axes of the slice: x: 4, y: 4, z: 8, core: 2. Of those that a mesh axis runs over, the one named last changes fastest.
Arguments:
- tokens: bfloat16 [4096, 5120], P('row', 'col'), may hold values from -6 to 6
- target: bfloat16 [4096, 5120], P('row', 'col'), may hold values from -6 to 6
- w_gate: bfloat16 [5120, 13824], P('col', 'row'), may hold values from -0.078125 to 0.078125
- w_up: bfloat16 [5120, 13824], P('col', 'row'), may hold values from -0.078125 to 0.078125
- w_down: bfloat16 [13824, 5120], P('row', 'col'), may hold values from -0.0546875 to 0.0546875
- factor_u: bfloat16 [5120, 256], P('col'), may hold values from -0.078125 to 0.078125
- factor_v: bfloat16 [256, 13824], P(None, 'row'), may hold values from -3 to 3
Outputs:
- mixed: bfloat16 [4096, 5120], P('row', 'col')
- fitness: float32 [64], replicated
- update: float32 [5120, 13824], P('col', 'row')
All inputs are finite; a program needn't handle non-finite values.
Results may differ from a plain program's by a relative error of at most 0.0049.
Values may be sent and summed in bfloat16 or wider, within the bound.
No kernel may reach another device: no remote copies, remote signals or barrier semaphores. Data moves between devices by JAX's collectives and lax.ppermute only.
A program may use at most 128 MiB of HBM per device.

v0:
```python
import math

import jax
import jax.numpy as jnp
from jax import lax
from jax.sharding import PartitionSpec as P

D = 5120
RANK = 4
SEQ = 64


sigma_scale = 0.5


def apply_factors(low_three, v_three):
    return jnp.einsum("psr,prf->psf", low_three, v_three, precision=lax.Precision.HIGHEST)


def body(tokens, target, w_gate, w_up, w_down, factor_u, factor_v):
    dev_rows, dev_feat = tokens.shape
    members = factor_u.shape[1] // RANK
    units = w_up.shape[1]
    every = lax.all_gather(tokens, "row", axis=0, tiled=True)
    total_rows = every.shape[0]
    gate_part = jnp.dot(every, w_gate, preferred_element_type=jnp.float32)
    up_part = jnp.dot(every, w_up, preferred_element_type=jnp.float32)
    grouped = every.reshape(members, SEQ, dev_feat)
    u_three = factor_u.reshape(dev_feat, members, RANK)
    v_three = factor_v.reshape(members, RANK, units).astype(jnp.float32)
    low_part = jnp.einsum("psd,dpr->psr", grouped, u_three, preferred_element_type=jnp.float32)
    up_part = up_part + sigma_scale * apply_factors(low_part, v_three).reshape(total_rows, units)
    gate, up = (
        lax.psum_scatter(gate_part, "col", scatter_dimension=0, tiled=True),
        lax.psum_scatter(up_part, "col", scatter_dimension=0, tiled=True),
    )
    hidden = (jax.nn.silu(gate) * up).astype(jnp.bfloat16)
    hidden_all = lax.all_gather(hidden, "col", axis=0, tiled=True)
    out = lax.psum_scatter(
        jnp.dot(hidden_all, w_down, preferred_element_type=jnp.float32),
        "row",
        scatter_dimension=0,
        tiled=True,
    )
    mixed = out.astype(jnp.bfloat16)
    local_members = dev_rows // SEQ
    prod = (out * target.astype(jnp.float32)).reshape(local_members, SEQ * dev_feat)
    score = jnp.sum(prod, axis=1) / math.sqrt(SEQ * D)
    placed = lax.dynamic_update_slice(
        jnp.zeros((members,), jnp.float32), score, (lax.axis_index("row") * local_members,)
    )
    fitness = lax.psum(placed, ("row", "col"))
    weights = jnp.repeat(fitness, RANK)
    update = jnp.dot(
        factor_u.astype(jnp.float32) * weights[None, :],
        factor_v.astype(jnp.float32),
        precision=lax.Precision.HIGHEST,
        preferred_element_type=jnp.float32,
    ) * math.sqrt(D / members)
    return (mixed, fitness, update)


def solution(mesh):
    return jax.shard_map(
        body,
        mesh=mesh,
        in_specs=(
            P("row", "col"),
            P("row", "col"),
            P("col", "row"),
            P("col", "row"),
            P("row", "col"),
            P("col", None),
            P(None, "row"),
        ),
        out_specs=(P("row", "col"), P(), P("col", "row")),
        check_vma=False,
    )
```

profile of v0, /device:TPU:1, one launch (start us, length us, event | category | flops | bytes accessed | tf_op | source)
XLA Modules:
  0.0 587.6 jit_solution(11700659747309950121)
XLA Ops:
  7.2 0.7 all-gather.3.cloned.1.call-update
  8.0 1.2 copy.12
  9.1 0.1 reshape.22
  9.2 1.1 copy.13
  10.4 86.9 %all-gather.3.cloned.1.call-done = bf16[4096,640]{1,0:T(8,128)(2,1)} async-done(((bf16[128,640]{1,0:T(8,128)(2,1)}), bf16[4096,640]{1,0:T(8,128)(2,1)}) %all-gather.3.cloned.1.call-update) | async-done | bytes 5242896 | tf_op jit(solution)/shard_map/all_gather | solution.py:24
  97.3 4.2 fusion.4
  101.5 5.8 broadcast_multiply_fusion
  107.3 8.6 %copy.14 = f32[4096,432]{0,1:T(8,128)} copy(f32[4096,432]{1,0:T(8,128)} %bitcast.15) | data formatting | bytes 14155776 | tf_op jit(solution)/shard_map/mul | solution.py:32
  115.9 9.4 %convolution_add_fusion = f32[4096,432]{0,1:T(8,128)} fusion(f32[4096,432]{0,1:T(8,128)} %copy.14, bf16[4096,640]{1,0:T(8,128)(2,1)} %all-gather.3.cloned.1.call-done, bf16[640,432]{0,1:T(8,128)(2,1)S(1)} %copy-done.3), kind=kOutput, calls=%fused_computation | convolution fusion | flops 2266693632 | bytes 19951616 | tf_op jit(solution)/shard_map/dot_general | solution.py:27
  125.4 1.0 copy-done.6
  126.4 8.3 %fusion.3 = f32[4096,432]{0,1:T(8,128)} fusion(bf16[4096,640]{1,0:T(8,128)(2,1)} %all-gather.3.cloned.1.call-done, bf16[640,432]{0,1:T(8,128)(2,1)S(1)} %copy-done.6), kind=kOutput, calls=%fused_computation.9 | convolution fusion | flops 2264924160 | bytes 12873728 | tf_op jit(solution)/shard_map/dot_general | solution.py:26
  134.8 38.4 %reduce-scatter.6.cloned.1.call-done = f32[512,432]{0,1:T(8,128)} async-done(((f32[4096,432]{0,1:T(8,128)}), f32[512,432]{0,1:T(8,128)}) %reduce-scatter.6.cloned.1.call-update) | async-done | bytes 884752 | tf_op jit(solution)/shard_map/reduce_scatter | solution.py:35
  173.2 51.0 %reduce-scatter.4.cloned.1.call-done = f32[512,432]{0,1:T(8,128)} async-done(((f32[4096,432]{0,1:T(8,128)}), f32[512,432]{0,1:T(8,128)}) %reduce-scatter.4.cloned.1.call-update) | async-done | bytes 884752 | tf_op jit(solution)/shard_map/reduce_scatter | solution.py:34
  224.2 2.5 multiply_convert_fusion
  226.7 32.6 %all-gather.5.cloned.1.call-done = bf16[4096,432]{0,1:T(8,128)(2,1)} async-done(((bf16[512,432]{0,1:T(8,128)(2,1)}), bf16[4096,432]{0,1:T(8,128)(2,1)}) %all-gather.5.cloned.1.call-update) | async-done | bytes 3538960 | tf_op jit(solution)/shard_map/all_gather | solution.py:38
  259.3 9.5 %fusion.5 = f32[4096,640]{1,0:T(8,128)} fusion(bf16[4096,432]{0,1:T(8,128)(2,1)} %all-gather.5.cloned.1.call-done, bf16[432,640]{1,0:T(8,128)(2,1)S(1)} %copy-done), kind=kOutput, calls=%fused_computation.11 | convolution fusion | flops 2264924160 | bytes 14577664 | tf_op jit(solution)/shard_map/dot_general | solution.py:40
  268.8 229.8 %reduce-scatter.8.cloned.1.call-done = f32[128,640]{1,0:T(8,128)} async-done(((f32[4096,640]{1,0:T(8,128)}), f32[128,640]{1,0:T(8,128)}) %reduce-scatter.8.cloned.1.call-update) | async-done | bytes 327696 | tf_op jit(solution)/shard_map/reduce_scatter | solution.py:39
  498.6 1.8 multiply_reduce_fusion
  500.4 0.1 reduce_sum.14
  500.5 0.1 reduce_sum.18
  500.6 0.1 multiply_dynamic-update-slice_fusion
  500.7 78.4 %psum.7 = f32[64]{0:T(128)S(1)} all-reduce(f32[64]{0:T(128)S(1)} %multiply_dynamic-update-slice_fusion), channel_id=1, replica_groups=mesh['row'=32,'col'=8] {'row','col'}, use_global_device_ids=true, to_apply=%region_5.6 | all-reduce | flops 64 | bytes 512 | tf_op jit(solution)/shard_map/psum | solution.py:52
  579.2 0.1 mul.45
  579.3 1.8 convolution_multiply_fusion
  (25 shorter events, 0.4 us)
Async XLA Ops:
  7.2 252.2 %copy-start = (bf16[432,640]{1,0:T(8,128)(2,1)S(1)}, bf16[432,640]{1,0:T(8,128)(2,1)}, u32[]{:S(2)}) copy-start(bf16[432,640]{1,0:T(8,128)(2,1)} %param.11) | copy-start | bytes 1658884
  7.2 90.1 %all-gather.3.cloned.1.call-start = ((), (), s32[]{:S(2)}) async-start(), calls=%async_computation.3 | async-start | bytes 5406720 | tf_op jit(solution)/shard_map/all_gather | solution.py:24
  7.9 165.3 %reduce-scatter.6.cloned.1.call-start = ((), (), s32[]{:S(2)}) async-start(), calls=%async_computation.5 | async-start | bytes 7962624 | tf_op jit(solution)/shard_map/reduce_scatter | solution.py:35
  107.3 8.7 %copy-start.3 = (bf16[640,432]{0,1:T(8,128)(2,1)S(1)}, bf16[640,432]{0,1:T(8,128)(2,1)}, u32[]{:S(2)}) copy-start(bf16[640,432]{0,1:T(8,128)(2,1)} %param.10) | copy-start | bytes 1658884
  125.3 1.1 copy-start.6
  125.4 98.8 %reduce-scatter.4.cloned.1.call-start = ((), (), s32[]{:S(2)}) async-start(), calls=%async_computation.4 | async-start | bytes 7962624 | tf_op jit(solution)/shard_map/reduce_scatter | solution.py:34
  134.7 124.6 %all-gather.5.cloned.1.call-start = ((), (), s32[]{:S(2)}) async-start(), calls=%async_computation.6 | async-start | bytes 3981312 | tf_op jit(solution)/shard_map/all_gather | solution.py:38
  226.6 272.0 %reduce-scatter.8.cloned.1.call-start = ((), (), s32[]{:S(2)}) async-start(), calls=%async_computation.7 | async-start | bytes 10813440 | tf_op jit(solution)/shard_map/reduce_scatter | solution.py:39
  268.8 229.8 %copy-start.4 = (bf16[128,640]{1,0:T(8,128)(2,1)S(1)}, bf16[128,640]{1,0:T(8,128)(2,1)}, u32[]{:S(2)}) copy-start(bf16[128,640]{1,0:T(8,128)(2,1)} %param.8) | copy-start | bytes 491524
  268.8 310.5 %copy-start.1 = (bf16[640,256]{1,0:T(8,128)(2,1)S(1)}, bf16[640,256]{1,0:T(8,128)(2,1)}, u32[]{:S(2)}) copy-start(bf16[640,256]{1,0:T(8,128)(2,1)} %param.12) | copy-start | bytes 983044
  268.8 310.5 %copy-start.2 = (bf16[256,432]{0,1:T(8,128)(2,1)S(1)}, bf16[256,432]{0,1:T(8,128)(2,1)}, u32[]{:S(2)}) copy-start(bf16[256,432]{0,1:T(8,128)(2,1)} %param.13) | copy-start | bytes 663556
  579.1 2.0 copy-start.5
Sparse Core Ops, SparseCore 0:
  10.6 86.6 all-gather.2
  125.5 47.6 reduce-scatter.5
  175.8 48.3 reduce-scatter.3
  226.8 32.5 all-gather.4
  268.9 229.6 reduce-scatter.7
where the time goes:
time: 588 us
  waiting for transfers between devices  439 us (75%)
  blocking collectives  78.4 us (13%)
  matrix products  39 us (7%)
  between operations  13.8 us (2%)
  local copies, waits for them, and re-layouts  12.3 us (2%)
    reduce_scatter x1, waiting for transfers between devices, body(): lax.psum_scatter(jnp.dot(hidden_all, w_down, preferred_element_type=jnp.f...  230 us
    all_gather x1, waiting for transfers between devices, body(): every = lax.all_gather(tokens, 'row', axis=0, tiled=True)  86.9 us
    psum x1, blocking collectives, body(): fitness = lax.psum(placed, ('row', 'col'))  78.4 us
    reduce_scatter x1, waiting for transfers between devices, body(): lax.psum_scatter(gate_part, 'col', scatter_dimension=0, tiled=True)  51 us
    reduce_scatter x1, waiting for transfers between devices, body(): lax.psum_scatter(up_part, 'col', scatter_dimension=0, tiled=True)  38.4 us
    all_gather x1, waiting for transfers between devices, body(): hidden_all = lax.all_gather(hidden, 'col', axis=0, tiled=True)  32.6 us
  transfers between devices with their start and end apart: 5, of which 5 were waited for; matrix products, arithmetic and copies ran while one was open for 2% of the time, Pallas kernels for 0%

commit v1 on v0

v1 whole, which is shorter than its diff:
```python
import math

import jax
import jax.numpy as jnp
from jax import lax
from jax.sharding import Mesh
from jax.sharding import PartitionSpec as P

D = 5120
RANK = 4
SEQ = 64
SIGMA = 0.5
LANES = 128

Z, Y, X, C = 8, 4, 4, 2
ROW = ("z", "y")
COL = ("x", "core")
PLANE = ("y", "x", "core")
ALL = ("z", "y", "x", "core")
F32 = jnp.float32
BF16 = jnp.bfloat16


def shift(value, step):
    return lax.ppermute(value, "z", [(i, (i + step) % Z) for i in range(Z)])


def ring_gather(chunks):
    half = Z // 2
    blocks = [[chunk] + [None] * (Z - 1) for chunk in chunks]
    ends = [[chunk, chunk] for chunk in chunks]
    for step in range(1, half + 1):
        for k, end in enumerate(ends):
            if step < half or k % 2 == 0:
                end[0] = shift(end[0], 1)
                blocks[k][Z - step] = end[0]
            if step < half or k % 2 == 1:
                end[1] = shift(end[1], -1)
                blocks[k][step] = end[1]
    return blocks


def ring_scatter(chunks):
    half = Z // 2
    ends = [[None, None] for _ in chunks]
    for step in range(half, 0, -1):
        for k, blocks in enumerate(chunks):
            for side, sign in ((0, 1), (1, -1)):
                if step == half and side != k % 2:
                    continue
                send = blocks[(sign * step) % Z]
                if ends[k][side] is not None:
                    send = send + ends[k][side]
                ends[k][side] = shift(send.astype(BF16), sign).astype(F32)
    return [blocks[0] + end[0] + end[1] for blocks, end in zip(chunks, ends)]


def split_two(value):
    high = value.astype(BF16)
    return high, (value - high.astype(F32)).astype(BF16)


def body(tokens, target, w_gate, w_up, w_down, factor_u, factor_v):
    dev_rows, dev_feat = tokens.shape
    members = factor_u.shape[1] // RANK
    units = w_up.shape[1]
    cols = X * C
    model = dev_feat * cols
    own = dev_rows // cols
    local = dev_rows // SEQ
    z, y = lax.axis_index("z"), lax.axis_index("y")
    x, core = lax.axis_index("x"), lax.axis_index("core")

    weights = lax.all_gather(
        jnp.concatenate([w_down.T, w_gate, w_up], axis=1), COL, axis=0, tiled=True
    )
    v_twice = jnp.concatenate([factor_v, factor_v], axis=0)

    first = (z * Y + y) * local * RANK
    u_own = lax.dynamic_slice(factor_u, (0, first), (dev_feat, local * RANK))
    low = jnp.dot(tokens, u_own, preferred_element_type=F32)
    low = low.reshape(local, SEQ, local, RANK)
    low = jnp.concatenate([low[m, :, m] for m in range(local)], axis=0)
    extra = jnp.concatenate(split_two(low), axis=1)
    extra = jnp.pad(extra, ((0, 0), (0, LANES - extra.shape[1])))
    wide = jnp.concatenate([tokens, extra], axis=1).reshape(1, cols, own, dev_feat + LANES)
    wide = jnp.broadcast_to(wide, (Y, cols, own, dev_feat + LANES))
    moved = lax.all_to_all(wide.reshape(Y * cols, own, dev_feat + LANES), PLANE, 0, 0, tiled=True)
    moved = moved.reshape(Y, cols, own, dev_feat + LANES)
    part = moved[..., dev_feat:].astype(F32)
    part = part[..., :RANK] + part[..., RANK : 2 * RANK]
    extra = jnp.concatenate(split_two(jnp.sum(part, axis=1)), axis=-1)
    extra = jnp.pad(extra, ((0, 0), (0, 0), (0, LANES - extra.shape[-1])))
    rows = jnp.swapaxes(moved[..., :dev_feat], 1, 2).reshape(Y, own, model)
    rows = jnp.concatenate([rows, extra], axis=2).reshape(Y * own, model + LANES)
    plane = Y * own
    mid = plane // 2

    gathered = ring_gather([rows[:mid], rows[mid:]])
    every = jnp.concatenate(gathered[0] + gathered[1], axis=0)

    row = lax.broadcasted_iota(jnp.int32, (Z * plane, members * RANK * 2), 0)
    column = lax.broadcasted_iota(jnp.int32, (Z * plane, members * RANK * 2), 1)
    row_y = row // (Z * mid) * (Y // 2) + row % mid // own
    row_z = (z + row // mid) % Z
    member = (row_z * Y + row_y) * local + (x * C + core) * own // SEQ
    spread_row = lax.broadcasted_iota(jnp.int32, (LANES, members * RANK * 2), 0)
    spread_col = lax.broadcasted_iota(jnp.int32, (LANES, members * RANK * 2), 1)
    spread = spread_col // (members * RANK) * RANK + spread_col % RANK == spread_row
    low = jnp.dot(every[:, model:], spread.astype(BF16), preferred_element_type=F32)
    low = jnp.where(column % (members * RANK) // RANK == member, low, 0.0).astype(BF16)
    corr = jnp.dot(low, v_twice, preferred_element_type=F32)

    both = jnp.dot(every[:, :model], weights, preferred_element_type=F32)
    gate, up = both[:, units : 2 * units], both[:, 2 * units :] + SIGMA * corr
    hidden = (jax.nn.silu(gate) * up).astype(BF16)
    hidden, weights = lax.optimization_barrier((hidden, weights))
    out = lax.dot_general(
        hidden, weights[:, :units], (((1,), (1,)), ((), ())), preferred_element_type=F32
    )
    out = out.reshape(2, Z, mid, model)
    sums = ring_scatter([[out[k, d] for d in range(Z)] for k in range(2)])
    back = jnp.concatenate([s.astype(BF16) for s in sums], axis=0).reshape(Y, own, cols, dev_feat)
    back = jnp.swapaxes(back, 1, 2).reshape(Y * cols, own, dev_feat)
    back = lax.all_to_all(back, PLANE, 0, 0, tiled=True).reshape(Y, dev_rows, dev_feat)
    final = jnp.sum(back.astype(F32), axis=0)
    mixed = final.astype(BF16)

    score = jnp.sum((final * target.astype(F32)).reshape(local, SEQ, dev_feat), axis=(1, 2))
    score = jnp.pad(score / math.sqrt(SEQ * D), (0, LANES - local))
    devices = Z * Y * cols
    scores = lax.all_to_all(
        jnp.broadcast_to(score, (devices, 1, LANES)), ALL, 0, 0, tiled=True
    )
    scores = scores.reshape(Z * Y, cols, LANES)[:, :, :local]
    fitness = jnp.sum(scores, axis=1).reshape(members)

    scale = jnp.repeat(fitness, RANK) * math.sqrt(D / members)
    scaled = jnp.concatenate(split_two(factor_u.astype(F32) * scale[None, :]), axis=1)
    update = jnp.dot(scaled, v_twice, preferred_element_type=F32)
    return (mixed, fitness, update)


def solution(mesh):
    fine = Mesh(mesh.devices.reshape(Z, Y, X, C), ALL)
    return jax.shard_map(
        body,
        mesh=fine,
        in_specs=(
            P(ROW, COL),
            P(ROW, COL),
            P(COL, ROW),
            P(COL, ROW),
            P(ROW, COL),
            P(COL, None),
            P(None, ROW),
        ),
        out_specs=(P(ROW, COL), P(), P(COL, ROW)),
        check_vma=False,
    )
```

time: 588 us -> 263 us (0.45)
  waiting for transfers between devices: 439 us -> 94.9 us
  starting transfers between devices: 0.2 us -> 51.1 us
  blocking collectives: 78.4 us -> 55 us
  matrix products: 39 us -> 22.9 us
    reduce_scatter x3 -> x0, waiting for transfers between devices: 319 us -> none  [the longest x1 230 us: body(): lax.psum_scatter(jnp.dot(hidden_all, w_down, preferred_element_type=jnp.f...]
    all_gather x2 -> x1, waiting for transfers between devices: 119 us -> 0.01 us  [body(): lax.all_gather(jnp.concatenate([w_down.T, w_gate, w_up], axis=1), COL, ax...]
    ppermute x0 -> x28, waiting for transfers between devices: none -> 79.5 us  [shift(): return lax.ppermute(value, 'z', [(i, (i + step) % Z) for i in range(Z)])]
    psum x1 -> x0, blocking collectives: 78.4 us -> none  [body(): fitness = lax.psum(placed, ('row', 'col'))]
    all_to_all x0 -> x2, blocking collectives: none -> 55 us  [the longest x1 34.8 us: body(): lax.all_to_all(back, PLANE, 0, 0, tiled=True).reshape(Y, dev_rows, dev_feat)]
    ppermute x0 -> x28, starting transfers between devices: none -> 42.5 us  [shift(): return lax.ppermute(value, 'z', [(i, (i + step) % Z) for i in range(Z)])]
    dot_general x6 -> x5, matrix products: 39 us -> 22.9 us  [the longest x1 12.7 us: body(): both = jnp.dot(every[:, :model], weights, preferred_element_type=F32)]
    all_to_all x0 -> x1, waiting for transfers between devices: none -> 15.4 us  [body(): lax.all_to_all(wide.reshape(Y * cols, own, dev_feat + LANES), PLANE, 0, 0...]
  transfers between devices with their start and end apart: 5 -> 30, of which waited for: 5 -> 21; matrix products, arithmetic and copies ran while one was open for 2% -> 6% of each run, Pallas kernels for 0% -> 0%
where the time goes in v1:
time: 263 us; the launch traced here: 262 us
  waiting for transfers between devices  94.9 us (36%)
  blocking collectives  55 us (21%)
  starting transfers between devices  51.1 us (19%)
  matrix products  22.9 us (9%)
  local copies, waits for them, and re-layouts  15.7 us (6%)
  between operations  14.5 us (6%)
  other arithmetic  8.27 us (3%)
    ppermute x28, waiting for transfers between devices, shift(): return lax.ppermute(value, 'z', [(i, (i + step) % Z) for i in range(Z)])  79.5 us
    ppermute x28, starting transfers between devices, shift(): return lax.ppermute(value, 'z', [(i, (i + step) % Z) for i in range(Z)])  42.5 us
    all_to_all x1, blocking collectives, body(): lax.all_to_all(back, PLANE, 0, 0, tiled=True).reshape(Y, dev_rows, dev_feat)  34.8 us
    all_to_all x1, blocking collectives, body(): lax.all_to_all(jnp.broadcast_to(score, (devices, 1, LANES)), ALL, 0, 0, t...  20.1 us
    all_to_all x1, waiting for transfers between devices, body(): lax.all_to_all(wide.reshape(Y * cols, own, dev_feat + LANES), PLANE, 0, 0...  15.4 us
    dot_general x1, matrix products, body(): both = jnp.dot(every[:, :model], weights, preferred_element_type=F32)  12.7 us
    unnamed x30, local copies, waits for them, and re-layouts  11.7 us
    all_to_all x1, starting transfers between devices, body(): lax.all_to_all(wide.reshape(Y * cols, own, dev_feat + LANES), PLANE, 0, 0...  8.59 us
  transfers between devices with their start and end apart: 30, of which 21 were waited for; matrix products, arithmetic and copies ran while one was open for 6% of the time, Pallas kernels for 0%

profile of v1, /device:TPU:1, one launch (start us, length us, event | category | flops | bytes accessed | tf_op | source)
XLA Modules:
  0.0 262.4 jit_solution(16569874213093620193)
XLA Ops:
  12.7 8.6 %all-to-all-start = ((bf16[32,16,768]{2,1,0:T(8,128)(2,1)}), bf16[32,16,768]{2,1,0:T(8,128)(2,1)S(1)}, u32[]{:S(2)}, u32[]{:S(2)}) async-start(bf16[32,16,768]{2,1,0:T(8,128)(2,1)} %bitcast.4), calls=%async_computation | async-start | bytes 1572864 | tf_op jit(solution)/shard_map/all_to_all | solution.py:88
  21.5 15.4 %all-to-all-done = bf16[32,16,768]{2,1,0:T(8,128)(2,1)S(1)} async-done(((bf16[32,16,768]{2,1,0:T(8,128)(2,1)}), bf16[32,16,768]{2,1,0:T(8,128)(2,1)S(1)}, u32[]{:S(2)}, u32[]{:S(2)}) %all-to-all-start) | async-done | bytes 786464 | tf_op jit(solution)/shard_map/all_to_all | solution.py:88
  37.5 7.7 %collective-permute-start = (bf16[32,5248]{1,0:T(8,128)(2,1)S(1)}, bf16[32,5248]{1,0:T(8,128)(2,1)S(1)}, u32[]{:S(2)}, u32[]{:S(2)}) collective-permute-start(bf16[32,5248]{1,0:T(8,128)(2,1)S(1)} %bitcast.142), channel_id=1, source_target_pairs={{0,224},{32,0},{64,32},{96,64},{128,96},{160,128},{192,160},{224,1... | collective-permute-start | bytes 1007624 | tf_op jit(solution)/shard_map/ppermute | solution.py:25
  51.4 3.5 %collective-permute-start.1 = (bf16[32,5248]{1,0:T(8,128)(2,1)S(1)}, bf16[32,5248]{1,0:T(8,128)(2,1)S(1)}, u32[]{:S(2)}, u32[]{:S(2)}) collective-permute-start(bf16[32,5248]{1,0:T(8,128)(2,1)S(1)} %collective-permute-done), channel_id=1, source_target_pairs={{0,224},{32,0},{64,32},{96,64},{128,96},{160,128},{192,160},{224,1... | collective-permute-start | bytes 1007624 | tf_op jit(solution)/shard_map/ppermute | solution.py:25
  54.9 3.7 %collective-permute-done.7 = bf16[32,5248]{1,0:T(8,128)(2,1)S(1)} collective-permute-done((bf16[32,5248]{1,0:T(8,128)(2,1)S(1)}, bf16[32,5248]{1,0:T(8,128)(2,1)S(1)}, u32[]{:S(2)}, u32[]{:S(2)}) %collective-permute-start.7) | collective-permute-done | bytes 335904 | tf_op jit(solution)/shard_map/ppermute | solution.py:25
  58.6 3.5 %collective-permute-start.8 = (bf16[32,5248]{1,0:T(8,128)(2,1)S(1)}, bf16[32,5248]{1,0:T(8,128)(2,1)S(1)}, u32[]{:S(2)}, u32[]{:S(2)}) collective-permute-start(bf16[32,5248]{1,0:T(8,128)(2,1)S(1)} %collective-permute-done.7), channel_id=1, source_target_pairs={{0,224},{32,0},{64,32},{96,64},{128,96},{160,128},{192,160},{224,1... | collective-permute-start | bytes 1007624 | tf_op jit(solution)/shard_map/ppermute | solution.py:25
  65.8 3.5 %collective-permute-start.2 = (bf16[32,5248]{1,0:T(8,128)(2,1)S(1)}, bf16[32,5248]{1,0:T(8,128)(2,1)S(1)}, u32[]{:S(2)}, u32[]{:S(2)}) collective-permute-start(bf16[32,5248]{1,0:T(8,128)(2,1)S(1)} %collective-permute-done.1), channel_id=1, source_target_pairs={{0,224},{32,0},{64,32},{96,64},{128,96},{160,128},{192,160},{224,1... | collective-permute-start | bytes 1007624 | tf_op jit(solution)/shard_map/ppermute | solution.py:25
  69.3 3.7 %collective-permute-done.8 = bf16[32,5248]{1,0:T(8,128)(2,1)S(1)} collective-permute-done((bf16[32,5248]{1,0:T(8,128)(2,1)S(1)}, bf16[32,5248]{1,0:T(8,128)(2,1)S(1)}, u32[]{:S(2)}, u32[]{:S(2)}) %collective-permute-start.8) | collective-permute-done | bytes 335904 | tf_op jit(solution)/shard_map/ppermute | solution.py:25
  73.0 3.5 %collective-permute-start.9 = (bf16[32,5248]{1,0:T(8,128)(2,1)S(1)}, bf16[32,5248]{1,0:T(8,128)(2,1)S(1)}, u32[]{:S(2)}, u32[]{:S(2)}) collective-permute-start(bf16[32,5248]{1,0:T(8,128)(2,1)S(1)} %collective-permute-done.8), channel_id=1, source_target_pairs={{0,224},{32,0},{64,32},{96,64},{128,96},{160,128},{192,160},{224,1... | collective-permute-start | bytes 1007624 | tf_op jit(solution)/shard_map/ppermute | solution.py:25
  77.3 6.1 %collective-permute-done.5 = bf16[32,5248]{1,0:T(8,128)(2,1)S(1)} collective-permute-done((bf16[32,5248]{1,0:T(8,128)(2,1)S(1)}, bf16[32,5248]{1,0:T(8,128)(2,1)S(1)}, u32[]{:S(2)}, u32[]{:S(2)}) %collective-permute-start.5) | collective-permute-done | bytes 335904 | tf_op jit(solution)/shard_map/ppermute | solution.py:25
  83.4 4.0 %collective-permute-done.9 = bf16[32,5248]{1,0:T(8,128)(2,1)S(1)} collective-permute-done((bf16[32,5248]{1,0:T(8,128)(2,1)S(1)}, bf16[32,5248]{1,0:T(8,128)(2,1)S(1)}, u32[]{:S(2)}, u32[]{:S(2)}) %collective-permute-start.9) | collective-permute-done | bytes 335904 | tf_op jit(solution)/shard_map/ppermute | solution.py:25
  87.4 3.5 %collective-permute-start.10 = (bf16[32,5248]{1,0:T(8,128)(2,1)S(1)}, bf16[32,5248]{1,0:T(8,128)(2,1)S(1)}, u32[]{:S(2)}, u32[]{:S(2)}) collective-permute-start(bf16[32,5248]{1,0:T(8,128)(2,1)S(1)} %collective-permute-done.9), channel_id=1, source_target_pairs={{0,224},{32,0},{64,32},{96,64},{128,96},{160,128},{192,160},{224,1... | collective-permute-start | bytes 1007624 | tf_op jit(solution)/shard_map/ppermute | solution.py:25
  91.7 6.0 %collective-permute-done.6 = bf16[32,5248]{1,0:T(8,128)(2,1)S(1)} collective-permute-done((bf16[32,5248]{1,0:T(8,128)(2,1)S(1)}, bf16[32,5248]{1,0:T(8,128)(2,1)S(1)}, u32[]{:S(2)}, u32[]{:S(2)}) %collective-permute-start.6) | collective-permute-done | bytes 335904 | tf_op jit(solution)/shard_map/ppermute | solution.py:25
  106.8 12.7 %fusion = f32[512,1296]{0,1:T(8,128)} fusion(bf16[5120,1296]{0,1:T(8,128)(2,1)} %all-gather.2.cloned.1.call-done, bf16[512,5248]{1,0:T(8,128)(2,1)} %constant_dynamic-update-slice_fusion), kind=kOutput, calls=%fused_computation | convolution fusion | flops 6794772480 | bytes 21168128 | tf_op jit(solution)/shard_map/dot_general | solution.py:114
  122.1 4.8 %fusion.2 = f32[512,5120]{1,0:T(8,128)S(1)} fusion(bf16[512,432]{0,1:T(8,128)(2,1)S(1)} %fusion.28, bf16[5120,1296]{0,1:T(8,128)(2,1)} %all-gather.2.cloned.1.call-done), kind=kOutput, calls=%fused_computation.2 | convolution fusion | flops 2264924160 | bytes 15351808 | tf_op jit(solution)/shard_map/dot_general | solution.py:118
  131.5 8.1 %collective-permute-done.14 = bf16[32,5120]{1,0:T(8,128)(2,1)S(1)} collective-permute-done((bf16[32,5120]{1,0:T(8,128)(2,1)S(1)}, bf16[32,5120]{1,0:T(8,128)(2,1)S(1)}, u32[]{:S(2)}, u32[]{:S(2)}) %collective-permute-start.14) | collective-permute-done | bytes 327712 | tf_op jit(solution)/shard_map/ppermute | solution.py:25
  142.4 4.5 %collective-permute-done.15 = bf16[32,5120]{1,0:T(8,128)(2,1)S(1)} collective-permute-done((bf16[32,5120]{1,0:T(8,128)(2,1)S(1)}, bf16[32,5120]{1,0:T(8,128)(2,1)S(1)}, u32[]{:S(2)}, u32[]{:S(2)}) %collective-permute-start.15) | collective-permute-done | bytes 327712 | tf_op jit(solution)/shard_map/ppermute | solution.py:25
  147.0 7.1 %collective-permute-done.16 = bf16[32,5120]{1,0:T(8,128)(2,1)S(1)} collective-permute-done((bf16[32,5120]{1,0:T(8,128)(2,1)S(1)}, bf16[32,5120]{1,0:T(8,128)(2,1)S(1)}, u32[]{:S(2)}, u32[]{:S(2)}) %collective-permute-start.16) | collective-permute-done | bytes 327712 | tf_op jit(solution)/shard_map/ppermute | solution.py:25
  167.3 3.9 %collective-permute-done.20 = bf16[32,5120]{1,0:T(8,128)(2,1)S(1)} collective-permute-done((bf16[32,5120]{1,0:T(8,128)(2,1)S(1)}, bf16[32,5120]{1,0:T(8,128)(2,1)S(1)}, u32[]{:S(2)}, u32[]{:S(2)}) %collective-permute-start.20) | collective-permute-done | bytes 327712 | tf_op jit(solution)/shard_map/ppermute | solution.py:25
  174.3 4.5 %collective-permute-done.22 = bf16[32,5120]{1,0:T(8,128)(2,1)S(1)} collective-permute-done((bf16[32,5120]{1,0:T(8,128)(2,1)S(1)}, bf16[32,5120]{1,0:T(8,128)(2,1)S(1)}, u32[]{:S(2)}, u32[]{:S(2)}) %collective-permute-start.22) | collective-permute-done | bytes 327712 | tf_op jit(solution)/shard_map/ppermute | solution.py:25
  183.7 6.5 %collective-permute-done.26 = bf16[32,5120]{1,0:T(8,128)(2,1)S(1)} collective-permute-done((bf16[32,5120]{1,0:T(8,128)(2,1)S(1)}, bf16[32,5120]{1,0:T(8,128)(2,1)S(1)}, u32[]{:S(2)}, u32[]{:S(2)}) %collective-permute-start.26) | collective-permute-done | bytes 327712 | tf_op jit(solution)/shard_map/ppermute | solution.py:25
  193.5 3.6 %collective-permute-done.27 = bf16[32,5120]{1,0:T(8,128)(2,1)S(1)} collective-permute-done((bf16[32,5120]{1,0:T(8,128)(2,1)S(1)}, bf16[32,5120]{1,0:T(8,128)(2,1)S(1)}, u32[]{:S(2)}, u32[]{:S(2)}) %collective-permute-start.27) | collective-permute-done | bytes 327712 | tf_op jit(solution)/shard_map/ppermute | solution.py:25
  197.5 34.8 %all_to_all.15 = bf16[32,16,640]{2,1,0:T(8,128)(2,1)S(1)} all-to-all(bf16[32,16,640]{2,1,0:T(8,128)(2,1)S(1)} %bitcast.137), channel_id=1, replica_groups=mesh['z'=8,'y'=4,'x'=4,'core'=2] {'y','x','core'}, dimensions={0} | all-to-all | bytes 1310720 | tf_op jit(solution)/shard_map/all_to_all | solution.py:125
  233.4 20.1 %all_to_all.16 = f32[256,1,128]{2,1,0:T(1,128)S(1)} all-to-all(f32[256,1,128]{2,1,0:T(1,128)S(1)} %broadcast_in_dim.21), channel_id=1, replica_groups=mesh['z'=8,'y'=4,'x'=4,'core'=2] {'z','y','x','core'}, dimensions={0} | all-to-all | bytes 262144 | tf_op jit(solution)/shard_map/all_to_all | solution.py:132
  (126 shorter events, 64.5 us)
Async XLA Ops:
  7.2 99.6 %all-gather.2.cloned.1.call-start = ((), (), s32[]{:S(2)}) async-start(), calls=%async_computation.3 | async-start | bytes 14929920 | tf_op jit(solution)/shard_map/all_gather | solution.py:74
  12.7 24.2 %all-to-all-start = ((bf16[32,16,768]{2,1,0:T(8,128)(2,1)}), bf16[32,16,768]{2,1,0:T(8,128)(2,1)S(1)}, u32[]{:S(2)}, u32[]{:S(2)}) async-start(bf16[32,16,768]{2,1,0:T(8,128)(2,1)} %bitcast.4), calls=%async_computation | async-start | bytes 1572864 | tf_op jit(solution)/shard_map/all_to_all | solution.py:88
  37.5 13.8 %collective-permute-start = (bf16[32,5248]{1,0:T(8,128)(2,1)S(1)}, bf16[32,5248]{1,0:T(8,128)(2,1)S(1)}, u32[]{:S(2)}, u32[]{:S(2)}) collective-permute-start(bf16[32,5248]{1,0:T(8,128)(2,1)S(1)} %bitcast.142), channel_id=1, source_target_pairs={{0,224},{32,0},{64,32},{96,64},{128,96},{160,128},{192,160},{224,1... | collective-permute-start | bytes 1007624 | tf_op jit(solution)/shard_map/ppermute | solution.py:25
  45.3 9.6 %collective-permute-start.3 = (bf16[32,5248]{1,0:T(8,128)(2,1)S(1)}, bf16[32,5248]{1,0:T(8,128)(2,1)S(1)}, u32[]{:S(2)}, u32[]{:S(2)}) collective-permute-start(bf16[32,5248]{1,0:T(8,128)(2,1)S(1)} %bitcast.143), channel_id=1, source_target_pairs={{0,32},{32,64},{64,96},{96,128},{128,160},{160,192},{192,224},{224... | collective-permute-start | bytes 1007624 | tf_op jit(solution)/shard_map/ppermute | solution.py:25
  45.3 13.3 %collective-permute-start.7 = (bf16[32,5248]{1,0:T(8,128)(2,1)S(1)}, bf16[32,5248]{1,0:T(8,128)(2,1)S(1)}, u32[]{:S(2)}, u32[]{:S(2)}) collective-permute-start(bf16[32,5248]{1,0:T(8,128)(2,1)S(1)} %bitcast.139), channel_id=1, source_target_pairs={{0,224},{32,0},{64,32},{96,64},{128,96},{160,128},{192,160},{224,1... | collective-permute-start | bytes 1007624 | tf_op jit(solution)/shard_map/ppermute | solution.py:25
  48.7 14.1 %collective-permute-start.11 = (bf16[32,5248]{1,0:T(8,128)(2,1)S(1)}, bf16[32,5248]{1,0:T(8,128)(2,1)S(1)}, u32[]{:S(2)}, u32[]{:S(2)}) collective-permute-start(bf16[32,5248]{1,0:T(8,128)(2,1)S(1)} %bitcast.140), channel_id=1, source_target_pairs={{0,32},{32,64},{64,96},{96,128},{128,160},{160,192},{192,224},{224... | collective-permute-start | bytes 1007624 | tf_op jit(solution)/shard_map/ppermute | solution.py:25
  51.4 14.4 %collective-permute-start.1 = (bf16[32,5248]{1,0:T(8,128)(2,1)S(1)}, bf16[32,5248]{1,0:T(8,128)(2,1)S(1)}, u32[]{:S(2)}, u32[]{:S(2)}) collective-permute-start(bf16[32,5248]{1,0:T(8,128)(2,1)S(1)} %collective-permute-done), channel_id=1, source_target_pairs={{0,224},{32,0},{64,32},{96,64},{128,96},{160,128},{192,160},{224,1... | collective-permute-start | bytes 1007624 | tf_op jit(solution)/shard_map/ppermute | solution.py:25
  54.9 14.4 %collective-permute-start.4 = (bf16[32,5248]{1,0:T(8,128)(2,1)S(1)}, bf16[32,5248]{1,0:T(8,128)(2,1)S(1)}, u32[]{:S(2)}, u32[]{:S(2)}) collective-permute-start(bf16[32,5248]{1,0:T(8,128)(2,1)S(1)} %collective-permute-done.3), channel_id=1, source_target_pairs={{0,32},{32,64},{64,96},{96,128},{128,160},{160,192},{192,224},{224... | collective-permute-start | bytes 1007624 | tf_op jit(solution)/shard_map/ppermute | solution.py:25
  58.6 14.4 %collective-permute-start.8 = (bf16[32,5248]{1,0:T(8,128)(2,1)S(1)}, bf16[32,5248]{1,0:T(8,128)(2,1)S(1)}, u32[]{:S(2)}, u32[]{:S(2)}) collective-permute-start(bf16[32,5248]{1,0:T(8,128)(2,1)S(1)} %collective-permute-done.7), channel_id=1, source_target_pairs={{0,224},{32,0},{64,32},{96,64},{128,96},{160,128},{192,160},{224,1... | collective-permute-start | bytes 1007624 | tf_op jit(solution)/shard_map/ppermute | solution.py:25
  62.8 14.4 %collective-permute-start.12 = (bf16[32,5248]{1,0:T(8,128)(2,1)S(1)}, bf16[32,5248]{1,0:T(8,128)(2,1)S(1)}, u32[]{:S(2)}, u32[]{:S(2)}) collective-permute-start(bf16[32,5248]{1,0:T(8,128)(2,1)S(1)} %collective-permute-done.11), channel_id=1, source_target_pairs={{0,32},{32,64},{64,96},{96,128},{128,160},{160,192},{192,224},{224... | collective-permute-start | bytes 1007624 | tf_op jit(solution)/shard_map/ppermute | solution.py:25
  65.8 25.1 %collective-permute-start.2 = (bf16[32,5248]{1,0:T(8,128)(2,1)S(1)}, bf16[32,5248]{1,0:T(8,128)(2,1)S(1)}, u32[]{:S(2)}, u32[]{:S(2)}) collective-permute-start(bf16[32,5248]{1,0:T(8,128)(2,1)S(1)} %collective-permute-done.1), channel_id=1, source_target_pairs={{0,224},{32,0},{64,32},{96,64},{128,96},{160,128},{192,160},{224,1... | collective-permute-start | bytes 1007624 | tf_op jit(solution)/shard_map/ppermute | solution.py:25
  69.3 14.1 %collective-permute-start.5 = (bf16[32,5248]{1,0:T(8,128)(2,1)S(1)}, bf16[32,5248]{1,0:T(8,128)(2,1)S(1)}, u32[]{:S(2)}, u32[]{:S(2)}) collective-permute-start(bf16[32,5248]{1,0:T(8,128)(2,1)S(1)} %collective-permute-done.4), channel_id=1, source_target_pairs={{0,32},{32,64},{64,96},{96,128},{128,160},{160,192},{192,224},{224... | collective-permute-start | bytes 1007624 | tf_op jit(solution)/shard_map/ppermute | solution.py:25
  73.0 14.4 %collective-permute-start.9 = (bf16[32,5248]{1,0:T(8,128)(2,1)S(1)}, bf16[32,5248]{1,0:T(8,128)(2,1)S(1)}, u32[]{:S(2)}, u32[]{:S(2)}) collective-permute-start(bf16[32,5248]{1,0:T(8,128)(2,1)S(1)} %collective-permute-done.8), channel_id=1, source_target_pairs={{0,224},{32,0},{64,32},{96,64},{128,96},{160,128},{192,160},{224,1... | collective-permute-start | bytes 1007624 | tf_op jit(solution)/shard_map/ppermute | solution.py:25
  77.3 27.3 %collective-permute-start.13 = (bf16[32,5248]{1,0:T(8,128)(2,1)S(1)}, bf16[32,5248]{1,0:T(8,128)(2,1)S(1)}, u32[]{:S(2)}, u32[]{:S(2)}) collective-permute-start(bf16[32,5248]{1,0:T(8,128)(2,1)S(1)} %collective-permute-done.12), channel_id=1, source_target_pairs={{0,32},{32,64},{64,96},{96,128},{128,160},{160,192},{192,224},{224... | collective-permute-start | bytes 1007624 | tf_op jit(solution)/shard_map/ppermute | solution.py:25
  83.4 14.3 %collective-permute-start.6 = (bf16[32,5248]{1,0:T(8,128)(2,1)S(1)}, bf16[32,5248]{1,0:T(8,128)(2,1)S(1)}, u32[]{:S(2)}, u32[]{:S(2)}) collective-permute-start(bf16[32,5248]{1,0:T(8,128)(2,1)S(1)} %collective-permute-done.5), channel_id=1, source_target_pairs={{0,32},{32,64},{64,96},{96,128},{128,160},{160,192},{192,224},{224... | collective-permute-start | bytes 1007624 | tf_op jit(solution)/shard_map/ppermute | solution.py:25
  87.4 16.4 %collective-permute-start.10 = (bf16[32,5248]{1,0:T(8,128)(2,1)S(1)}, bf16[32,5248]{1,0:T(8,128)(2,1)S(1)}, u32[]{:S(2)}, u32[]{:S(2)}) collective-permute-start(bf16[32,5248]{1,0:T(8,128)(2,1)S(1)} %collective-permute-done.9), channel_id=1, source_target_pairs={{0,224},{32,0},{64,32},{96,64},{128,96},{160,128},{192,160},{224,1... | collective-permute-start | bytes 1007624 | tf_op jit(solution)/shard_map/ppermute | solution.py:25
  131.4 8.2 %collective-permute-start.14 = (bf16[32,5120]{1,0:T(8,128)(2,1)S(1)}, bf16[32,5120]{1,0:T(8,128)(2,1)S(1)}, u32[]{:S(2)}, u32[]{:S(2)}) collective-permute-start(bf16[32,5120]{1,0:T(8,128)(2,1)S(1)} %get-tuple-element.16), channel_id=1, source_target_pairs={{0,32},{32,64},{64,96},{96,128},{128,160},{160,192},{192,224},{224... | collective-permute-start | bytes 983048 | tf_op jit(solution)/shard_map/ppermute | solution.py:25
  154.3 8.1 %collective-permute-start.21 = (bf16[32,5120]{1,0:T(8,128)(2,1)S(1)}, bf16[32,5120]{1,0:T(8,128)(2,1)S(1)}, u32[]{:S(2)}, u32[]{:S(2)}) collective-permute-start(bf16[32,5120]{1,0:T(8,128)(2,1)S(1)} %get-tuple-element.18), channel_id=1, source_target_pairs={{0,32},{32,64},{64,96},{96,128},{128,160},{160,192},{192,224},{224... | collective-permute-start | bytes 983048 | tf_op jit(solution)/shard_map/ppermute | solution.py:25
  155.8 8.4 %collective-permute-start.24 = (bf16[32,5120]{1,0:T(8,128)(2,1)S(1)}, bf16[32,5120]{1,0:T(8,128)(2,1)S(1)}, u32[]{:S(2)}, u32[]{:S(2)}) collective-permute-start(bf16[32,5120]{1,0:T(8,128)(2,1)S(1)} %get-tuple-element.17), channel_id=1, source_target_pairs={{0,224},{32,0},{64,32},{96,64},{128,96},{160,128},{192,160},{224,1... | collective-permute-start | bytes 983048 | tf_op jit(solution)/shard_map/ppermute | solution.py:25
  157.1 10.2 %collective-permute-start.17 = (bf16[32,5120]{1,0:T(8,128)(2,1)S(1)}, bf16[32,5120]{1,0:T(8,128)(2,1)S(1)}, u32[]{:S(2)}, u32[]{:S(2)}) collective-permute-start(bf16[32,5120]{1,0:T(8,128)(2,1)S(1)} %get-tuple-element.12), channel_id=1, source_target_pairs={{0,32},{32,64},{64,96},{96,128},{128,160},{160,192},{192,224},{224... | collective-permute-start | bytes 983048 | tf_op jit(solution)/shard_map/ppermute | solution.py:25
  160.3 10.9 %collective-permute-start.20 = (bf16[32,5120]{1,0:T(8,128)(2,1)S(1)}, bf16[32,5120]{1,0:T(8,128)(2,1)S(1)}, u32[]{:S(2)}, u32[]{:S(2)}) collective-permute-start(bf16[32,5120]{1,0:T(8,128)(2,1)S(1)} %fusion.46), channel_id=1, source_target_pairs={{0,224},{32,0},{64,32},{96,64},{128,96},{160,128},{192,160},{224,1... | collective-permute-start | bytes 983048 | tf_op jit(solution)/shard_map/ppermute | solution.py:25
  171.6 9.9 %collective-permute-start.25 = (bf16[32,5120]{1,0:T(8,128)(2,1)S(1)}, bf16[32,5120]{1,0:T(8,128)(2,1)S(1)}, u32[]{:S(2)}, u32[]{:S(2)}) collective-permute-start(bf16[32,5120]{1,0:T(8,128)(2,1)S(1)} %get-tuple-element.10), channel_id=1, source_target_pairs={{0,224},{32,0},{64,32},{96,64},{128,96},{160,128},{192,160},{224,1... | collective-permute-start | bytes 983048 | tf_op jit(solution)/shard_map/ppermute | solution.py:25
  181.6 8.6 %collective-permute-start.26 = (bf16[32,5120]{1,0:T(8,128)(2,1)S(1)}, bf16[32,5120]{1,0:T(8,128)(2,1)S(1)}, u32[]{:S(2)}, u32[]{:S(2)}) collective-permute-start(bf16[32,5120]{1,0:T(8,128)(2,1)S(1)} %get-tuple-element.15), channel_id=1, source_target_pairs={{0,224},{32,0},{64,32},{96,64},{128,96},{160,128},{192,160},{224,1... | collective-permute-start | bytes 983048 | tf_op jit(solution)/shard_map/ppermute | solution.py:25
  183.7 9.7 %collective-permute-start.23 = (bf16[32,5120]{1,0:T(8,128)(2,1)S(1)}, bf16[32,5120]{1,0:T(8,128)(2,1)S(1)}, u32[]{:S(2)}, u32[]{:S(2)}) collective-permute-start(bf16[32,5120]{1,0:T(8,128)(2,1)S(1)} %get-tuple-element.14), channel_id=1, source_target_pairs={{0,32},{32,64},{64,96},{96,128},{128,160},{160,192},{192,224},{224... | collective-permute-start | bytes 983048 | tf_op jit(solution)/shard_map/ppermute | solution.py:25
  (11 other events, 176.8 us)
Sparse Core Ops, SparseCore 0:
  10.2 78.8 all-gather.1

commit v2 on v1

--- a/solution.py
+++ b/solution.py
@@ -27,32 +27,47 @@
 
 def ring_gather(chunks):
     half = Z // 2
-    blocks = [[chunk] + [None] * (Z - 1) for chunk in chunks]
+    rows = chunks[0].shape[0]
+    total = jnp.zeros((len(chunks), Z) + chunks[0].shape, chunks[0].dtype)
     ends = [[chunk, chunk] for chunk in chunks]
+    landed = [(k, 0, chunk) for k, chunk in enumerate(chunks)]
     for step in range(1, half + 1):
+        coming = []
         for k, end in enumerate(ends):
             if step < half or k % 2 == 0:
                 end[0] = shift(end[0], 1)
-                blocks[k][Z - step] = end[0]
+                coming.append((k, Z - step, end[0]))
             if step < half or k % 2 == 1:
                 end[1] = shift(end[1], -1)
-                blocks[k][step] = end[1]
-    return blocks
+                coming.append((k, step, end[1]))
+        for k, place, block in landed:
+            total = total.at[k, place].set(block)
+        if step < half:
+            total, ends[0] = lax.optimization_barrier((total, ends[0]))
+        landed = coming
+    for k, place, block in landed:
+        total = total.at[k, place].set(block)
+    return total.reshape(len(chunks) * Z * rows, -1)
 
 
 def ring_scatter(chunks):
     half = Z // 2
-    ends = [[None, None] for _ in chunks]
+    ends = {}
     for step in range(half, 0, -1):
+        sends = {}
         for k, blocks in enumerate(chunks):
             for side, sign in ((0, 1), (1, -1)):
                 if step == half and side != k % 2:
                     continue
-                send = blocks[(sign * step) % Z]
-                if ends[k][side] is not None:
-                    send = send + ends[k][side]
-                ends[k][side] = shift(send.astype(BF16), sign).astype(F32)
-    return [blocks[0] + end[0] + end[1] for blocks, end in zip(chunks, ends)]
+                block = blocks((sign * step) % Z)
+                if (k, sign) in ends:
+                    block = block + ends[k, sign]
+                else:
+                    block = lax.optimization_barrier(block)
+                sends[k, sign] = block.astype(BF16)
+        sends = lax.optimization_barrier(sends)
+        ends = {key: shift(value, key[1]).astype(F32) for key, value in sends.items()}
+    return [blocks(0) + ends[k, 1] + ends[k, -1] for k, blocks in enumerate(chunks)]
 
 
 def split_two(value):
@@ -86,6 +101,10 @@
     wide = jnp.concatenate([tokens, extra], axis=1).reshape(1, cols, own, dev_feat + LANES)
     wide = jnp.broadcast_to(wide, (Y, cols, own, dev_feat + LANES))
     moved = lax.all_to_all(wide.reshape(Y * cols, own, dev_feat + LANES), PLANE, 0, 0, tiled=True)
+    target, moved = lax.optimization_barrier((target, moved))
+    goal = jnp.broadcast_to(target.reshape(1, cols, own, dev_feat), (Y, cols, own, dev_feat))
+    goal = lax.all_to_all(goal.reshape(Y * cols, own, dev_feat), PLANE, 0, 0, tiled=True)
+    goal = jnp.swapaxes(goal.reshape(Y, cols, own, dev_feat), 1, 2).reshape(Y, own, model)
     moved = moved.reshape(Y, cols, own, dev_feat + LANES)
     part = moved[..., dev_feat:].astype(F32)
     part = part[..., :RANK] + part[..., RANK : 2 * RANK]
@@ -96,8 +115,7 @@
     plane = Y * own
     mid = plane // 2
 
-    gathered = ring_gather([rows[:mid], rows[mid:]])
-    every = jnp.concatenate(gathered[0] + gathered[1], axis=0)
+    every = ring_gather([rows[:mid], rows[mid:]])
 
     row = lax.broadcasted_iota(jnp.int32, (Z * plane, members * RANK * 2), 0)
     column = lax.broadcasted_iota(jnp.int32, (Z * plane, members * RANK * 2), 1)
@@ -119,21 +137,21 @@
         hidden, weights[:, :units], (((1,), (1,)), ((), ())), preferred_element_type=F32
     )
     out = out.reshape(2, Z, mid, model)
-    sums = ring_scatter([[out[k, d] for d in range(Z)] for k in range(2)])
-    back = jnp.concatenate([s.astype(BF16) for s in sums], axis=0).reshape(Y, own, cols, dev_feat)
-    back = jnp.swapaxes(back, 1, 2).reshape(Y * cols, own, dev_feat)
+    sums = ring_scatter([lambda d: out[0, d], lambda d: out[1, d]])
+    total = jnp.concatenate(sums, axis=0).reshape(Y, own, model)
+    back = jnp.swapaxes(total.astype(BF16).reshape(Y, own, cols, dev_feat), 1, 2)
+    back = back.reshape(Y * cols, own, dev_feat)
     back = lax.all_to_all(back, PLANE, 0, 0, tiled=True).reshape(Y, dev_rows, dev_feat)
-    final = jnp.sum(back.astype(F32), axis=0)
-    mixed = final.astype(BF16)
+    mixed = jnp.sum(back.astype(F32), axis=0).astype(BF16)
 
-    score = jnp.sum((final * target.astype(F32)).reshape(local, SEQ, dev_feat), axis=(1, 2))
-    score = jnp.pad(score / math.sqrt(SEQ * D), (0, LANES - local))
+    score = jnp.sum(total * goal.astype(F32), axis=(1, 2)) / math.sqrt(SEQ * D)
+    score = jnp.pad(score, (0, LANES - Y))
     devices = Z * Y * cols
     scores = lax.all_to_all(
         jnp.broadcast_to(score, (devices, 1, LANES)), ALL, 0, 0, tiled=True
     )
-    scores = scores.reshape(Z * Y, cols, LANES)[:, :, :local]
-    fitness = jnp.sum(scores, axis=1).reshape(members)
+    scores = scores.reshape(Z, Y, local, cols // local, LANES)[..., :Y]
+    fitness = jnp.swapaxes(jnp.sum(scores, axis=(1, 3)), 1, 2).reshape(members)
 
     scale = jnp.repeat(fitness, RANK) * math.sqrt(D / members)
     scaled = jnp.concatenate(split_two(factor_u.astype(F32) * scale[None, :]), axis=1)

time: 263 us -> 237 us (0.901)
  blocking collectives: 55 us -> 0 us
  waiting for transfers between devices: 94.9 us -> 63.2 us
  starting transfers between devices: 51.1 us -> 81.9 us
  other arithmetic: 8.27 us -> 33.6 us
  local copies, waits for them, and re-layouts: 15.7 us -> 20 us
    all_to_all x2 -> x0, blocking collectives: 55 us -> none  [the longest x1 34.8 us: body(): lax.all_to_all(back, PLANE, 0, 0, tiled=True).reshape(Y, dev_rows, dev_feat)]
    ppermute x28, waiting for transfers between devices: 79.5 us -> 29.7 us  [shift(): return lax.ppermute(value, 'z', [(i, (i + step) % Z) for i in range(Z)])]
    all_to_all x0 -> x3, starting transfers between devices: none -> 32.2 us  [the longest x1 16.5 us: body(): lax.all_to_all(jnp.broadcast_to(score, (devices, 1, LANES)), ALL, 0, 0, t...]
    all_to_all x0 -> x3, waiting for transfers between devices: none -> 28.2 us  [the longest x1 11.9 us: body(): lax.all_to_all(jnp.broadcast_to(score, (devices, 1, LANES)), ALL, 0, 0, t...]
    scatter x0 -> x6, other arithmetic: none -> 22.2 us  [ring_gather(): total = total.at[k, place].set(block)]
    unnamed x30 -> x17, local copies, waits for them, and re-layouts: 11.7 us -> 0.56 us
    scatter x0 -> x10, local copies, waits for them, and re-layouts: none -> 10.7 us  [ring_gather(): total = total.at[k, place].set(block)]
    all_to_all x1, waiting for transfers between devices: 15.4 us -> 5.28 us  [body(): lax.all_to_all(wide.reshape(Y * cols, own, dev_feat + LANES), PLANE, 0, 0...]
  transfers between devices with their start and end apart: 30 -> 33, of which waited for: 21 -> 15; matrix products, arithmetic and copies ran while one was open for 6% -> 20% of each run, Pallas kernels for 0% -> 0%
where the time goes in v2:
time: 237 us; the launch traced here: 236 us
  starting transfers between devices  81.9 us (35%)
  waiting for transfers between devices  63.2 us (27%)
  other arithmetic  33.6 us (14%)
  matrix products  23 us (10%)
  local copies, waits for them, and re-layouts  20 us (8%)
  between operations  14.5 us (6%)
    ppermute x28, starting transfers between devices, shift(): return lax.ppermute(value, 'z', [(i, (i + step) % Z) for i in range(Z)])  41.1 us
    ppermute x28, waiting for transfers between devices, shift(): return lax.ppermute(value, 'z', [(i, (i + step) % Z) for i in range(Z)])  29.7 us
    scatter x6, other arithmetic, ring_gather(): total = total.at[k, place].set(block)  22.2 us
    all_to_all x1, starting transfers between devices, body(): lax.all_to_all(jnp.broadcast_to(score, (devices, 1, LANES)), ALL, 0, 0, t...  16.5 us
    dot_general x1, matrix products, body(): both = jnp.dot(every[:, :model], weights, preferred_element_type=F32)  12.7 us
    all_to_all x1, waiting for transfers between devices, body(): lax.all_to_all(jnp.broadcast_to(score, (devices, 1, LANES)), ALL, 0, 0, t...  11.9 us
    all_to_all x1, starting transfers between devices, body(): lax.all_to_all(goal.reshape(Y * cols, own, dev_feat), PLANE, 0, 0, tiled=...  11.6 us
    all_to_all x1, waiting for transfers between devices, body(): lax.all_to_all(back, PLANE, 0, 0, tiled=True).reshape(Y, dev_rows, dev_feat)  10.9 us
  transfers between devices with their start and end apart: 33, of which 15 were waited for; matrix products, arithmetic and copies ran while one was open for 20% of the time, Pallas kernels for 0%

profile of v2, /device:TPU:1, one launch (start us, length us, event | category | flops | bytes accessed | tf_op | source)
XLA Modules:
  0.0 236.2 jit_solution(7020579978357013893)
XLA Ops:
  10.8 8.6 %all-to-all-start = ((bf16[32,16,768]{2,1,0:T(8,128)(2,1)}), bf16[32,16,768]{2,1,0:T(8,128)(2,1)S(1)}, u32[]{:S(2)}, u32[]{:S(2)}) async-start(bf16[32,16,768]{2,1,0:T(8,128)(2,1)} %bitcast.4), calls=%async_computation | async-start | bytes 1572864 | tf_op jit(solution)/shard_map/all_to_all | solution.py:103
  28.4 5.3 %all-to-all-done = bf16[32,16,768]{2,1,0:T(8,128)(2,1)S(1)} async-done(((bf16[32,16,768]{2,1,0:T(8,128)(2,1)}), bf16[32,16,768]{2,1,0:T(8,128)(2,1)S(1)}, u32[]{:S(2)}, u32[]{:S(2)}) %all-to-all-start) | async-done | bytes 786464 | tf_op jit(solution)/shard_map/all_to_all | solution.py:103
  36.0 4.0 %collective-permute-start.1 = (bf16[32,5248]{1,0:T(8,128)(2,1)S(1)}, bf16[32,5248]{1,0:T(8,128)(2,1)S(1)}, u32[]{:S(2)}, u32[]{:S(2)}) collective-permute-start(bf16[32,5248]{1,0:T(8,128)(2,1)S(1)} %bitcast.203), channel_id=1, source_target_pairs={{0,224},{32,0},{64,32},{96,64},{128,96},{160,128},{192,160},{224,1... | collective-permute-start | bytes 1007624 | tf_op jit(solution)/shard_map/ppermute | solution.py:25
  50.4 4.5 %collective-permute-done.2 = bf16[32,5248]{1,0:T(8,128)(2,1)S(1)} collective-permute-done((bf16[32,5248]{1,0:T(8,128)(2,1)S(1)}, bf16[32,5248]{1,0:T(8,128)(2,1)S(1)}, u32[]{:S(2)}, u32[]{:S(2)}) %collective-permute-start.2) | collective-permute-done | bytes 335904 | tf_op jit(solution)/shard_map/ppermute | solution.py:25
  57.6 3.7 %fusion.91 = bf16[2,8,32,5248]{3,2,1,0:T(8,128)(2,1)} fusion(bf16[2,8,32,5248]{3,2,1,0:T(8,128)(2,1)} %constant_dynamic-update-slice_fusion.2, s32[]{:T(128)} %bitcast.11, s32[]{:T(128)} %bitcast.12, bf16[32,5248]{1,0:T(8,128)(2,1)S(1)} %collective-permute-done, pred[]{:T(512)} %get-tuple-element.279), kind=kLoop, calls=%fused_computation.151 | loop fusion | flops 167936 | bytes 1009152 | tf_op jit(solution)/shard_map/scatter | solution.py:44
  72.0 3.8 %fusion.90 = bf16[2,8,32,5248]{3,2,1,0:T(8,128)(2,1)} fusion(bf16[2,8,32,5248]{3,2,1,0:T(8,128)(2,1)} %bitcast_dynamic-update-slice_fusion.5, s32[]{:T(128)} %bitcast.20, s32[]{:T(128)} %bitcast.21, bf16[32,5248]{1,0:T(8,128)(2,1)S(1)} %collective-permute-done.4, pred[]{:T(512)} %get-tuple-element.280), kind=kLoop, calls=%fused_computation.146 | loop fusion | flops 167936 | bytes 1009152 | tf_op jit(solution)/shard_map/scatter | solution.py:44
  75.8 3.6 %fusion.89 = bf16[2,8,32,5248]{3,2,1,0:T(8,128)(2,1)} fusion(bf16[2,8,32,5248]{3,2,1,0:T(8,128)(2,1)} %fusion.90, s32[]{:T(128)} %bitcast.23, s32[]{:T(128)} %bitcast.24, bf16[32,5248]{1,0:T(8,128)(2,1)S(1)} %collective-permute-done.5, pred[]{:T(512)} %get-tuple-element.250), kind=kLoop, calls=%fused_computation.144 | loop fusion | flops 167936 | bytes 1009152 | tf_op jit(solution)/shard_map/scatter | solution.py:44
  81.8 3.5 %collective-permute-start.13 = (bf16[32,5248]{1,0:T(8,128)(2,1)S(1)}, bf16[32,5248]{1,0:T(8,128)(2,1)S(1)}, u32[]{:S(2)}, u32[]{:S(2)}) collective-permute-start(bf16[32,5248]{1,0:T(8,128)(2,1)S(1)} %collective-permute-done.11), channel_id=1, source_target_pairs={{0,224},{32,0},{64,32},{96,64},{128,96},{160,128},{192,160},{224,1... | collective-permute-start | bytes 1007624 | tf_op jit(solution)/shard_map/ppermute | solution.py:25
  85.3 3.8 %fusion.88 = bf16[2,8,32,5248]{3,2,1,0:T(8,128)(2,1)} fusion(bf16[2,8,32,5248]{3,2,1,0:T(8,128)(2,1)} %bitcast_dynamic-update-slice_fusion.3, s32[]{:T(128)} %bitcast.28, s32[]{:T(128)} %bitcast.29, bf16[32,5248]{1,0:T(8,128)(2,1)S(1)} %collective-permute-done.8, pred[]{:T(512)} %get-tuple-element.249), kind=kLoop, calls=%fused_computation.140 | loop fusion | flops 167936 | bytes 1009152 | tf_op jit(solution)/shard_map/scatter | solution.py:44
  89.1 3.6 %fusion.87 = bf16[2,8,32,5248]{3,2,1,0:T(8,128)(2,1)} fusion(bf16[2,8,32,5248]{3,2,1,0:T(8,128)(2,1)} %fusion.88, s32[]{:T(128)} %bitcast.31, s32[]{:T(128)} %bitcast.32, bf16[32,5248]{1,0:T(8,128)(2,1)S(1)} %collective-permute-done.9, pred[]{:T(512)} %get-tuple-element.248), kind=kLoop, calls=%fused_computation.138 | loop fusion | flops 167936 | bytes 1009152 | tf_op jit(solution)/shard_map/scatter | solution.py:44
  94.2 3.7 %fusion.86 = bf16[2,8,32,5248]{3,2,1,0:T(8,128)(2,1)} fusion(bf16[2,8,32,5248]{3,2,1,0:T(8,128)(2,1)} %bitcast_dynamic-update-slice_fusion.1, s32[]{:T(128)} %bitcast.36, s32[]{:T(128)} %bitcast.37, bf16[32,5248]{1,0:T(8,128)(2,1)S(1)} %collective-permute-done.12, pred[]{:T(512)} %get-tuple-element.247), kind=kLoop, calls=%fused_computation.134 | loop fusion | flops 167936 | bytes 1009152 | tf_op jit(solution)/shard_map/scatter | solution.py:49
  98.7 12.7 %fusion = f32[512,1296]{0,1:T(8,128)} fusion(bf16[5120,1296]{0,1:T(8,128)(2,1)} %all-gather.2.cloned.1.call-done, bf16[512,5248]{1,0:T(8,128)(2,1)} %bitcast.39), kind=kOutput, calls=%fused_computation | convolution fusion | flops 6794772480 | bytes 21168128 | tf_op jit(solution)/shard_map/dot_general | solution.py:132
  114.1 4.8 %fusion.2 = f32[512,5120]{1,0:T(8,128)S(1)} fusion(bf16[512,432]{0,1:T(8,128)(2,1)S(1)} %fusion.29, bf16[5120,1296]{0,1:T(8,128)(2,1)} %all-gather.2.cloned.1.call-done), kind=kOutput, calls=%fused_computation.2 | convolution fusion | flops 2264924160 | bytes 15351808 | tf_op jit(solution)/shard_map/dot_general | solution.py:136
  121.8 5.2 %collective-permute-done.14 = bf16[32,5120]{1,0:T(8,128)(2,1)S(1)} collective-permute-done((bf16[32,5120]{1,0:T(8,128)(2,1)S(1)}, bf16[32,5120]{1,0:T(8,128)(2,1)S(1)}, u32[]{:S(2)}, u32[]{:S(2)}) %collective-permute-start.14) | collective-permute-done | bytes 327712 | tf_op jit(solution)/shard_map/ppermute | solution.py:25
  127.1 3.6 %collective-permute-start.16 = (bf16[32,5120]{1,0:T(8,128)(2,1)S(1)}, bf16[32,5120]{1,0:T(8,128)(2,1)S(1)}, u32[]{:S(2)}, u32[]{:S(2)}) collective-permute-start(bf16[32,5120]{1,0:T(8,128)(2,1)S(1)} %get-tuple-element.234), channel_id=1, source_target_pairs={{0,224},{32,0},{64,32},{96,64},{128,96},{160,128},{192,160},{224,1... | collective-permute-start | bytes 983048 | tf_op jit(solution)/shard_map/ppermute | solution.py:25
  135.2 3.1 %collective-permute-done.17 = bf16[32,5120]{1,0:T(8,128)(2,1)S(1)} collective-permute-done((bf16[32,5120]{1,0:T(8,128)(2,1)S(1)}, bf16[32,5120]{1,0:T(8,128)(2,1)S(1)}, u32[]{:S(2)}, u32[]{:S(2)}) %collective-permute-start.17) | collective-permute-done | bytes 327712 | tf_op jit(solution)/shard_map/ppermute | solution.py:25
  138.3 3.9 %collective-permute-done.18 = bf16[32,5120]{1,0:T(8,128)(2,1)S(1)} collective-permute-done((bf16[32,5120]{1,0:T(8,128)(2,1)S(1)}, bf16[32,5120]{1,0:T(8,128)(2,1)S(1)}, u32[]{:S(2)}, u32[]{:S(2)}) %collective-permute-start.18) | collective-permute-done | bytes 327712 | tf_op jit(solution)/shard_map/ppermute | solution.py:25
  150.5 11.6 %all-to-all-start.2 = ((bf16[32,16,640]{2,1,0:T(8,128)(2,1)}), bf16[32,16,640]{2,1,0:T(8,128)(2,1)S(1)}, u32[]{:S(2)}, u32[]{:S(2)}) async-start(bf16[32,16,640]{2,1,0:T(8,128)(2,1)} %bitcast.62), calls=%async_computation.2 | async-start | bytes 1310720 | tf_op jit(solution)/shard_map/all_to_all | solution.py:106
  169.6 5.4 %all-to-all-done.2 = bf16[32,16,640]{2,1,0:T(8,128)(2,1)S(1)} async-done(((bf16[32,16,640]{2,1,0:T(8,128)(2,1)}), bf16[32,16,640]{2,1,0:T(8,128)(2,1)S(1)}, u32[]{:S(2)}, u32[]{:S(2)}) %all-to-all-start.2) | async-done | bytes 655392 | tf_op jit(solution)/shard_map/all_to_all | solution.py:106
  175.1 3.3 %collective-permute-done.26 = bf16[32,5120]{1,0:T(8,128)(2,1)S(1)} collective-permute-done((bf16[32,5120]{1,0:T(8,128)(2,1)S(1)}, bf16[32,5120]{1,0:T(8,128)(2,1)S(1)}, u32[]{:S(2)}, u32[]{:S(2)}) %collective-permute-start.26) | collective-permute-done | bytes 327712 | tf_op jit(solution)/shard_map/ppermute | solution.py:25
  182.0 16.5 %all-to-all-start.3 = ((f32[256,1,128]{2,1,0:T(1,128)}), f32[256,1,128]{2,1,0:T(1,128)S(1)}, u32[]{:S(2)}, u32[]{:S(2)}) async-start(f32[256,1,128]{2,1,0:T(1,128)} %broadcast_in_dim.31), calls=%async_computation.3 | async-start | bytes 262144 | tf_op jit(solution)/shard_map/all_to_all | solution.py:150
  199.6 11.9 %all-to-all-done.3 = f32[256,1,128]{2,1,0:T(1,128)S(1)} async-done(((f32[256,1,128]{2,1,0:T(1,128)}), f32[256,1,128]{2,1,0:T(1,128)S(1)}, u32[]{:S(2)}, u32[]{:S(2)}) %all-to-all-start.3) | async-done | bytes 131104 | tf_op jit(solution)/shard_map/all_to_all | solution.py:150
  211.5 4.1 %all-to-all-start.1 = ((bf16[32,16,640]{2,1,0:T(8,128)(2,1)}), bf16[32,16,640]{2,1,0:T(8,128)(2,1)S(1)}, u32[]{:S(2)}, u32[]{:S(2)}) async-start(bf16[32,16,640]{2,1,0:T(8,128)(2,1)} %bitcast.59), calls=%async_computation.1 | async-start | bytes 1310720 | tf_op jit(solution)/shard_map/all_to_all | solution.py:144
  217.7 10.9 %all-to-all-done.1 = bf16[32,16,640]{2,1,0:T(8,128)(2,1)S(1)} async-done(((bf16[32,16,640]{2,1,0:T(8,128)(2,1)}), bf16[32,16,640]{2,1,0:T(8,128)(2,1)S(1)}, u32[]{:S(2)}, u32[]{:S(2)}) %all-to-all-start.1) | async-done | bytes 655392 | tf_op jit(solution)/shard_map/all_to_all | solution.py:144
  (141 shorter events, 76.5 us)
Async XLA Ops:
  10.8 22.8 %all-to-all-start = ((bf16[32,16,768]{2,1,0:T(8,128)(2,1)}), bf16[32,16,768]{2,1,0:T(8,128)(2,1)S(1)}, u32[]{:S(2)}, u32[]{:S(2)}) async-start(bf16[32,16,768]{2,1,0:T(8,128)(2,1)} %bitcast.4), calls=%async_computation | async-start | bytes 1572864 | tf_op jit(solution)/shard_map/all_to_all | solution.py:103
  19.4 79.3 %all-gather.2.cloned.1.call-start = ((), (), s32[]{:S(2)}) async-start(), calls=%async_computation.4 | async-start | bytes 14929920 | tf_op jit(solution)/shard_map/all_gather | solution.py:89
  34.3 13.5 %collective-permute-start = (bf16[32,5248]{1,0:T(8,128)(2,1)S(1)}, bf16[32,5248]{1,0:T(8,128)(2,1)S(1)}, u32[]{:S(2)}, u32[]{:S(2)}) collective-permute-start(bf16[32,5248]{1,0:T(8,128)(2,1)S(1)} %bitcast.202), channel_id=1, source_target_pairs={{0,32},{32,64},{64,96},{96,128},{128,160},{160,192},{192,224},{224... | collective-permute-start | bytes 1007624 | tf_op jit(solution)/shard_map/ppermute | solution.py:25
  40.0 14.9 %collective-permute-start.2 = (bf16[32,5248]{1,0:T(8,128)(2,1)S(1)}, bf16[32,5248]{1,0:T(8,128)(2,1)S(1)}, u32[]{:S(2)}, u32[]{:S(2)}) collective-permute-start(bf16[32,5248]{1,0:T(8,128)(2,1)S(1)} %bitcast.205), channel_id=1, source_target_pairs={{0,32},{32,64},{64,96},{96,128},{128,160},{160,192},{192,224},{224... | collective-permute-start | bytes 1007624 | tf_op jit(solution)/shard_map/ppermute | solution.py:25
  40.0 14.9 %collective-permute-start.3 = (bf16[32,5248]{1,0:T(8,128)(2,1)S(1)}, bf16[32,5248]{1,0:T(8,128)(2,1)S(1)}, u32[]{:S(2)}, u32[]{:S(2)}) collective-permute-start(bf16[32,5248]{1,0:T(8,128)(2,1)S(1)} %bitcast.206), channel_id=1, source_target_pairs={{0,224},{32,0},{64,32},{96,64},{128,96},{160,128},{192,160},{224,1... | collective-permute-start | bytes 1007624 | tf_op jit(solution)/shard_map/ppermute | solution.py:25
  47.8 17.1 %collective-permute-start.4 = (bf16[32,5248]{1,0:T(8,128)(2,1)S(1)}, bf16[32,5248]{1,0:T(8,128)(2,1)S(1)}, u32[]{:S(2)}, u32[]{:S(2)}) collective-permute-start(bf16[32,5248]{1,0:T(8,128)(2,1)S(1)} %collective-permute-done), channel_id=1, source_target_pairs={{0,32},{32,64},{64,96},{96,128},{128,160},{160,192},{192,224},{224... | collective-permute-start | bytes 1007624 | tf_op jit(solution)/shard_map/ppermute | solution.py:25
  47.8 17.1 %collective-permute-start.5 = (bf16[32,5248]{1,0:T(8,128)(2,1)S(1)}, bf16[32,5248]{1,0:T(8,128)(2,1)S(1)}, u32[]{:S(2)}, u32[]{:S(2)}) collective-permute-start(bf16[32,5248]{1,0:T(8,128)(2,1)S(1)} %collective-permute-done.1), channel_id=1, source_target_pairs={{0,224},{32,0},{64,32},{96,64},{128,96},{160,128},{192,160},{224,1... | collective-permute-start | bytes 1007624 | tf_op jit(solution)/shard_map/ppermute | solution.py:25
  55.0 14.4 %collective-permute-start.6 = (bf16[32,5248]{1,0:T(8,128)(2,1)S(1)}, bf16[32,5248]{1,0:T(8,128)(2,1)S(1)}, u32[]{:S(2)}, u32[]{:S(2)}) collective-permute-start(bf16[32,5248]{1,0:T(8,128)(2,1)S(1)} %collective-permute-done.2), channel_id=1, source_target_pairs={{0,32},{32,64},{64,96},{96,128},{128,160},{160,192},{192,224},{224... | collective-permute-start | bytes 1007624 | tf_op jit(solution)/shard_map/ppermute | solution.py:25
  55.0 14.4 %collective-permute-start.7 = (bf16[32,5248]{1,0:T(8,128)(2,1)S(1)}, bf16[32,5248]{1,0:T(8,128)(2,1)S(1)}, u32[]{:S(2)}, u32[]{:S(2)}) collective-permute-start(bf16[32,5248]{1,0:T(8,128)(2,1)S(1)} %collective-permute-done.3), channel_id=1, source_target_pairs={{0,224},{32,0},{64,32},{96,64},{128,96},{160,128},{192,160},{224,1... | collective-permute-start | bytes 1007624 | tf_op jit(solution)/shard_map/ppermute | solution.py:25
  64.8 16.1 %collective-permute-start.8 = (bf16[32,5248]{1,0:T(8,128)(2,1)S(1)}, bf16[32,5248]{1,0:T(8,128)(2,1)S(1)}, u32[]{:S(2)}, u32[]{:S(2)}) collective-permute-start(bf16[32,5248]{1,0:T(8,128)(2,1)S(1)} %collective-permute-done.4), channel_id=1, source_target_pairs={{0,32},{32,64},{64,96},{96,128},{128,160},{160,192},{192,224},{224... | collective-permute-start | bytes 1007624 | tf_op jit(solution)/shard_map/ppermute | solution.py:25
  64.8 16.1 %collective-permute-start.9 = (bf16[32,5248]{1,0:T(8,128)(2,1)S(1)}, bf16[32,5248]{1,0:T(8,128)(2,1)S(1)}, u32[]{:S(2)}, u32[]{:S(2)}) collective-permute-start(bf16[32,5248]{1,0:T(8,128)(2,1)S(1)} %collective-permute-done.5), channel_id=1, source_target_pairs={{0,224},{32,0},{64,32},{96,64},{128,96},{160,128},{192,160},{224,1... | collective-permute-start | bytes 1007624 | tf_op jit(solution)/shard_map/ppermute | solution.py:25
  69.3 23.3 %collective-permute-start.10 = (bf16[32,5248]{1,0:T(8,128)(2,1)S(1)}, bf16[32,5248]{1,0:T(8,128)(2,1)S(1)}, u32[]{:S(2)}, u32[]{:S(2)}) collective-permute-start(bf16[32,5248]{1,0:T(8,128)(2,1)S(1)} %collective-permute-done.6), channel_id=1, source_target_pairs={{0,32},{32,64},{64,96},{96,128},{128,160},{160,192},{192,224},{224... | collective-permute-start | bytes 1007624 | tf_op jit(solution)/shard_map/ppermute | solution.py:25
  69.4 12.4 %collective-permute-start.11 = (bf16[32,5248]{1,0:T(8,128)(2,1)S(1)}, bf16[32,5248]{1,0:T(8,128)(2,1)S(1)}, u32[]{:S(2)}, u32[]{:S(2)}) collective-permute-start(bf16[32,5248]{1,0:T(8,128)(2,1)S(1)} %collective-permute-done.7), channel_id=1, source_target_pairs={{0,224},{32,0},{64,32},{96,64},{128,96},{160,128},{192,160},{224,1... | collective-permute-start | bytes 1007624 | tf_op jit(solution)/shard_map/ppermute | solution.py:25
  80.9 13.2 %collective-permute-start.12 = (bf16[32,5248]{1,0:T(8,128)(2,1)S(1)}, bf16[32,5248]{1,0:T(8,128)(2,1)S(1)}, u32[]{:S(2)}, u32[]{:S(2)}) collective-permute-start(bf16[32,5248]{1,0:T(8,128)(2,1)S(1)} %collective-permute-done.8), channel_id=1, source_target_pairs={{0,32},{32,64},{64,96},{96,128},{128,160},{160,192},{192,224},{224... | collective-permute-start | bytes 1007624 | tf_op jit(solution)/shard_map/ppermute | solution.py:25
  81.8 16.1 %collective-permute-start.13 = (bf16[32,5248]{1,0:T(8,128)(2,1)S(1)}, bf16[32,5248]{1,0:T(8,128)(2,1)S(1)}, u32[]{:S(2)}, u32[]{:S(2)}) collective-permute-start(bf16[32,5248]{1,0:T(8,128)(2,1)S(1)} %collective-permute-done.11), channel_id=1, source_target_pairs={{0,224},{32,0},{64,32},{96,64},{128,96},{160,128},{192,160},{224,1... | collective-permute-start | bytes 1007624 | tf_op jit(solution)/shard_map/ppermute | solution.py:25
  133.4 11.9 %collective-permute-start.19 = (bf16[32,5120]{1,0:T(8,128)(2,1)S(1)}, bf16[32,5120]{1,0:T(8,128)(2,1)S(1)}, u32[]{:S(2)}, u32[]{:S(2)}) collective-permute-start(bf16[32,5120]{1,0:T(8,128)(2,1)S(1)} %get-tuple-element.237), channel_id=1, source_target_pairs={{0,32},{32,64},{64,96},{96,128},{128,160},{160,192},{192,224},{224... | collective-permute-start | bytes 983048 | tf_op jit(solution)/shard_map/ppermute | solution.py:25
  145.6 16.4 %collective-permute-start.20 = (bf16[32,5120]{1,0:T(8,128)(2,1)S(1)}, bf16[32,5120]{1,0:T(8,128)(2,1)S(1)}, u32[]{:S(2)}, u32[]{:S(2)}) collective-permute-start(bf16[32,5120]{1,0:T(8,128)(2,1)S(1)} %get-tuple-element.238), channel_id=1, source_target_pairs={{0,224},{32,0},{64,32},{96,64},{128,96},{160,128},{192,160},{224,1... | collective-permute-start | bytes 983048 | tf_op jit(solution)/shard_map/ppermute | solution.py:25
  146.9 15.2 %collective-permute-start.21 = (bf16[32,5120]{1,0:T(8,128)(2,1)S(1)}, bf16[32,5120]{1,0:T(8,128)(2,1)S(1)}, u32[]{:S(2)}, u32[]{:S(2)}) collective-permute-start(bf16[32,5120]{1,0:T(8,128)(2,1)S(1)} %get-tuple-element.239), channel_id=1, source_target_pairs={{0,32},{32,64},{64,96},{96,128},{128,160},{160,192},{192,224},{224... | collective-permute-start | bytes 983048 | tf_op jit(solution)/shard_map/ppermute | solution.py:25
  147.4 14.7 %collective-permute-start.22 = (bf16[32,5120]{1,0:T(8,128)(2,1)S(1)}, bf16[32,5120]{1,0:T(8,128)(2,1)S(1)}, u32[]{:S(2)}, u32[]{:S(2)}) collective-permute-start(bf16[32,5120]{1,0:T(8,128)(2,1)S(1)} %get-tuple-element.240), channel_id=1, source_target_pairs={{0,224},{32,0},{64,32},{96,64},{128,96},{160,128},{192,160},{224,1... | collective-permute-start | bytes 983048 | tf_op jit(solution)/shard_map/ppermute | solution.py:25
  149.6 12.5 %collective-permute-start.23 = (bf16[32,5120]{1,0:T(8,128)(2,1)S(1)}, bf16[32,5120]{1,0:T(8,128)(2,1)}, u32[]{:S(2)}, u32[]{:S(2)}) collective-permute-start(bf16[32,5120]{1,0:T(8,128)(2,1)S(1)} %get-tuple-element.241), channel_id=1, source_target_pairs={{0,32},{32,64},{64,96},{96,128},{128,160},{160,192},{192,224},{224... | collective-permute-start | bytes 983048 | tf_op jit(solution)/shard_map/ppermute | solution.py:25
  150.5 24.5 %all-to-all-start.2 = ((bf16[32,16,640]{2,1,0:T(8,128)(2,1)}), bf16[32,16,640]{2,1,0:T(8,128)(2,1)S(1)}, u32[]{:S(2)}, u32[]{:S(2)}) async-start(bf16[32,16,640]{2,1,0:T(8,128)(2,1)} %bitcast.62), calls=%async_computation.2 | async-start | bytes 1310720 | tf_op jit(solution)/shard_map/all_to_all | solution.py:106
  166.9 12.0 %collective-permute-start.27 = (bf16[32,5120]{1,0:T(8,128)(2,1)S(1)}, bf16[32,5120]{1,0:T(8,128)(2,1)}, u32[]{:S(2)}, u32[]{:S(2)}) collective-permute-start(bf16[32,5120]{1,0:T(8,128)(2,1)S(1)} %get-tuple-element.245), channel_id=1, source_target_pairs={{0,224},{32,0},{64,32},{96,64},{128,96},{160,128},{192,160},{224,1... | collective-permute-start | bytes 983048 | tf_op jit(solution)/shard_map/ppermute | solution.py:25
  182.0 29.5 %all-to-all-start.3 = ((f32[256,1,128]{2,1,0:T(1,128)}), f32[256,1,128]{2,1,0:T(1,128)S(1)}, u32[]{:S(2)}, u32[]{:S(2)}) async-start(f32[256,1,128]{2,1,0:T(1,128)} %broadcast_in_dim.31), calls=%async_computation.3 | async-start | bytes 262144 | tf_op jit(solution)/shard_map/all_to_all | solution.py:150
  211.5 17.1 %all-to-all-start.1 = ((bf16[32,16,640]{2,1,0:T(8,128)(2,1)}), bf16[32,16,640]{2,1,0:T(8,128)(2,1)S(1)}, u32[]{:S(2)}, u32[]{:S(2)}) async-start(bf16[32,16,640]{2,1,0:T(8,128)(2,1)} %bitcast.59), calls=%async_computation.1 | async-start | bytes 1310720 | tf_op jit(solution)/shard_map/all_to_all | solution.py:144
  (15 other events, 239.3 us)
Sparse Core Ops, SparseCore 0:
  22.3 75.6 all-gather.1

commit v3 on v1

--- a/solution.py
+++ b/solution.py
@@ -3,6 +3,8 @@
 import jax
 import jax.numpy as jnp
 from jax import lax
+from jax.experimental import pallas as pl
+from jax.experimental.pallas import tpu as pltpu
 from jax.sharding import Mesh
 from jax.sharding import PartitionSpec as P
 
@@ -42,22 +44,103 @@
 
 def ring_scatter(chunks):
     half = Z // 2
-    ends = [[None, None] for _ in chunks]
+    rows = chunks[0].shape[0] // Z
+    ends = [{} for _ in chunks]
     for step in range(half, 0, -1):
-        for k, blocks in enumerate(chunks):
+        for k, chunk in enumerate(chunks):
+            sends = {}
             for side, sign in ((0, 1), (1, -1)):
                 if step == half and side != k % 2:
                     continue
-                send = blocks[(sign * step) % Z]
-                if ends[k][side] is not None:
-                    send = send + ends[k][side]
-                ends[k][side] = shift(send.astype(BF16), sign).astype(F32)
-    return [blocks[0] + end[0] + end[1] for blocks, end in zip(chunks, ends)]
+                place = (sign * step) % Z
+                block = chunk[place * rows : (place + 1) * rows]
+                if sign in ends[k]:
+                    block = block + ends[k][sign]
+                else:
+                    block = lax.optimization_barrier(block)
+                sends[sign] = block.astype(BF16)
+            sends = lax.optimization_barrier(sends)
+            ends[k] = {sign: shift(value, sign).astype(F32) for sign, value in sends.items()}
+    return [chunk[:rows] + end[1] + end[-1] for chunk, end in zip(chunks, ends)]
+
+
+def layer_kernel(count, steps, units, *refs):
+    blocks, (w_ref, corr_ref, *outs, acc, down, hidden) = refs[:count], refs[count:]
+    step = pl.program_id(0)
+    skip = units // LANES * LANES
+
+    @pl.when(step < steps)
+    def _():
+        down[step] = w_ref[:, :units]
+        rows = jnp.concatenate([block[...] for block in blocks], axis=0)
+        part = jnp.dot(rows, w_ref[:, skip:], preferred_element_type=F32)
+
+        @pl.when(step == 0)
+        def _():
+            acc[...] = part
+
+        @pl.when(step > 0)
+        def _():
+            acc[...] += part
+
+    @pl.when(step == steps - 1)
+    def _():
+        both = acc[...]
+        gate = both[:, units - skip : 2 * units - skip]
+        up = both[:, 2 * units - skip :] + SIGMA * corr_ref[...]
+        hidden[...] = (gate / (1.0 + jnp.exp(-gate)) * up).astype(BF16)
+
+    @pl.when(step >= steps)
+    def _():
+        out = lax.dot_general(
+            hidden[...], down[step - steps], (((1,), (1,)), ((), ())), preferred_element_type=F32
+        )
+        rows = out.shape[0] // len(outs)
+        for k, ref in enumerate(outs):
+            ref[...] = out[k * rows : (k + 1) * rows]
+
+
+def layer(blocks, weights, corr, steps):
+    count = len(blocks)
+    rows, units = corr.shape
+    model, wide = weights.shape
+    feat = model // steps
+    small = blocks[0].shape[0]
+    skip = units // LANES * LANES
+    return pl.pallas_call(
+        lambda *refs: layer_kernel(count, steps, units, *refs),
+        grid=(2 * steps,),
+        in_specs=[pl.BlockSpec((small, feat), lambda i: (0, jnp.minimum(i, steps - 1)))] * count
+        + [
+            pl.BlockSpec((feat, wide), lambda i: (jnp.minimum(i, steps - 1), 0)),
+            pl.BlockSpec((rows, units), lambda i: (0, 0)),
+        ],
+        out_specs=[pl.BlockSpec((rows // 2, feat), lambda i: (0, jnp.maximum(i - steps, 0)))] * 2,
+        out_shape=[jax.ShapeDtypeStruct((rows // 2, model), F32)] * 2,
+        scratch_shapes=[
+            pltpu.VMEM((rows, wide - skip), F32),
+            pltpu.VMEM((steps, feat, units), BF16),
+            pltpu.VMEM((rows, units), BF16),
+        ],
+        compiler_params=pltpu.CompilerParams(
+            dimension_semantics=("arbitrary",), vmem_limit_bytes=40 * 1024 * 1024
+        ),
+        cost_estimate=pl.CostEstimate(
+            flops=2 * rows * model * wide,
+            bytes_accessed=2 * model * (wide + rows) + 4 * rows * model,
+            transcendentals=rows * units,
+        ),
+    )(*blocks, weights, corr)
 
 
 def split_two(value):
     high = value.astype(BF16)
     return high, (value - high.astype(F32)).astype(BF16)
+
+
+def split_three(value):
+    high = value.astype(BF16)
+    return (high,) + split_two(value - high.astype(F32))
 
 
 def body(tokens, target, w_gate, w_up, w_down, factor_u, factor_v):
@@ -71,9 +154,7 @@
     z, y = lax.axis_index("z"), lax.axis_index("y")
     x, core = lax.axis_index("x"), lax.axis_index("core")
 
-    weights = lax.all_gather(
-        jnp.concatenate([w_down.T, w_gate, w_up], axis=1), COL, axis=0, tiled=True
-    )
+    packed = jnp.concatenate([w_down.T, w_gate, w_up], axis=1)
     v_twice = jnp.concatenate([factor_v, factor_v], axis=0)
 
     first = (z * Y + y) * local * RANK
@@ -85,7 +166,13 @@
     extra = jnp.pad(extra, ((0, 0), (0, LANES - extra.shape[1])))
     wide = jnp.concatenate([tokens, extra], axis=1).reshape(1, cols, own, dev_feat + LANES)
     wide = jnp.broadcast_to(wide, (Y, cols, own, dev_feat + LANES))
+    packed, wide = lax.optimization_barrier((packed, wide))
+    weights = lax.all_gather(packed, COL, axis=0, tiled=True)
     moved = lax.all_to_all(wide.reshape(Y * cols, own, dev_feat + LANES), PLANE, 0, 0, tiled=True)
+    target, moved = lax.optimization_barrier((target, moved))
+    goal = jnp.broadcast_to(target.reshape(1, cols, own, dev_feat), (Y, cols, own, dev_feat))
+    goal = lax.all_to_all(goal.reshape(Y * cols, own, dev_feat), PLANE, 0, 0, tiled=True)
+    goal = jnp.swapaxes(goal.reshape(Y, cols, own, dev_feat), 1, 2).reshape(Y, own, model)
     moved = moved.reshape(Y, cols, own, dev_feat + LANES)
     part = moved[..., dev_feat:].astype(F32)
     part = part[..., :RANK] + part[..., RANK : 2 * RANK]
@@ -96,8 +183,8 @@
     plane = Y * own
     mid = plane // 2
 
-    gathered = ring_gather([rows[:mid], rows[mid:]])
-    every = jnp.concatenate(gathered[0] + gathered[1], axis=0)
+    first, second = ring_gather([rows[:mid], rows[mid:]])
+    blocks = first + second
 
     row = lax.broadcasted_iota(jnp.int32, (Z * plane, members * RANK * 2), 0)
     column = lax.broadcasted_iota(jnp.int32, (Z * plane, members * RANK * 2), 1)
@@ -107,33 +194,32 @@
     spread_row = lax.broadcasted_iota(jnp.int32, (LANES, members * RANK * 2), 0)
     spread_col = lax.broadcasted_iota(jnp.int32, (LANES, members * RANK * 2), 1)
     spread = spread_col // (members * RANK) * RANK + spread_col % RANK == spread_row
-    low = jnp.dot(every[:, model:], spread.astype(BF16), preferred_element_type=F32)
+    low = jnp.dot(
+        jnp.concatenate([block[:, model:] for block in blocks], axis=0),
+        spread.astype(BF16),
+        preferred_element_type=F32,
+    )
     low = jnp.where(column % (members * RANK) // RANK == member, low, 0.0).astype(BF16)
     corr = jnp.dot(low, v_twice, preferred_element_type=F32)
 
-    both = jnp.dot(every[:, :model], weights, preferred_element_type=F32)
-    gate, up = both[:, units : 2 * units], both[:, 2 * units :] + SIGMA * corr
-    hidden = (jax.nn.silu(gate) * up).astype(BF16)
-    hidden, weights = lax.optimization_barrier((hidden, weights))
-    out = lax.dot_general(
-        hidden, weights[:, :units], (((1,), (1,)), ((), ())), preferred_element_type=F32
-    )
-    out = out.reshape(2, Z, mid, model)
-    sums = ring_scatter([[out[k, d] for d in range(Z)] for k in range(2)])
-    back = jnp.concatenate([s.astype(BF16) for s in sums], axis=0).reshape(Y, own, cols, dev_feat)
-    back = jnp.swapaxes(back, 1, 2).reshape(Y * cols, own, dev_feat)
-    back = lax.all_to_all(back, PLANE, 0, 0, tiled=True).reshape(Y, dev_rows, dev_feat)
-    final = jnp.sum(back.astype(F32), axis=0)
-    mixed = final.astype(BF16)
-
-    score = jnp.sum((final * target.astype(F32)).reshape(local, SEQ, dev_feat), axis=(1, 2))
-    score = jnp.pad(score / math.sqrt(SEQ * D), (0, LANES - local))
-    devices = Z * Y * cols
-    scores = lax.all_to_all(
-        jnp.broadcast_to(score, (devices, 1, LANES)), ALL, 0, 0, tiled=True
-    )
-    scores = scores.reshape(Z * Y, cols, LANES)[:, :, :local]
-    fitness = jnp.sum(scores, axis=1).reshape(members)
+    sums = ring_scatter(layer(blocks, weights, corr, cols))
+    total = jnp.concatenate(sums, axis=0).reshape(Y, own, model)
+    score = jnp.sum(total * goal.astype(F32), axis=(1, 2)) / math.sqrt(SEQ * D)
+    score = jnp.concatenate(split_three(score))
+    score = jnp.broadcast_to(jnp.pad(score, (0, LANES - score.shape[0])), (Y * cols, own, LANES))
+
+    back = jnp.swapaxes(total.astype(BF16).reshape(Y, own, cols, dev_feat), 1, 2)
+    back = jnp.concatenate([back.reshape(Y * cols, own, dev_feat), score], axis=2)
+    back = lax.all_to_all(back, PLANE, 0, 0, tiled=True)
+    mixed = jnp.sum(back[..., :dev_feat].reshape(Y, dev_rows, dev_feat).astype(F32), axis=0)
+    mixed = mixed.astype(BF16)
+
+    score = back[:, 0, dev_feat : dev_feat + 3 * Y].astype(F32).reshape(Y, local, cols // local, 3, Y)
+    score = (score[..., 2, :] + score[..., 1, :]) + score[..., 0, :]
+    score = jnp.sum(score, axis=(0, 2)).T.reshape(Y * local)
+    score = jnp.broadcast_to(jnp.pad(score, (0, LANES - Y * local)), (Z, 1, LANES))
+    score = lax.all_to_all(score, "z", 0, 0, tiled=True)
+    fitness = score[:, 0, : Y * local].reshape(members)
 
     scale = jnp.repeat(fitness, RANK) * math.sqrt(D / members)
     scaled = jnp.concatenate(split_two(factor_u.astype(F32) * scale[None, :]), axis=1)

time: 263 us -> 239 us (0.909)
  blocking collectives: 55 us -> 20.6 us
  Pallas kernels: 0 us -> 24.4 us
  matrix products: 22.9 us -> 5.81 us
  waiting for transfers between devices: 94.9 us -> 82.5 us
  starting transfers between devices: 51.1 us -> 63 us
  local copies, waits for them, and re-layouts: 15.7 us -> 21.4 us
    all_to_all x2 -> x1, blocking collectives: 55 us -> 20.6 us  [body(): back = lax.all_to_all(back, PLANE, 0, 0, tiled=True)]
    pallas_call x0 -> x1, Pallas kernels: none -> 24.4 us  [layer(): pl.pallas_call(lambda *refs: layer_kernel(count, steps, units, *refs), gr...]
    dot_general x2 -> x0, matrix products: 17.5 us -> none  [the longest x1 12.7 us: body(): both = jnp.dot(every[:, :model], weights, preferred_element_type=F32)]
    ppermute x28, waiting for transfers between devices: 79.5 us -> 62.4 us  [shift(): return lax.ppermute(value, 'z', [(i, (i + step) % Z) for i in range(Z)])]
    all_to_all x0 -> x2, starting transfers between devices: none -> 11.6 us  [the longest x1 6.56 us: body(): lax.all_to_all(goal.reshape(Y * cols, own, dev_feat), PLANE, 0, 0, tiled=...]
    all_to_all x0 -> x2, waiting for transfers between devices: none -> 5.63 us  [the longest x1 5.63 us: body(): score = lax.all_to_all(score, 'z', 0, 0, tiled=True)]
    another operation x1 -> x0, other arithmetic: 3.1 us -> none
    unnamed x30 -> x68, local copies, waits for them, and re-layouts: 11.7 us -> 14 us
  transfers between devices with their start and end apart: 30 -> 32, of which waited for: 21 -> 21; matrix products, arithmetic and copies ran while one was open for 6% -> 4% of each run, Pallas kernels for 0% -> 10%
where the time goes in v3:
time: 239 us; the launch traced here: 238 us
  waiting for transfers between devices  82.5 us (35%)
  starting transfers between devices  63 us (26%)
  Pallas kernels  24.4 us (10%)
  local copies, waits for them, and re-layouts  21.4 us (9%)
  blocking collectives  20.6 us (9%)
  between operations  14.6 us (6%)
  other arithmetic  5.95 us (2%)
  matrix products  5.81 us (2%)
    ppermute x28, waiting for transfers between devices, shift(): return lax.ppermute(value, 'z', [(i, (i + step) % Z) for i in range(Z)])  62.4 us
    ppermute x28, starting transfers between devices, shift(): return lax.ppermute(value, 'z', [(i, (i + step) % Z) for i in range(Z)])  42.8 us
    pallas_call x1, Pallas kernels, layer(): pl.pallas_call(lambda *refs: layer_kernel(count, steps, units, *refs), gr...  24.4 us
    all_to_all x1, blocking collectives, body(): back = lax.all_to_all(back, PLANE, 0, 0, tiled=True)  20.6 us
    all_to_all x1, waiting for transfers between devices, body(): lax.all_to_all(wide.reshape(Y * cols, own, dev_feat + LANES), PLANE, 0, 0...  14.2 us
    unnamed x68, local copies, waits for them, and re-layouts  14 us
    all_to_all x1, starting transfers between devices, body(): lax.all_to_all(wide.reshape(Y * cols, own, dev_feat + LANES), PLANE, 0, 0...  8.6 us
    all_to_all x1, starting transfers between devices, body(): lax.all_to_all(goal.reshape(Y * cols, own, dev_feat), PLANE, 0, 0, tiled=...  6.56 us
  transfers between devices with their start and end apart: 32, of which 21 were waited for; matrix products, arithmetic and copies ran while one was open for 4% of the time, Pallas kernels for 10%

profile of v3, /device:TPU:1, one launch (start us, length us, event | category | flops | bytes accessed | tf_op | source)
XLA Modules:
  0.0 238.1 jit_solution(17329222950883581014)
XLA Ops:
  15.2 8.6 %all-to-all-start = ((bf16[32,16,768]{2,1,0:T(8,128)(2,1)}), bf16[32,16,768]{2,1,0:T(8,128)(2,1)S(1)}, u32[]{:S(2)}, u32[]{:S(2)}) async-start(bf16[32,16,768]{2,1,0:T(8,128)(2,1)} %bitcast.5), calls=%async_computation | async-start | bytes 1572864 | tf_op jit(solution)/shard_map/all_to_all | solution.py:171
  23.8 14.2 %all-to-all-done = bf16[32,16,768]{2,1,0:T(8,128)(2,1)S(1)} async-done(((bf16[32,16,768]{2,1,0:T(8,128)(2,1)}), bf16[32,16,768]{2,1,0:T(8,128)(2,1)S(1)}, u32[]{:S(2)}, u32[]{:S(2)}) %all-to-all-start) | async-done | bytes 786464 | tf_op jit(solution)/shard_map/all_to_all | solution.py:171
  40.4 6.0 %collective-permute-start = (bf16[32,5248]{1,0:T(8,128)(2,1)S(1)}, bf16[32,5248]{1,0:T(8,128)(2,1)S(1)}, u32[]{:S(2)}, u32[]{:S(2)}) collective-permute-start(bf16[32,5248]{1,0:T(8,128)(2,1)S(1)} %bitcast.51), channel_id=1, source_target_pairs={{0,224},{32,0},{64,32},{96,64},{128,96},{160,128},{192,160},{224,1... | collective-permute-start | bytes 1007624 | tf_op jit(solution)/shard_map/ppermute | solution.py:27
  47.1 6.4 %collective-permute-done.3.refs_7_ = bf16[32,5248]{1,0:T(8,128)(2,1)S(1)} collective-permute-done((bf16[32,5248]{1,0:T(8,128)(2,1)S(1)}, bf16[32,5248]{1,0:T(8,128)(2,1)S(1)}, u32[]{:S(2)}, u32[]{:S(2)}) %collective-permute-start.3) | collective-permute-done | bytes 335904 | tf_op jit(solution)/shard_map/ppermute | solution.py:27
  53.7 3.0 %collective-permute-start.1 = (bf16[32,5248]{1,0:T(8,128)(2,1)S(1)}, bf16[32,5248]{1,0:T(8,128)(2,1)S(1)}, u32[]{:S(2)}, u32[]{:S(2)}) collective-permute-start(bf16[32,5248]{1,0:T(8,128)(2,1)S(1)} %collective-permute-done.refs_1_), channel_id=1, source_target_pairs={{0,224},{32,0},{64,32},{96,64},{128,96},{160,128},{192,160},{224,1... | collective-permute-start | bytes 1007624 | tf_op jit(solution)/shard_map/ppermute | solution.py:27
  56.7 3.7 %collective-permute-done.7.refs_9_ = bf16[32,5248]{1,0:T(8,128)(2,1)S(1)} collective-permute-done((bf16[32,5248]{1,0:T(8,128)(2,1)S(1)}, bf16[32,5248]{1,0:T(8,128)(2,1)S(1)}, u32[]{:S(2)}, u32[]{:S(2)}) %collective-permute-start.7) | collective-permute-done | bytes 335904 | tf_op jit(solution)/shard_map/ppermute | solution.py:27
  60.4 3.5 %collective-permute-start.8 = (bf16[32,5248]{1,0:T(8,128)(2,1)S(1)}, bf16[32,5248]{1,0:T(8,128)(2,1)S(1)}, u32[]{:S(2)}, u32[]{:S(2)}) collective-permute-start(bf16[32,5248]{1,0:T(8,128)(2,1)S(1)} %collective-permute-done.7.refs_9_), channel_id=1, source_target_pairs={{0,224},{32,0},{64,32},{96,64},{128,96},{160,128},{192,160},{224,1... | collective-permute-start | bytes 1007624 | tf_op jit(solution)/shard_map/ppermute | solution.py:27
  65.0 6.6 %all-to-all-start.1 = ((bf16[32,16,640]{2,1,0:T(8,128)(2,1)}), bf16[32,16,640]{2,1,0:T(8,128)(2,1)}, u32[]{:S(2)}, u32[]{:S(2)}) async-start(bf16[32,16,640]{2,1,0:T(8,128)(2,1)} %bitcast.60), calls=%async_computation.1 | async-start | bytes 1310720 | tf_op jit(solution)/shard_map/all_to_all | solution.py:174
  74.8 3.5 %collective-permute-start.9 = (bf16[32,5248]{1,0:T(8,128)(2,1)S(1)}, bf16[32,5248]{1,0:T(8,128)(2,1)S(1)}, u32[]{:S(2)}, u32[]{:S(2)}) collective-permute-start(bf16[32,5248]{1,0:T(8,128)(2,1)S(1)} %collective-permute-done.8.refs_10_), channel_id=1, source_target_pairs={{0,224},{32,0},{64,32},{96,64},{128,96},{160,128},{192,160},{224,1... | collective-permute-start | bytes 1007624 | tf_op jit(solution)/shard_map/ppermute | solution.py:27
  78.4 6.7 %collective-permute-done.12.refs_14_ = bf16[32,5248]{1,0:T(8,128)(2,1)S(1)} collective-permute-done((bf16[32,5248]{1,0:T(8,128)(2,1)S(1)}, bf16[32,5248]{1,0:T(8,128)(2,1)S(1)}, u32[]{:S(2)}, u32[]{:S(2)}) %collective-permute-start.12) | collective-permute-done | bytes 335904 | tf_op jit(solution)/shard_map/ppermute | solution.py:27
  85.0 3.1 %collective-permute-done.9.refs_11_ = bf16[32,5248]{1,0:T(8,128)(2,1)S(1)} collective-permute-done((bf16[32,5248]{1,0:T(8,128)(2,1)S(1)}, bf16[32,5248]{1,0:T(8,128)(2,1)S(1)}, u32[]{:S(2)}, u32[]{:S(2)}) %collective-permute-start.9) | collective-permute-done | bytes 335904 | tf_op jit(solution)/shard_map/ppermute | solution.py:27
  88.2 3.5 %collective-permute-start.10 = (bf16[32,5248]{1,0:T(8,128)(2,1)S(1)}, bf16[32,5248]{1,0:T(8,128)(2,1)S(1)}, u32[]{:S(2)}, u32[]{:S(2)}) collective-permute-start(bf16[32,5248]{1,0:T(8,128)(2,1)S(1)} %collective-permute-done.9.refs_11_), channel_id=1, source_target_pairs={{0,224},{32,0},{64,32},{96,64},{128,96},{160,128},{192,160},{224,1... | collective-permute-start | bytes 1007624 | tf_op jit(solution)/shard_map/ppermute | solution.py:27
  94.0 3.3 %collective-permute-done.10.refs_12_ = bf16[32,5248]{1,0:T(8,128)(2,1)S(1)} collective-permute-done((bf16[32,5248]{1,0:T(8,128)(2,1)S(1)}, bf16[32,5248]{1,0:T(8,128)(2,1)S(1)}, u32[]{:S(2)}, u32[]{:S(2)}) %collective-permute-start.10) | collective-permute-done | bytes 335904 | tf_op jit(solution)/shard_map/ppermute | solution.py:27
  111.2 24.4 %shard_map.94 = (f32[256,5120]{1,0:T(8,128)S(1)}, f32[256,5120]{1,0:T(8,128)}) custom-call(bf16[32,5248]{1,0:T(8,128)(2,1)S(1)} %bitcast.53, bf16[32,5248]{1,0:T(8,128)(2,1)S(1)} %collective-permute-done.refs_1_, bf16[32,5248]{1,0:T(8,128)(2,1)S(1)} %collective-permute-done.1.refs_2_, bf16[32,5248]{1,0:T(8,128)(2,1)S(1)} %copy-done.3, ...), custom_call_target="tpu_custom_call" | custom-call | flops 6794772480 | bytes 28999680 | tf_op jit(solution)/shard_map/pallas_call | solution.py:110
  138.3 3.6 %collective-permute-start.21 = (bf16[32,5120]{1,0:T(8,128)(2,1)S(1)}, bf16[32,5120]{1,0:T(8,128)(2,1)S(1)}, u32[]{:S(2)}, u32[]{:S(2)}) collective-permute-start(bf16[32,5120]{1,0:T(8,128)(2,1)S(1)} %get-tuple-element.52), channel_id=1, source_target_pairs={{0,224},{32,0},{64,32},{96,64},{128,96},{160,128},{192,160},{224,1... | collective-permute-start | bytes 983048 | tf_op jit(solution)/shard_map/ppermute | solution.py:27
  141.9 6.5 %collective-permute-done.14 = bf16[32,5120]{1,0:T(8,128)(2,1)S(1)} collective-permute-done((bf16[32,5120]{1,0:T(8,128)(2,1)S(1)}, bf16[32,5120]{1,0:T(8,128)(2,1)S(1)}, u32[]{:S(2)}, u32[]{:S(2)}) %collective-permute-start.14) | collective-permute-done | bytes 327712 | tf_op jit(solution)/shard_map/ppermute | solution.py:27
  153.6 3.4 %collective-permute-done.15 = bf16[32,5120]{1,0:T(8,128)(2,1)S(1)} collective-permute-done((bf16[32,5120]{1,0:T(8,128)(2,1)S(1)}, bf16[32,5120]{1,0:T(8,128)(2,1)S(1)}, u32[]{:S(2)}, u32[]{:S(2)}) %collective-permute-start.15) | collective-permute-done | bytes 327712 | tf_op jit(solution)/shard_map/ppermute | solution.py:27
  160.4 3.6 %collective-permute-done.22 = bf16[32,5120]{1,0:T(8,128)(2,1)S(1)} collective-permute-done((bf16[32,5120]{1,0:T(8,128)(2,1)S(1)}, bf16[32,5120]{1,0:T(8,128)(2,1)S(1)}, u32[]{:S(2)}, u32[]{:S(2)}) %collective-permute-start.22) | collective-permute-done | bytes 327712 | tf_op jit(solution)/shard_map/ppermute | solution.py:27
  167.4 3.6 %collective-permute-done.17 = bf16[32,5120]{1,0:T(8,128)(2,1)S(1)} collective-permute-done((bf16[32,5120]{1,0:T(8,128)(2,1)S(1)}, bf16[32,5120]{1,0:T(8,128)(2,1)S(1)}, u32[]{:S(2)}, u32[]{:S(2)}) %collective-permute-start.17) | collective-permute-done | bytes 327712 | tf_op jit(solution)/shard_map/ppermute | solution.py:27
  182.7 4.2 %collective-permute-done.19 = bf16[32,5120]{1,0:T(8,128)(2,1)S(1)} collective-permute-done((bf16[32,5120]{1,0:T(8,128)(2,1)S(1)}, bf16[32,5120]{1,0:T(8,128)(2,1)S(1)}, u32[]{:S(2)}, u32[]{:S(2)}) %collective-permute-start.19) | collective-permute-done | bytes 327712 | tf_op jit(solution)/shard_map/ppermute | solution.py:27
  186.9 6.9 %collective-permute-done.26 = bf16[32,5120]{1,0:T(8,128)(2,1)S(1)} collective-permute-done((bf16[32,5120]{1,0:T(8,128)(2,1)S(1)}, bf16[32,5120]{1,0:T(8,128)(2,1)S(1)}, u32[]{:S(2)}, u32[]{:S(2)}) %collective-permute-start.26) | collective-permute-done | bytes 327712 | tf_op jit(solution)/shard_map/ppermute | solution.py:27
  196.2 20.6 %all_to_all.20 = bf16[32,16,768]{2,1,0:T(8,128)(2,1)S(1)} all-to-all(bf16[32,16,768]{2,1,0:T(8,128)(2,1)S(1)} %pad_maximum_fusion.1), channel_id=1, replica_groups=mesh['z'=8,'y'=4,'x'=4,'core'=2] {'y','x','core'}, dimensions={0} | all-to-all | bytes 1572864 | tf_op jit(solution)/shard_map/all_to_all | solution.py:213
  217.8 5.0 %all-to-all-start.3 = ((f32[8,1,128]{2,1,0:T(1,128)}), f32[8,1,128]{2,1,0:T(1,128)S(1)}, u32[]{:S(2)}, u32[]{:S(2)}) async-start(f32[8,1,128]{2,1,0:T(1,128)} %broadcast_in_dim.34), calls=%async_computation.3 | async-start | bytes 8192 | tf_op jit(solution)/shard_map/all_to_all | solution.py:221
  223.7 5.6 %all-to-all-done.3 = f32[8,1,128]{2,1,0:T(1,128)S(1)} async-done(((f32[8,1,128]{2,1,0:T(1,128)}), f32[8,1,128]{2,1,0:T(1,128)S(1)}, u32[]{:S(2)}, u32[]{:S(2)}) %all-to-all-start.3) | async-done | bytes 4128 | tf_op jit(solution)/shard_map/all_to_all | solution.py:221
  (173 shorter events, 64.0 us)
Async XLA Ops:
  7.2 97.0 %all-gather.2.cloned.1.call-start = ((), (), s32[]{:S(2)}) async-start(), calls=%async_computation.4 | async-start | bytes 16220160 | tf_op jit(solution)/shard_map/all_gather | solution.py:170
  15.2 22.8 %all-to-all-start = ((bf16[32,16,768]{2,1,0:T(8,128)(2,1)}), bf16[32,16,768]{2,1,0:T(8,128)(2,1)S(1)}, u32[]{:S(2)}, u32[]{:S(2)}) async-start(bf16[32,16,768]{2,1,0:T(8,128)(2,1)} %bitcast.5), calls=%async_computation | async-start | bytes 1572864 | tf_op jit(solution)/shard_map/all_to_all | solution.py:171
  38.7 14.9 %collective-permute-start.3 = (bf16[32,5248]{1,0:T(8,128)(2,1)S(1)}, bf16[32,5248]{1,0:T(8,128)(2,1)S(1)}, u32[]{:S(2)}, u32[]{:S(2)}) collective-permute-start(bf16[32,5248]{1,0:T(8,128)(2,1)S(1)} %bitcast.50), channel_id=1, source_target_pairs={{0,32},{32,64},{64,96},{96,128},{128,160},{160,192},{192,224},{224... | collective-permute-start | bytes 1007624 | tf_op jit(solution)/shard_map/ppermute | solution.py:27
  40.4 13.3 %collective-permute-start = (bf16[32,5248]{1,0:T(8,128)(2,1)S(1)}, bf16[32,5248]{1,0:T(8,128)(2,1)S(1)}, u32[]{:S(2)}, u32[]{:S(2)}) collective-permute-start(bf16[32,5248]{1,0:T(8,128)(2,1)S(1)} %bitcast.51), channel_id=1, source_target_pairs={{0,224},{32,0},{64,32},{96,64},{128,96},{160,128},{192,160},{224,1... | collective-permute-start | bytes 1007624 | tf_op jit(solution)/shard_map/ppermute | solution.py:27
  46.4 14.0 %collective-permute-start.7 = (bf16[32,5248]{1,0:T(8,128)(2,1)S(1)}, bf16[32,5248]{1,0:T(8,128)(2,1)S(1)}, u32[]{:S(2)}, u32[]{:S(2)}) collective-permute-start(bf16[32,5248]{1,0:T(8,128)(2,1)S(1)} %bitcast.46), channel_id=1, source_target_pairs={{0,224},{32,0},{64,32},{96,64},{128,96},{160,128},{192,160},{224,1... | collective-permute-start | bytes 1007624 | tf_op jit(solution)/shard_map/ppermute | solution.py:27
  53.6 17.9 %collective-permute-start.11 = (bf16[32,5248]{1,0:T(8,128)(2,1)S(1)}, bf16[32,5248]{1,0:T(8,128)(2,1)S(1)}, u32[]{:S(2)}, u32[]{:S(2)}) collective-permute-start(bf16[32,5248]{1,0:T(8,128)(2,1)S(1)} %bitcast.47), channel_id=1, source_target_pairs={{0,32},{32,64},{64,96},{96,128},{128,160},{160,192},{192,224},{224... | collective-permute-start | bytes 1007624 | tf_op jit(solution)/shard_map/ppermute | solution.py:27
  53.7 17.9 %collective-permute-start.1 = (bf16[32,5248]{1,0:T(8,128)(2,1)S(1)}, bf16[32,5248]{1,0:T(8,128)(2,1)S(1)}, u32[]{:S(2)}, u32[]{:S(2)}) collective-permute-start(bf16[32,5248]{1,0:T(8,128)(2,1)S(1)} %collective-permute-done.refs_1_), channel_id=1, source_target_pairs={{0,224},{32,0},{64,32},{96,64},{128,96},{160,128},{192,160},{224,1... | collective-permute-start | bytes 1007624 | tf_op jit(solution)/shard_map/ppermute | solution.py:27
  60.4 14.4 %collective-permute-start.8 = (bf16[32,5248]{1,0:T(8,128)(2,1)S(1)}, bf16[32,5248]{1,0:T(8,128)(2,1)S(1)}, u32[]{:S(2)}, u32[]{:S(2)}) collective-permute-start(bf16[32,5248]{1,0:T(8,128)(2,1)S(1)} %collective-permute-done.7.refs_9_), channel_id=1, source_target_pairs={{0,224},{32,0},{64,32},{96,64},{128,96},{160,128},{192,160},{224,1... | collective-permute-start | bytes 1007624 | tf_op jit(solution)/shard_map/ppermute | solution.py:27
  64.0 14.4 %collective-permute-start.5 = (bf16[32,5248]{1,0:T(8,128)(2,1)S(1)}, bf16[32,5248]{1,0:T(8,128)(2,1)S(1)}, u32[]{:S(2)}, u32[]{:S(2)}) collective-permute-start(bf16[32,5248]{1,0:T(8,128)(2,1)S(1)} %collective-permute-done.4.refs_6_), channel_id=1, source_target_pairs={{0,32},{32,64},{64,96},{96,128},{128,160},{160,192},{192,224},{224... | collective-permute-start | bytes 1007624 | tf_op jit(solution)/shard_map/ppermute | solution.py:27
  65.0 129.5 %all-to-all-start.1 = ((bf16[32,16,640]{2,1,0:T(8,128)(2,1)}), bf16[32,16,640]{2,1,0:T(8,128)(2,1)}, u32[]{:S(2)}, u32[]{:S(2)}) async-start(bf16[32,16,640]{2,1,0:T(8,128)(2,1)} %bitcast.60), calls=%async_computation.1 | async-start | bytes 1310720 | tf_op jit(solution)/shard_map/all_to_all | solution.py:174
  71.6 13.5 %collective-permute-start.12 = (bf16[32,5248]{1,0:T(8,128)(2,1)S(1)}, bf16[32,5248]{1,0:T(8,128)(2,1)S(1)}, u32[]{:S(2)}, u32[]{:S(2)}) collective-permute-start(bf16[32,5248]{1,0:T(8,128)(2,1)S(1)} %collective-permute-done.11.refs_15_), channel_id=1, source_target_pairs={{0,32},{32,64},{64,96},{96,128},{128,160},{160,192},{192,224},{224... | collective-permute-start | bytes 1007624 | tf_op jit(solution)/shard_map/ppermute | solution.py:27
  71.7 20.0 %collective-permute-start.2 = (bf16[32,5248]{1,0:T(8,128)(2,1)S(1)}, bf16[32,5248]{1,0:T(8,128)(2,1)S(1)}, u32[]{:S(2)}, u32[]{:S(2)}) collective-permute-start(bf16[32,5248]{1,0:T(8,128)(2,1)S(1)} %collective-permute-done.1.refs_2_), channel_id=1, source_target_pairs={{0,224},{32,0},{64,32},{96,64},{128,96},{160,128},{192,160},{224,1... | collective-permute-start | bytes 1007624 | tf_op jit(solution)/shard_map/ppermute | solution.py:27
  74.8 13.3 %collective-permute-start.9 = (bf16[32,5248]{1,0:T(8,128)(2,1)S(1)}, bf16[32,5248]{1,0:T(8,128)(2,1)S(1)}, u32[]{:S(2)}, u32[]{:S(2)}) collective-permute-start(bf16[32,5248]{1,0:T(8,128)(2,1)S(1)} %collective-permute-done.8.refs_10_), channel_id=1, source_target_pairs={{0,224},{32,0},{64,32},{96,64},{128,96},{160,128},{192,160},{224,1... | collective-permute-start | bytes 1007624 | tf_op jit(solution)/shard_map/ppermute | solution.py:27
  78.4 14.1 %collective-permute-start.6 = (bf16[32,5248]{1,0:T(8,128)(2,1)S(1)}, bf16[32,5248]{1,0:T(8,128)(2,1)S(1)}, u32[]{:S(2)}, u32[]{:S(2)}) collective-permute-start(bf16[32,5248]{1,0:T(8,128)(2,1)S(1)} %collective-permute-done.5.refs_5_), channel_id=1, source_target_pairs={{0,32},{32,64},{64,96},{96,128},{128,160},{160,192},{192,224},{224... | collective-permute-start | bytes 1007624 | tf_op jit(solution)/shard_map/ppermute | solution.py:27
  85.0 14.4 %collective-permute-start.13 = (bf16[32,5248]{1,0:T(8,128)(2,1)S(1)}, bf16[32,5248]{1,0:T(8,128)(2,1)S(1)}, u32[]{:S(2)}, u32[]{:S(2)}) collective-permute-start(bf16[32,5248]{1,0:T(8,128)(2,1)S(1)} %collective-permute-done.12.refs_14_), channel_id=1, source_target_pairs={{0,32},{32,64},{64,96},{96,128},{128,160},{160,192},{192,224},{224... | collective-permute-start | bytes 1007624 | tf_op jit(solution)/shard_map/ppermute | solution.py:27
  135.7 12.7 %collective-permute-start.14 = (bf16[32,5120]{1,0:T(8,128)(2,1)S(1)}, bf16[32,5120]{1,0:T(8,128)(2,1)S(1)}, u32[]{:S(2)}, u32[]{:S(2)}) collective-permute-start(bf16[32,5120]{1,0:T(8,128)(2,1)S(1)} %get-tuple-element.45), channel_id=1, source_target_pairs={{0,32},{32,64},{64,96},{96,128},{128,160},{160,192},{192,224},{224... | collective-permute-start | bytes 983048 | tf_op jit(solution)/shard_map/ppermute | solution.py:27
  151.2 12.9 %collective-permute-start.22 = (bf16[32,5120]{1,0:T(8,128)(2,1)S(1)}, bf16[32,5120]{1,0:T(8,128)(2,1)S(1)}, u32[]{:S(2)}, u32[]{:S(2)}) collective-permute-start(bf16[32,5120]{1,0:T(8,128)(2,1)S(1)} %add_convert_fusion.4), channel_id=1, source_target_pairs={{0,224},{32,0},{64,32},{96,64},{128,96},{160,128},{192,160},{224,1... | collective-permute-start | bytes 983048 | tf_op jit(solution)/shard_map/ppermute | solution.py:27
  158.9 12.2 %collective-permute-start.17 = (bf16[32,5120]{1,0:T(8,128)(2,1)S(1)}, bf16[32,5120]{1,0:T(8,128)(2,1)S(1)}, u32[]{:S(2)}, u32[]{:S(2)}) collective-permute-start(bf16[32,5120]{1,0:T(8,128)(2,1)S(1)} %get-tuple-element.27), channel_id=1, source_target_pairs={{0,224},{32,0},{64,32},{96,64},{128,96},{160,128},{192,160},{224,1... | collective-permute-start | bytes 983048 | tf_op jit(solution)/shard_map/ppermute | solution.py:27
  159.2 13.6 %collective-permute-start.18 = (bf16[32,5120]{1,0:T(8,128)(2,1)S(1)}, bf16[32,5120]{1,0:T(8,128)(2,1)S(1)}, u32[]{:S(2)}, u32[]{:S(2)}) collective-permute-start(bf16[32,5120]{1,0:T(8,128)(2,1)S(1)} %get-tuple-element.28), channel_id=1, source_target_pairs={{0,32},{32,64},{64,96},{96,128},{128,160},{160,192},{192,224},{224... | collective-permute-start | bytes 983048 | tf_op jit(solution)/shard_map/ppermute | solution.py:27
  166.2 13.6 %collective-permute-start.25 = (bf16[32,5120]{1,0:T(8,128)(2,1)S(1)}, bf16[32,5120]{1,0:T(8,128)(2,1)S(1)}, u32[]{:S(2)}, u32[]{:S(2)}) collective-permute-start(bf16[32,5120]{1,0:T(8,128)(2,1)S(1)} %get-tuple-element.35), channel_id=1, source_target_pairs={{0,32},{32,64},{64,96},{96,128},{128,160},{160,192},{192,224},{224... | collective-permute-start | bytes 983048 | tf_op jit(solution)/shard_map/ppermute | solution.py:27
  172.9 13.9 %collective-permute-start.19 = (bf16[32,5120]{1,0:T(8,128)(2,1)S(1)}, bf16[32,5120]{1,0:T(8,128)(2,1)S(1)}, u32[]{:S(2)}, u32[]{:S(2)}) collective-permute-start(bf16[32,5120]{1,0:T(8,128)(2,1)S(1)} %get-tuple-element.29), channel_id=1, source_target_pairs={{0,32},{32,64},{64,96},{96,128},{128,160},{160,192},{192,224},{224... | collective-permute-start | bytes 983048 | tf_op jit(solution)/shard_map/ppermute | solution.py:27
  173.0 13.8 %collective-permute-start.20 = (bf16[32,5120]{1,0:T(8,128)(2,1)S(1)}, bf16[32,5120]{1,0:T(8,128)(2,1)S(1)}, u32[]{:S(2)}, u32[]{:S(2)}) collective-permute-start(bf16[32,5120]{1,0:T(8,128)(2,1)S(1)} %get-tuple-element.30), channel_id=1, source_target_pairs={{0,224},{32,0},{64,32},{96,64},{128,96},{160,128},{192,160},{224,1... | collective-permute-start | bytes 983048 | tf_op jit(solution)/shard_map/ppermute | solution.py:27
  179.9 13.9 %collective-permute-start.26 = (bf16[32,5120]{1,0:T(8,128)(2,1)S(1)}, bf16[32,5120]{1,0:T(8,128)(2,1)S(1)}, u32[]{:S(2)}, u32[]{:S(2)}) collective-permute-start(bf16[32,5120]{1,0:T(8,128)(2,1)S(1)} %get-tuple-element.36), channel_id=1, source_target_pairs={{0,32},{32,64},{64,96},{96,128},{128,160},{160,192},{192,224},{224... | collective-permute-start | bytes 983048 | tf_op jit(solution)/shard_map/ppermute | solution.py:27
  180.0 13.8 %collective-permute-start.27 = (bf16[32,5120]{1,0:T(8,128)(2,1)S(1)}, bf16[32,5120]{1,0:T(8,128)(2,1)S(1)}, u32[]{:S(2)}, u32[]{:S(2)}) collective-permute-start(bf16[32,5120]{1,0:T(8,128)(2,1)S(1)} %get-tuple-element.37), channel_id=1, source_target_pairs={{0,224},{32,0},{64,32},{96,64},{128,96},{160,128},{192,160},{224,1... | collective-permute-start | bytes 983048 | tf_op jit(solution)/shard_map/ppermute | solution.py:27
  (30 other events, 179.4 us)
Sparse Core Ops, SparseCore 0:
  15.3 88.8 all-gather.1

commit v4 on v3

--- a/solution.py
+++ b/solution.py
@@ -3,8 +3,6 @@
 import jax
 import jax.numpy as jnp
 from jax import lax
-from jax.experimental import pallas as pl
-from jax.experimental.pallas import tpu as pltpu
 from jax.sharding import Mesh
 from jax.sharding import PartitionSpec as P
 
@@ -29,17 +27,21 @@
 
 def ring_gather(chunks):
     half = Z // 2
-    blocks = [[chunk] + [None] * (Z - 1) for chunk in chunks]
+    rows, width = chunks[0].shape
+    total = jnp.zeros((len(chunks) * Z * rows, width), chunks[0].dtype)
     ends = [[chunk, chunk] for chunk in chunks]
+    landed = [(k, 0, chunk) for k, chunk in enumerate(chunks)]
     for step in range(1, half + 1):
         for k, end in enumerate(ends):
             if step < half or k % 2 == 0:
                 end[0] = shift(end[0], 1)
-                blocks[k][Z - step] = end[0]
+                landed.append((k, Z - step, end[0]))
             if step < half or k % 2 == 1:
                 end[1] = shift(end[1], -1)
-                blocks[k][step] = end[1]
-    return blocks
+                landed.append((k, step, end[1]))
+    for k, place, block in landed:
+        total = lax.dynamic_update_slice(total, block, ((k * Z + place) * rows, 0))
+    return total
 
 
 def ring_scatter(chunks):
@@ -62,75 +64,6 @@
             sends = lax.optimization_barrier(sends)
             ends[k] = {sign: shift(value, sign).astype(F32) for sign, value in sends.items()}
     return [chunk[:rows] + end[1] + end[-1] for chunk, end in zip(chunks, ends)]
-
-
-def layer_kernel(count, steps, units, *refs):
-    blocks, (w_ref, corr_ref, *outs, acc, down, hidden) = refs[:count], refs[count:]
-    step = pl.program_id(0)
-    skip = units // LANES * LANES
-
-    @pl.when(step < steps)
-    def _():
-        down[step] = w_ref[:, :units]
-        rows = jnp.concatenate([block[...] for block in blocks], axis=0)
-        part = jnp.dot(rows, w_ref[:, skip:], preferred_element_type=F32)
-
-        @pl.when(step == 0)
-        def _():
-            acc[...] = part
-
-        @pl.when(step > 0)
-        def _():
-            acc[...] += part
-
-    @pl.when(step == steps - 1)
-    def _():
-        both = acc[...]
-        gate = both[:, units - skip : 2 * units - skip]
-        up = both[:, 2 * units - skip :] + SIGMA * corr_ref[...]
-        hidden[...] = (gate / (1.0 + jnp.exp(-gate)) * up).astype(BF16)
-
-    @pl.when(step >= steps)
-    def _():
-        out = lax.dot_general(
-            hidden[...], down[step - steps], (((1,), (1,)), ((), ())), preferred_element_type=F32
-        )
-        rows = out.shape[0] // len(outs)
-        for k, ref in enumerate(outs):
-            ref[...] = out[k * rows : (k + 1) * rows]
-
-
-def layer(blocks, weights, corr, steps):
-    count = len(blocks)
-    rows, units = corr.shape
-    model, wide = weights.shape
-    feat = model // steps
-    small = blocks[0].shape[0]
-    skip = units // LANES * LANES
-    return pl.pallas_call(
-        lambda *refs: layer_kernel(count, steps, units, *refs),
-        grid=(2 * steps,),
-        in_specs=[pl.BlockSpec((small, feat), lambda i: (0, jnp.minimum(i, steps - 1)))] * count
-        + [
-            pl.BlockSpec((feat, wide), lambda i: (jnp.minimum(i, steps - 1), 0)),
-            pl.BlockSpec((rows, units), lambda i: (0, 0)),
-        ],
-        out_specs=[pl.BlockSpec((rows // 2, feat), lambda i: (0, jnp.maximum(i - steps, 0)))] * 2,
-        out_shape=[jax.ShapeDtypeStruct((rows // 2, model), F32)] * 2,
-        scratch_shapes=[
-            pltpu.VMEM((rows, wide - skip), F32),
-            pltpu.VMEM((steps, feat, units), BF16),
-            pltpu.VMEM((rows, units), BF16),
-        ],
-        compiler_params=pltpu.CompilerParams(
-            dimension_semantics=("arbitrary",), vmem_limit_bytes=40 * 1024 * 1024
-        ),
-        cost_estimate=pl.CostEstimate(
-            flops=2 * rows * model * wide,
-            bytes_accessed=2 * model * (wide + rows) + 4 * rows * model,
-            transcendentals=rows * units,
-        ),
-    )(*blocks, weights, corr)
 
 
 def split_two(value):
@@ -169,10 +102,6 @@
     packed, wide = lax.optimization_barrier((packed, wide))
     weights = lax.all_gather(packed, COL, axis=0, tiled=True)
     moved = lax.all_to_all(wide.reshape(Y * cols, own, dev_feat + LANES), PLANE, 0, 0, tiled=True)
-    target, moved = lax.optimization_barrier((target, moved))
-    goal = jnp.broadcast_to(target.reshape(1, cols, own, dev_feat), (Y, cols, own, dev_feat))
-    goal = lax.all_to_all(goal.reshape(Y * cols, own, dev_feat), PLANE, 0, 0, tiled=True)
-    goal = jnp.swapaxes(goal.reshape(Y, cols, own, dev_feat), 1, 2).reshape(Y, own, model)
     moved = moved.reshape(Y, cols, own, dev_feat + LANES)
     part = moved[..., dev_feat:].astype(F32)
     part = part[..., :RANK] + part[..., RANK : 2 * RANK]
@@ -183,8 +112,7 @@
     plane = Y * own
     mid = plane // 2
 
-    first, second = ring_gather([rows[:mid], rows[mid:]])
-    blocks = first + second
+    every = ring_gather([rows[:mid], rows[mid:]])
 
     row = lax.broadcasted_iota(jnp.int32, (Z * plane, members * RANK * 2), 0)
     column = lax.broadcasted_iota(jnp.int32, (Z * plane, members * RANK * 2), 1)
@@ -195,14 +123,29 @@
     spread_col = lax.broadcasted_iota(jnp.int32, (LANES, members * RANK * 2), 1)
     spread = spread_col // (members * RANK) * RANK + spread_col % RANK == spread_row
     low = jnp.dot(
-        jnp.concatenate([block[:, model:] for block in blocks], axis=0),
+        every[:, model:],
         spread.astype(BF16),
         preferred_element_type=F32,
     )
     low = jnp.where(column % (members * RANK) // RANK == member, low, 0.0).astype(BF16)
     corr = jnp.dot(low, v_twice, preferred_element_type=F32)
 
-    sums = ring_scatter(layer(blocks, weights, corr, cols))
+    skip = units // LANES * LANES
+    both = jnp.dot(every[:, :model], weights[:, skip:], preferred_element_type=F32)
+    gate = both[:, units - skip : 2 * units - skip]
+    up = both[:, 2 * units - skip :] + SIGMA * corr
+    hidden = (jax.nn.silu(gate) * up).astype(BF16)
+    hidden, target = lax.optimization_barrier((hidden, target))
+    goal = jnp.broadcast_to(target.reshape(1, cols, own, dev_feat), (Y, cols, own, dev_feat))
+    goal = lax.all_to_all(goal.reshape(Y * cols, own, dev_feat), PLANE, 0, 0, tiled=True)
+    goal = jnp.swapaxes(goal.reshape(Y, cols, own, dev_feat), 1, 2).reshape(Y, own, model)
+    outs = [
+        lax.dot_general(
+            part, weights[:, :units], (((1,), (1,)), ((), ())), preferred_element_type=F32
+        )
+        for part in (hidden[: Z * mid], hidden[Z * mid :])
+    ]
+    sums = ring_scatter(outs)
     total = jnp.concatenate(sums, axis=0).reshape(Y, own, model)
     score = jnp.sum(total * goal.astype(F32), axis=(1, 2)) / math.sqrt(SEQ * D)
     score = jnp.concatenate(split_three(score))

time: 239 us -> 225 us (0.941)
  Pallas kernels: 24.4 us -> 0 us
  matrix products: 5.81 us -> 21.8 us
  waiting for transfers between devices: 82.5 us -> 70.1 us
  other arithmetic: 5.95 us -> 12.4 us
  starting transfers between devices: 63 us -> 60.3 us
    pallas_call x1 -> x0, Pallas kernels: 24.4 us -> none  [layer(): pl.pallas_call(lambda *refs: layer_kernel(count, steps, units, *refs), gr...]
    dot_general x0 -> x3, matrix products: none -> 16.9 us  [the longest x1 9.16 us: body(): jnp.dot(every[:, :model], weights[:, skip:], preferred_element_type=F32)]
    dynamic_update_slice x0 -> x16, local copies, waits for them, and re-layouts: none -> 14 us  [ring_gather(): total = lax.dynamic_update_slice(total, block, ((k * Z + place) * rows, 0))]
    ppermute x28, waiting for transfers between devices: 62.4 us -> 50.4 us  [shift(): return lax.ppermute(value, 'z', [(i, (i + step) % Z) for i in range(Z)])]
    unnamed x68 -> x20, local copies, waits for them, and re-layouts: 14 us -> 5.15 us
    convert_element_type x6, other arithmetic: 1.65 us -> 5.46 us  [ring_scatter(): sends[sign] = block.astype(BF16)]
    concatenate x0 -> x1, other arithmetic: none -> 2.7 us  [body(): packed = jnp.concatenate([w_down.T, w_gate, w_up], axis=1)]
    concatenate x2 -> x0, local copies, waits for them, and re-layouts: 2.41 us -> none  [the longest x1 2.4 us: body(): packed = jnp.concatenate([w_down.T, w_gate, w_up], axis=1)]
  transfers between devices with their start and end apart: 32 -> 32, of which waited for: 21 -> 19; matrix products, arithmetic and copies ran while one was open for 4% -> 12% of each run, Pallas kernels for 10% -> 0%
where the time goes in v4:
time: 225 us; the launch traced here: 224 us
  waiting for transfers between devices  70.1 us (31%)
  starting transfers between devices  60.3 us (27%)
  local copies, waits for them, and re-layouts  22.9 us (10%)
  blocking collectives  22.4 us (10%)
  matrix products  21.8 us (10%)
  between operations  14.5 us (6%)
  other arithmetic  12.4 us (6%)
    ppermute x28, waiting for transfers between devices, shift(): return lax.ppermute(value, 'z', [(i, (i + step) % Z) for i in range(Z)])  50.4 us
    ppermute x28, starting transfers between devices, shift(): return lax.ppermute(value, 'z', [(i, (i + step) % Z) for i in range(Z)])  40.6 us
    all_to_all x1, blocking collectives, body(): back = lax.all_to_all(back, PLANE, 0, 0, tiled=True)  22.4 us
    all_to_all x1, waiting for transfers between devices, body(): lax.all_to_all(wide.reshape(Y * cols, own, dev_feat + LANES), PLANE, 0, 0...  14.1 us
    dynamic_update_slice x16, local copies, waits for them, and re-layouts, ring_gather(): total = lax.dynamic_update_slice(total, block, ((k * Z + place) * rows, 0))  14 us
    dot_general x1, matrix products, body(): jnp.dot(every[:, :model], weights[:, skip:], preferred_element_type=F32)  9.16 us
    all_to_all x1, starting transfers between devices, body(): lax.all_to_all(wide.reshape(Y * cols, own, dev_feat + LANES), PLANE, 0, 0...  8.6 us
    dot_general x2, matrix products, body(): lax.dot_general(part, weights[:, :units], (((1,), (1,)), ((), ())), prefe...  7.75 us
  transfers between devices with their start and end apart: 32, of which 19 were waited for; matrix products, arithmetic and copies ran while one was open for 12% of the time, Pallas kernels for 0%

profile of v4, /device:TPU:1, one launch (start us, length us, event | category | flops | bytes accessed | tf_op | source)
XLA Modules:
  0.0 224.4 jit_solution(8570849304996577203)
XLA Ops:
  9.9 2.7 %pad_maximum_fusion = bf16[640,1296]{0,1:T(8,128)(2,1)} fusion(bf16[640,432]{0,1:T(8,128)(2,1)} %param.10, bf16[640,432]{0,1:T(8,128)(2,1)} %param.9, bf16[640,432]{0,1:T(8,128)(2,1)} %bitcast.61), kind=kLoop, calls=%fused_computation.15 | loop fusion | flops 4976640 | bytes 3317760 | tf_op jit(solution)/shard_map/concatenate | solution.py:90
  13.6 8.6 %all-to-all-start = ((bf16[32,16,768]{2,1,0:T(8,128)(2,1)}), bf16[32,16,768]{2,1,0:T(8,128)(2,1)S(1)}, u32[]{:S(2)}, u32[]{:S(2)}) async-start(bf16[32,16,768]{2,1,0:T(8,128)(2,1)} %bitcast.5), calls=%async_computation | async-start | bytes 1572864 | tf_op jit(solution)/shard_map/all_to_all | solution.py:104
  22.3 14.1 %all-to-all-done = bf16[32,16,768]{2,1,0:T(8,128)(2,1)S(1)} async-done(((bf16[32,16,768]{2,1,0:T(8,128)(2,1)}), bf16[32,16,768]{2,1,0:T(8,128)(2,1)S(1)}, u32[]{:S(2)}, u32[]{:S(2)}) %all-to-all-start) | async-done | bytes 786464 | tf_op jit(solution)/shard_map/all_to_all | solution.py:104
  38.7 5.4 %collective-permute-start.1 = (bf16[32,5248]{1,0:T(8,128)(2,1)S(1)}, bf16[32,5248]{1,0:T(8,128)(2,1)S(1)}, u32[]{:S(2)}, u32[]{:S(2)}) collective-permute-start(bf16[32,5248]{1,0:T(8,128)(2,1)S(1)} %bitcast.55), channel_id=1, source_target_pairs={{0,224},{32,0},{64,32},{96,64},{128,96},{160,128},{192,160},{224,1... | collective-permute-start | bytes 1007624 | tf_op jit(solution)/shard_map/ppermute | solution.py:25
  44.2 2.7 %collective-permute-start.3 = (bf16[32,5248]{1,0:T(8,128)(2,1)S(1)}, bf16[32,5248]{1,0:T(8,128)(2,1)S(1)}, u32[]{:S(2)}, u32[]{:S(2)}) collective-permute-start(bf16[32,5248]{1,0:T(8,128)(2,1)S(1)} %bitcast.58), channel_id=1, source_target_pairs={{0,224},{32,0},{64,32},{96,64},{128,96},{160,128},{192,160},{224,1... | collective-permute-start | bytes 1007624 | tf_op jit(solution)/shard_map/ppermute | solution.py:25
  46.8 2.7 %dynamic_update_slice.48 = bf16[512,5248]{1,0:T(8,128)(2,1)} pad(bf16[32,5248]{1,0:T(8,128)(2,1)S(1)} %bitcast.56, bf16[]{:T(256)} %constant.158.clone.1), padding=0_480x0_0 | pad | bytes 5709826 | tf_op jit(solution)/shard_map/dynamic_update_slice | solution.py:43
  54.7 4.5 %collective-permute-done.2 = bf16[32,5248]{1,0:T(8,128)(2,1)S(1)} collective-permute-done((bf16[32,5248]{1,0:T(8,128)(2,1)S(1)}, bf16[32,5248]{1,0:T(8,128)(2,1)S(1)}, u32[]{:S(2)}, u32[]{:S(2)}) %collective-permute-start.2) | collective-permute-done | bytes 335904 | tf_op jit(solution)/shard_map/ppermute | solution.py:25
  69.1 4.5 %collective-permute-done.6 = bf16[32,5248]{1,0:T(8,128)(2,1)S(1)} collective-permute-done((bf16[32,5248]{1,0:T(8,128)(2,1)S(1)}, bf16[32,5248]{1,0:T(8,128)(2,1)S(1)}, u32[]{:S(2)}, u32[]{:S(2)}) %collective-permute-start.6) | collective-permute-done | bytes 335904 | tf_op jit(solution)/shard_map/ppermute | solution.py:25
  81.6 5.4 %collective-permute-done.11 = bf16[32,5248]{1,0:T(8,128)(2,1)S(1)} collective-permute-done((bf16[32,5248]{1,0:T(8,128)(2,1)S(1)}, bf16[32,5248]{1,0:T(8,128)(2,1)S(1)}, u32[]{:S(2)}, u32[]{:S(2)}) %collective-permute-start.11) | collective-permute-done | bytes 335904 | tf_op jit(solution)/shard_map/ppermute | solution.py:25
  86.9 3.5 %collective-permute-start.13 = (bf16[32,5248]{1,0:T(8,128)(2,1)S(1)}, bf16[32,5248]{1,0:T(8,128)(2,1)S(1)}, u32[]{:S(2)}, u32[]{:S(2)}) collective-permute-start(bf16[32,5248]{1,0:T(8,128)(2,1)S(1)} %collective-permute-done.11), channel_id=1, source_target_pairs={{0,224},{32,0},{64,32},{96,64},{128,96},{160,128},{192,160},{224,1... | collective-permute-start | bytes 1007624 | tf_op jit(solution)/shard_map/ppermute | solution.py:25
  97.2 9.2 %fusion = f32[512,912]{0,1:T(8,128)S(1)} fusion(bf16[5120,1296]{0,1:T(8,128)(2,1)} %all-gather.2.cloned.1.call-done, bf16[512,5248]{1,0:T(8,128)(2,1)} %constant_dynamic-update-slice_fusion.2), kind=kOutput, calls=%fused_computation | convolution fusion | flops 4781506560 | bytes 16449536 | tf_op jit(solution)/shard_map/dot_general | solution.py:134
  108.4 3.9 %fusion.5 = f32[256,5120]{1,0:T(8,128)S(1)} fusion(bf16[5120,1296]{0,1:T(8,128)(2,1)} %all-gather.2.cloned.1.call-done, bf16[512,432]{0,1:T(8,128)(2,1)S(1)} %fusion.33), kind=kOutput, calls=%fused_computation.5 | convolution fusion | flops 1132462080 | bytes 9887744 | tf_op jit(solution)/shard_map/dot_general | solution.py:143
  114.6 3.9 %fusion.3 = f32[256,5120]{1,0:T(8,128)S(1)} fusion(bf16[5120,1296]{0,1:T(8,128)(2,1)} %all-gather.2.cloned.1.call-done, bf16[512,432]{0,1:T(8,128)(2,1)S(1)} %fusion.33), kind=kOutput, calls=%fused_computation.3 | convolution fusion | flops 1132462080 | bytes 9887744 | tf_op jit(solution)/shard_map/dot_general | solution.py:143
  120.9 3.5 %collective-permute-start.21 = (bf16[32,5120]{1,0:T(8,128)(2,1)S(1)}, bf16[32,5120]{1,0:T(8,128)(2,1)S(1)}, u32[]{:S(2)}, u32[]{:S(2)}) collective-permute-start(bf16[32,5120]{1,0:T(8,128)(2,1)S(1)} %get-tuple-element.48), channel_id=1, source_target_pairs={{0,224},{32,0},{64,32},{96,64},{128,96},{160,128},{192,160},{224,1... | collective-permute-start | bytes 983048 | tf_op jit(solution)/shard_map/ppermute | solution.py:25
  125.3 7.0 %all-to-all-start.1 = ((bf16[32,16,640]{2,1,0:T(8,128)(2,1)}), bf16[32,16,640]{2,1,0:T(8,128)(2,1)S(1)}, u32[]{:S(2)}, u32[]{:S(2)}) async-start(bf16[32,16,640]{2,1,0:T(8,128)(2,1)} %bitcast.13), calls=%async_computation.1 | async-start | bytes 1310720 | tf_op jit(solution)/shard_map/all_to_all | solution.py:140
  136.5 2.7 %collective-permute-start.22 = (bf16[32,5120]{1,0:T(8,128)(2,1)S(1)}, bf16[32,5120]{1,0:T(8,128)(2,1)S(1)}, u32[]{:S(2)}, u32[]{:S(2)}) collective-permute-start(bf16[32,5120]{1,0:T(8,128)(2,1)S(1)} %fusion.37), channel_id=1, source_target_pairs={{0,224},{32,0},{64,32},{96,64},{128,96},{160,128},{192,160},{224,1... | collective-permute-start | bytes 983048 | tf_op jit(solution)/shard_map/ppermute | solution.py:25
  139.2 3.5 %collective-permute-done.15 = bf16[32,5120]{1,0:T(8,128)(2,1)S(1)} collective-permute-done((bf16[32,5120]{1,0:T(8,128)(2,1)S(1)}, bf16[32,5120]{1,0:T(8,128)(2,1)S(1)}, u32[]{:S(2)}, u32[]{:S(2)}) %collective-permute-start.15) | collective-permute-done | bytes 327712 | tf_op jit(solution)/shard_map/ppermute | solution.py:25
  156.2 3.1 %collective-permute-done.18 = bf16[32,5120]{1,0:T(8,128)(2,1)S(1)} collective-permute-done((bf16[32,5120]{1,0:T(8,128)(2,1)S(1)}, bf16[32,5120]{1,0:T(8,128)(2,1)S(1)}, u32[]{:S(2)}, u32[]{:S(2)}) %collective-permute-start.18) | collective-permute-done | bytes 327712 | tf_op jit(solution)/shard_map/ppermute | solution.py:25
  163.5 2.9 %collective-permute-done.25 = bf16[32,5120]{1,0:T(8,128)(2,1)S(1)} collective-permute-done((bf16[32,5120]{1,0:T(8,128)(2,1)S(1)}, bf16[32,5120]{1,0:T(8,128)(2,1)S(1)}, u32[]{:S(2)}, u32[]{:S(2)}) %collective-permute-start.25) | collective-permute-done | bytes 327712 | tf_op jit(solution)/shard_map/ppermute | solution.py:25
  169.2 4.2 %collective-permute-done.19 = bf16[32,5120]{1,0:T(8,128)(2,1)S(1)} collective-permute-done((bf16[32,5120]{1,0:T(8,128)(2,1)S(1)}, bf16[32,5120]{1,0:T(8,128)(2,1)S(1)}, u32[]{:S(2)}, u32[]{:S(2)}) %collective-permute-start.19) | collective-permute-done | bytes 327712 | tf_op jit(solution)/shard_map/ppermute | solution.py:25
  174.6 5.8 %collective-permute-done.26 = bf16[32,5120]{1,0:T(8,128)(2,1)S(1)} collective-permute-done((bf16[32,5120]{1,0:T(8,128)(2,1)S(1)}, bf16[32,5120]{1,0:T(8,128)(2,1)S(1)}, u32[]{:S(2)}, u32[]{:S(2)}) %collective-permute-start.26) | collective-permute-done | bytes 327712 | tf_op jit(solution)/shard_map/ppermute | solution.py:25
  181.6 22.4 %all_to_all.20 = bf16[32,16,768]{2,1,0:T(8,128)(2,1)S(1)} all-to-all(bf16[32,16,768]{2,1,0:T(8,128)(2,1)S(1)} %pad_maximum_fusion.2), channel_id=1, replica_groups=mesh['z'=8,'y'=4,'x'=4,'core'=2] {'y','x','core'}, dimensions={0} | all-to-all | bytes 1572864 | tf_op jit(solution)/shard_map/all_to_all | solution.py:156
  205.1 4.1 %all-to-all-start.3 = ((f32[8,1,128]{2,1,0:T(1,128)}), f32[8,1,128]{2,1,0:T(1,128)S(1)}, u32[]{:S(2)}, u32[]{:S(2)}) async-start(f32[8,1,128]{2,1,0:T(1,128)} %broadcast_in_dim.35), calls=%async_computation.3 | async-start | bytes 8192 | tf_op jit(solution)/shard_map/all_to_all | solution.py:164
  210.0 5.6 %all-to-all-done.3 = f32[8,1,128]{2,1,0:T(1,128)S(1)} async-done(((f32[8,1,128]{2,1,0:T(1,128)}), f32[8,1,128]{2,1,0:T(1,128)S(1)}, u32[]{:S(2)}, u32[]{:S(2)}) %all-to-all-start.3) | async-done | bytes 4128 | tf_op jit(solution)/shard_map/all_to_all | solution.py:164
  (142 shorter events, 74.3 us)
Async XLA Ops:
  7.2 90.0 %all-gather.2.cloned.1.call-start = ((), (), s32[]{:S(2)}) async-start(), calls=%async_computation.4 | async-start | bytes 14929920 | tf_op jit(solution)/shard_map/all_gather | solution.py:103
  13.6 22.8 %all-to-all-start = ((bf16[32,16,768]{2,1,0:T(8,128)(2,1)}), bf16[32,16,768]{2,1,0:T(8,128)(2,1)S(1)}, u32[]{:S(2)}, u32[]{:S(2)}) async-start(bf16[32,16,768]{2,1,0:T(8,128)(2,1)} %bitcast.5), calls=%async_computation | async-start | bytes 1572864 | tf_op jit(solution)/shard_map/all_to_all | solution.py:104
  37.0 15.0 %collective-permute-start = (bf16[32,5248]{1,0:T(8,128)(2,1)S(1)}, bf16[32,5248]{1,0:T(8,128)(2,1)S(1)}, u32[]{:S(2)}, u32[]{:S(2)}) collective-permute-start(bf16[32,5248]{1,0:T(8,128)(2,1)S(1)} %bitcast.54), channel_id=1, source_target_pairs={{0,32},{32,64},{64,96},{96,128},{128,160},{160,192},{192,224},{224... | collective-permute-start | bytes 1007624 | tf_op jit(solution)/shard_map/ppermute | solution.py:25
  38.7 13.3 %collective-permute-start.1 = (bf16[32,5248]{1,0:T(8,128)(2,1)S(1)}, bf16[32,5248]{1,0:T(8,128)(2,1)S(1)}, u32[]{:S(2)}, u32[]{:S(2)}) collective-permute-start(bf16[32,5248]{1,0:T(8,128)(2,1)S(1)} %bitcast.55), channel_id=1, source_target_pairs={{0,224},{32,0},{64,32},{96,64},{128,96},{160,128},{192,160},{224,1... | collective-permute-start | bytes 1007624 | tf_op jit(solution)/shard_map/ppermute | solution.py:25
  44.2 15.1 %collective-permute-start.2 = (bf16[32,5248]{1,0:T(8,128)(2,1)S(1)}, bf16[32,5248]{1,0:T(8,128)(2,1)S(1)}, u32[]{:S(2)}, u32[]{:S(2)}) collective-permute-start(bf16[32,5248]{1,0:T(8,128)(2,1)S(1)} %bitcast.57), channel_id=1, source_target_pairs={{0,32},{32,64},{64,96},{96,128},{128,160},{160,192},{192,224},{224... | collective-permute-start | bytes 1007624 | tf_op jit(solution)/shard_map/ppermute | solution.py:25
  44.2 15.1 %collective-permute-start.3 = (bf16[32,5248]{1,0:T(8,128)(2,1)S(1)}, bf16[32,5248]{1,0:T(8,128)(2,1)S(1)}, u32[]{:S(2)}, u32[]{:S(2)}) collective-permute-start(bf16[32,5248]{1,0:T(8,128)(2,1)S(1)} %bitcast.58), channel_id=1, source_target_pairs={{0,224},{32,0},{64,32},{96,64},{128,96},{160,128},{192,160},{224,1... | collective-permute-start | bytes 1007624 | tf_op jit(solution)/shard_map/ppermute | solution.py:25
  52.0 14.4 %collective-permute-start.4 = (bf16[32,5248]{1,0:T(8,128)(2,1)S(1)}, bf16[32,5248]{1,0:T(8,128)(2,1)S(1)}, u32[]{:S(2)}, u32[]{:S(2)}) collective-permute-start(bf16[32,5248]{1,0:T(8,128)(2,1)S(1)} %collective-permute-done), channel_id=1, source_target_pairs={{0,32},{32,64},{64,96},{96,128},{128,160},{160,192},{192,224},{224... | collective-permute-start | bytes 1007624 | tf_op jit(solution)/shard_map/ppermute | solution.py:25
  52.0 14.4 %collective-permute-start.5 = (bf16[32,5248]{1,0:T(8,128)(2,1)S(1)}, bf16[32,5248]{1,0:T(8,128)(2,1)S(1)}, u32[]{:S(2)}, u32[]{:S(2)}) collective-permute-start(bf16[32,5248]{1,0:T(8,128)(2,1)S(1)} %collective-permute-done.1), channel_id=1, source_target_pairs={{0,224},{32,0},{64,32},{96,64},{128,96},{160,128},{192,160},{224,1... | collective-permute-start | bytes 1007624 | tf_op jit(solution)/shard_map/ppermute | solution.py:25
  59.2 14.4 %collective-permute-start.6 = (bf16[32,5248]{1,0:T(8,128)(2,1)S(1)}, bf16[32,5248]{1,0:T(8,128)(2,1)S(1)}, u32[]{:S(2)}, u32[]{:S(2)}) collective-permute-start(bf16[32,5248]{1,0:T(8,128)(2,1)S(1)} %collective-permute-done.2), channel_id=1, source_target_pairs={{0,32},{32,64},{64,96},{96,128},{128,160},{160,192},{192,224},{224... | collective-permute-start | bytes 1007624 | tf_op jit(solution)/shard_map/ppermute | solution.py:25
  59.2 14.4 %collective-permute-start.7 = (bf16[32,5248]{1,0:T(8,128)(2,1)S(1)}, bf16[32,5248]{1,0:T(8,128)(2,1)S(1)}, u32[]{:S(2)}, u32[]{:S(2)}) collective-permute-start(bf16[32,5248]{1,0:T(8,128)(2,1)S(1)} %collective-permute-done.3), channel_id=1, source_target_pairs={{0,224},{32,0},{64,32},{96,64},{128,96},{160,128},{192,160},{224,1... | collective-permute-start | bytes 1007624 | tf_op jit(solution)/shard_map/ppermute | solution.py:25
  66.4 14.4 %collective-permute-start.8 = (bf16[32,5248]{1,0:T(8,128)(2,1)S(1)}, bf16[32,5248]{1,0:T(8,128)(2,1)S(1)}, u32[]{:S(2)}, u32[]{:S(2)}) collective-permute-start(bf16[32,5248]{1,0:T(8,128)(2,1)S(1)} %collective-permute-done.4), channel_id=1, source_target_pairs={{0,32},{32,64},{64,96},{96,128},{128,160},{160,192},{192,224},{224... | collective-permute-start | bytes 1007624 | tf_op jit(solution)/shard_map/ppermute | solution.py:25
  66.4 24.0 %collective-permute-start.9 = (bf16[32,5248]{1,0:T(8,128)(2,1)S(1)}, bf16[32,5248]{1,0:T(8,128)(2,1)S(1)}, u32[]{:S(2)}, u32[]{:S(2)}) collective-permute-start(bf16[32,5248]{1,0:T(8,128)(2,1)S(1)} %collective-permute-done.5), channel_id=1, source_target_pairs={{0,224},{32,0},{64,32},{96,64},{128,96},{160,128},{192,160},{224,1... | collective-permute-start | bytes 1007624 | tf_op jit(solution)/shard_map/ppermute | solution.py:25
  73.6 17.6 %collective-permute-start.10 = (bf16[32,5248]{1,0:T(8,128)(2,1)S(1)}, bf16[32,5248]{1,0:T(8,128)(2,1)S(1)}, u32[]{:S(2)}, u32[]{:S(2)}) collective-permute-start(bf16[32,5248]{1,0:T(8,128)(2,1)S(1)} %collective-permute-done.6), channel_id=1, source_target_pairs={{0,32},{32,64},{64,96},{96,128},{128,160},{160,192},{192,224},{224... | collective-permute-start | bytes 1007624 | tf_op jit(solution)/shard_map/ppermute | solution.py:25
  73.6 13.3 %collective-permute-start.11 = (bf16[32,5248]{1,0:T(8,128)(2,1)S(1)}, bf16[32,5248]{1,0:T(8,128)(2,1)S(1)}, u32[]{:S(2)}, u32[]{:S(2)}) collective-permute-start(bf16[32,5248]{1,0:T(8,128)(2,1)S(1)} %collective-permute-done.7), channel_id=1, source_target_pairs={{0,224},{32,0},{64,32},{96,64},{128,96},{160,128},{192,160},{224,1... | collective-permute-start | bytes 1007624 | tf_op jit(solution)/shard_map/ppermute | solution.py:25
  80.8 14.3 %collective-permute-start.12 = (bf16[32,5248]{1,0:T(8,128)(2,1)S(1)}, bf16[32,5248]{1,0:T(8,128)(2,1)S(1)}, u32[]{:S(2)}, u32[]{:S(2)}) collective-permute-start(bf16[32,5248]{1,0:T(8,128)(2,1)S(1)} %collective-permute-done.8), channel_id=1, source_target_pairs={{0,32},{32,64},{64,96},{96,128},{128,160},{160,192},{192,224},{224... | collective-permute-start | bytes 1007624 | tf_op jit(solution)/shard_map/ppermute | solution.py:25
  114.6 17.6 %collective-permute-start.14 = (bf16[32,5120]{1,0:T(8,128)(2,1)S(1)}, bf16[32,5120]{1,0:T(8,128)(2,1)S(1)}, u32[]{:S(2)}, u32[]{:S(2)}) collective-permute-start(bf16[32,5120]{1,0:T(8,128)(2,1)S(1)} %get-tuple-element.41), channel_id=1, source_target_pairs={{0,32},{32,64},{64,96},{96,128},{128,160},{160,192},{192,224},{224... | collective-permute-start | bytes 983048 | tf_op jit(solution)/shard_map/ppermute | solution.py:25
  120.9 14.5 %collective-permute-start.21 = (bf16[32,5120]{1,0:T(8,128)(2,1)S(1)}, bf16[32,5120]{1,0:T(8,128)(2,1)S(1)}, u32[]{:S(2)}, u32[]{:S(2)}) collective-permute-start(bf16[32,5120]{1,0:T(8,128)(2,1)S(1)} %get-tuple-element.48), channel_id=1, source_target_pairs={{0,224},{32,0},{64,32},{96,64},{128,96},{160,128},{192,160},{224,1... | collective-permute-start | bytes 983048 | tf_op jit(solution)/shard_map/ppermute | solution.py:25
  125.3 55.8 %all-to-all-start.1 = ((bf16[32,16,640]{2,1,0:T(8,128)(2,1)}), bf16[32,16,640]{2,1,0:T(8,128)(2,1)S(1)}, u32[]{:S(2)}, u32[]{:S(2)}) async-start(bf16[32,16,640]{2,1,0:T(8,128)(2,1)} %bitcast.13), calls=%async_computation.1 | async-start | bytes 1310720 | tf_op jit(solution)/shard_map/all_to_all | solution.py:140
  136.5 13.2 %collective-permute-start.22 = (bf16[32,5120]{1,0:T(8,128)(2,1)S(1)}, bf16[32,5120]{1,0:T(8,128)(2,1)S(1)}, u32[]{:S(2)}, u32[]{:S(2)}) collective-permute-start(bf16[32,5120]{1,0:T(8,128)(2,1)S(1)} %fusion.37), channel_id=1, source_target_pairs={{0,224},{32,0},{64,32},{96,64},{128,96},{160,128},{192,160},{224,1... | collective-permute-start | bytes 983048 | tf_op jit(solution)/shard_map/ppermute | solution.py:25
  139.2 13.1 %collective-permute-start.23 = (bf16[32,5120]{1,0:T(8,128)(2,1)S(1)}, bf16[32,5120]{1,0:T(8,128)(2,1)S(1)}, u32[]{:S(2)}, u32[]{:S(2)}) collective-permute-start(bf16[32,5120]{1,0:T(8,128)(2,1)S(1)} %get-tuple-element.29), channel_id=1, source_target_pairs={{0,32},{32,64},{64,96},{96,128},{128,160},{160,192},{192,224},{224... | collective-permute-start | bytes 983048 | tf_op jit(solution)/shard_map/ppermute | solution.py:25
  152.8 13.5 %collective-permute-start.25 = (bf16[32,5120]{1,0:T(8,128)(2,1)S(1)}, bf16[32,5120]{1,0:T(8,128)(2,1)S(1)}, u32[]{:S(2)}, u32[]{:S(2)}) collective-permute-start(bf16[32,5120]{1,0:T(8,128)(2,1)S(1)} %get-tuple-element.31), channel_id=1, source_target_pairs={{0,32},{32,64},{64,96},{96,128},{128,160},{160,192},{192,224},{224... | collective-permute-start | bytes 983048 | tf_op jit(solution)/shard_map/ppermute | solution.py:25
  160.7 12.6 %collective-permute-start.19 = (bf16[32,5120]{1,0:T(8,128)(2,1)S(1)}, bf16[32,5120]{1,0:T(8,128)(2,1)S(1)}, u32[]{:S(2)}, u32[]{:S(2)}) collective-permute-start(bf16[32,5120]{1,0:T(8,128)(2,1)S(1)} %get-tuple-element.26), channel_id=1, source_target_pairs={{0,32},{32,64},{64,96},{96,128},{128,160},{160,192},{192,224},{224... | collective-permute-start | bytes 983048 | tf_op jit(solution)/shard_map/ppermute | solution.py:25
  166.5 13.9 %collective-permute-start.26 = (bf16[32,5120]{1,0:T(8,128)(2,1)S(1)}, bf16[32,5120]{1,0:T(8,128)(2,1)S(1)}, u32[]{:S(2)}, u32[]{:S(2)}) collective-permute-start(bf16[32,5120]{1,0:T(8,128)(2,1)S(1)} %get-tuple-element.32), channel_id=1, source_target_pairs={{0,32},{32,64},{64,96},{96,128},{128,160},{160,192},{192,224},{224... | collective-permute-start | bytes 983048 | tf_op jit(solution)/shard_map/ppermute | solution.py:25
  166.6 13.8 %collective-permute-start.27 = (bf16[32,5120]{1,0:T(8,128)(2,1)S(1)}, bf16[32,5120]{1,0:T(8,128)(2,1)S(1)}, u32[]{:S(2)}, u32[]{:S(2)}) collective-permute-start(bf16[32,5120]{1,0:T(8,128)(2,1)S(1)} %get-tuple-element.33), channel_id=1, source_target_pairs={{0,224},{32,0},{64,32},{96,64},{128,96},{160,128},{192,160},{224,1... | collective-permute-start | bytes 983048 | tf_op jit(solution)/shard_map/ppermute | solution.py:25
  (15 other events, 171.3 us)
Sparse Core Ops, SparseCore 0:
  13.7 76.8 all-gather.1

commit v5 on v4

--- a/solution.py
+++ b/solution.py
@@ -16,13 +16,15 @@
 ROW = ("z", "y")
 COL = ("x", "core")
 PLANE = ("y", "x", "core")
+WALL = ("z", "x", "core")
 ALL = ("z", "y", "x", "core")
 F32 = jnp.float32
 BF16 = jnp.bfloat16
 
 
-def shift(value, step):
-    return lax.ppermute(value, "z", [(i, (i + step) % Z) for i in range(Z)])
+def shift(value, step, axis="z"):
+    n = {"z": Z, "y": Y}[axis]
+    return lax.ppermute(value, axis, [(i, (i + step) % n) for i in range(n)])
 
 
 def ring_gather(chunks):
@@ -44,26 +46,34 @@
     return total
 
 
-def ring_scatter(chunks):
-    half = Z // 2
-    rows = chunks[0].shape[0] // Z
-    ends = [{} for _ in chunks]
-    for step in range(half, 0, -1):
-        for k, chunk in enumerate(chunks):
-            sends = {}
-            for side, sign in ((0, 1), (1, -1)):
-                if step == half and side != k % 2:
-                    continue
-                place = (sign * step) % Z
-                block = chunk[place * rows : (place + 1) * rows]
-                if sign in ends[k]:
-                    block = block + ends[k][sign]
-                else:
-                    block = lax.optimization_barrier(block)
-                sends[sign] = block.astype(BF16)
-            sends = lax.optimization_barrier(sends)
-            ends[k] = {sign: shift(value, sign).astype(F32) for sign, value in sends.items()}
-    return [chunk[:rows] + end[1] + end[-1] for chunk, end in zip(chunks, ends)]
+def ring_scatter(value, axis, n):
+    half = n // 2
+    rows = value.shape[0] // n
+    mid = value.shape[1] // 2
+
+    def block(distance):
+        place = distance % n * rows
+        return value[place : place + rows]
+
+    sends = lax.optimization_barrier((block(half)[:, :mid], block(half)[:, mid:]))
+    sends = [send.astype(BF16) for send in sends]
+    ahead, behind = shift(sends[0], 1, axis), shift(sends[1], -1, axis)
+    for step in range(half - 1, 0, -1):
+        if step == half - 1:
+            ahead = jnp.pad(ahead.astype(F32), ((0, 0), (0, mid)))
+            behind = jnp.pad(behind.astype(F32), ((0, 0), (mid, 0)))
+        sends = (
+            (block(step) + ahead.astype(F32)).astype(BF16),
+            (block(-step) + behind.astype(F32)).astype(BF16),
+        )
+        sends = lax.optimization_barrier(sends)
+        ahead, behind = shift(sends[0], 1, axis), shift(sends[1], -1, axis)
+    return block(0) + ahead.astype(F32) + behind.astype(F32)
+
+
+def turn(value, start):
+    size = value.shape[0]
+    return lax.dynamic_slice_in_dim(jnp.concatenate([value, value], axis=0), start, size, axis=0)
 
 
 def split_two(value):
@@ -102,10 +112,16 @@
     packed, wide = lax.optimization_barrier((packed, wide))
     weights = lax.all_gather(packed, COL, axis=0, tiled=True)
     moved = lax.all_to_all(wide.reshape(Y * cols, own, dev_feat + LANES), PLANE, 0, 0, tiled=True)
+    target, moved = lax.optimization_barrier((target, moved))
+    part = own // 2
+    aims = target.reshape(cols, 2, part, dev_feat)
+    goal = jnp.broadcast_to(aims[:, 0], (Y, cols, part, dev_feat)).reshape(Y * cols, part, dev_feat)
+    goal = lax.all_to_all(goal, PLANE, 0, 0, tiled=True)
+    goal = jnp.swapaxes(goal.reshape(Y, cols, part, dev_feat), 1, 2).reshape(Y, part, model)
     moved = moved.reshape(Y, cols, own, dev_feat + LANES)
-    part = moved[..., dev_feat:].astype(F32)
-    part = part[..., :RANK] + part[..., RANK : 2 * RANK]
-    extra = jnp.concatenate(split_two(jnp.sum(part, axis=1)), axis=-1)
+    low = moved[..., dev_feat:].astype(F32)
+    low = low[..., :RANK] + low[..., RANK : 2 * RANK]
+    extra = jnp.concatenate(split_two(jnp.sum(low, axis=1)), axis=-1)
     extra = jnp.pad(extra, ((0, 0), (0, 0), (0, LANES - extra.shape[-1])))
     rows = jnp.swapaxes(moved[..., :dev_feat], 1, 2).reshape(Y, own, model)
     rows = jnp.concatenate([rows, extra], axis=2).reshape(Y * own, model + LANES)
@@ -135,31 +151,43 @@
     gate = both[:, units - skip : 2 * units - skip]
     up = both[:, 2 * units - skip :] + SIGMA * corr
     hidden = (jax.nn.silu(gate) * up).astype(BF16)
-    hidden, target = lax.optimization_barrier((hidden, target))
-    goal = jnp.broadcast_to(target.reshape(1, cols, own, dev_feat), (Y, cols, own, dev_feat))
-    goal = lax.all_to_all(goal.reshape(Y * cols, own, dev_feat), PLANE, 0, 0, tiled=True)
-    goal = jnp.swapaxes(goal.reshape(Y, cols, own, dev_feat), 1, 2).reshape(Y, own, model)
-    outs = [
-        lax.dot_general(
-            part, weights[:, :units], (((1,), (1,)), ((), ())), preferred_element_type=F32
-        )
-        for part in (hidden[: Z * mid], hidden[Z * mid :])
-    ]
-    sums = ring_scatter(outs)
-    total = jnp.concatenate(sums, axis=0).reshape(Y, own, model)
-    score = jnp.sum(total * goal.astype(F32), axis=(1, 2)) / math.sqrt(SEQ * D)
+    hidden, goal = lax.optimization_barrier((hidden, goal))
+
+    hidden = hidden.reshape(2, Z, Y // 2, 2, part, units)
+    first = jnp.transpose(hidden[:, :, :, 0], (1, 0, 2, 3, 4)).reshape(Z * Y * part, units)
+    second = jnp.transpose(hidden[:, :, :, 1], (1, 0, 2, 3, 4)).reshape(Z, Y, part, units)
+    second = jnp.swapaxes(turn(second, (Z - z) % Z), 0, 1)
+    second = turn(second, y).reshape(Y * Z * part, units)
+    down = weights[:, :units]
+
+    def project(rows_of):
+        return lax.dot_general(rows_of, down, (((1,), (1,)), ((), ())), preferred_element_type=F32)
+
+    def leave(total, devices):
+        out = total.astype(BF16).reshape(devices, part, cols, dev_feat)
+        return jnp.swapaxes(out, 1, 2).reshape(devices * cols, part, dev_feat)
+
+    second = ring_scatter(project(second), "y", Y)
+    second = lax.all_to_all(leave(second, Z), WALL, 0, 0, tiled=True)
+    second = jnp.sum(second.reshape(Z, cols, part, dev_feat).astype(F32), axis=0)
+    late = jnp.sum((second * aims[:, 1].astype(F32)).reshape(local, -1), axis=1)
+
+    first = ring_scatter(project(first), "z", Z)
+    early = jnp.sum(first.reshape(Y, part, model) * goal.astype(F32), axis=(1, 2))
+    score = jnp.concatenate([early, late]) / math.sqrt(SEQ * D)
+    count = Y + local
     score = jnp.concatenate(split_three(score))
-    score = jnp.broadcast_to(jnp.pad(score, (0, LANES - score.shape[0])), (Y * cols, own, LANES))
-
-    back = jnp.swapaxes(total.astype(BF16).reshape(Y, own, cols, dev_feat), 1, 2)
-    back = jnp.concatenate([back.reshape(Y * cols, own, dev_feat), score], axis=2)
+    score = jnp.broadcast_to(jnp.pad(score, (0, LANES - 3 * count)), (Y * cols, part, LANES))
+    back = jnp.concatenate([leave(first, Y), score], axis=2)
     back = lax.all_to_all(back, PLANE, 0, 0, tiled=True)
-    mixed = jnp.sum(back[..., :dev_feat].reshape(Y, dev_rows, dev_feat).astype(F32), axis=0)
-    mixed = mixed.astype(BF16)
-
-    score = back[:, 0, dev_feat : dev_feat + 3 * Y].astype(F32).reshape(Y, local, cols // local, 3, Y)
-    score = (score[..., 2, :] + score[..., 1, :]) + score[..., 0, :]
-    score = jnp.sum(score, axis=(0, 2)).T.reshape(Y * local)
+    first = jnp.sum(back[..., :dev_feat].reshape(Y, cols, part, dev_feat).astype(F32), axis=0)
+    mixed = jnp.stack([first, second], axis=1).astype(BF16).reshape(dev_rows, dev_feat)
+
+    score = back[:, 0, dev_feat : dev_feat + 3 * count].astype(F32).reshape(Y, cols, 3, count)
+    score = (score[:, :, 2] + score[:, :, 1]) + score[:, :, 0]
+    early = score[..., :Y].reshape(Y, local, cols // local, Y)
+    score = jnp.sum(early, axis=(0, 2)).T + jnp.sum(score[..., Y:], axis=1)
+    score = score.reshape(Y * local)
     score = jnp.broadcast_to(jnp.pad(score, (0, LANES - Y * local)), (Z, 1, LANES))
     score = lax.all_to_all(score, "z", 0, 0, tiled=True)
     fitness = score[:, 0, : Y * local].reshape(members)

time: 225 us -> 217 us (0.964)
  starting transfers between devices: 60.3 us -> 71.2 us
  waiting for transfers between devices: 70.1 us -> 63.2 us
  blocking collectives: 22.4 us -> 17.3 us
  local copies, waits for them, and re-layouts: 22.9 us -> 18.3 us
    ppermute x28 -> x26, waiting for transfers between devices: 50.4 us -> 25.8 us  [shift(): return lax.ppermute(value, axis, [(i, (i + step) % n) for i in range(n)])]
    all_to_all x1 -> x2, waiting for transfers between devices: 0.01 us -> 17.8 us  [the longest x1 17.8 us: body(): second = lax.all_to_all(leave(second, Z), WALL, 0, 0, tiled=True)]
    all_to_all x1 -> x2, starting transfers between devices: 6.95 us -> 17.3 us  [the longest x1 12.5 us: body(): second = lax.all_to_all(leave(second, Z), WALL, 0, 0, tiled=True)]
    all_to_all x1, blocking collectives: 22.4 us -> 17.3 us  [body(): back = lax.all_to_all(back, PLANE, 0, 0, tiled=True)]
    unnamed x20 -> x17, local copies, waits for them, and re-layouts: 5.15 us -> 0.43 us
    convert_element_type x8, other arithmetic: 5.5 us -> 2.88 us  [the longest x2 2.26 us: leave(): out = total.astype(BF16).reshape(devices, part, cols, dev_feat)]
    ppermute x28 -> x26, starting transfers between devices: 40.6 us -> 41.9 us  [shift(): return lax.ppermute(value, axis, [(i, (i + step) % n) for i in range(n)])]
  transfers between devices with their start and end apart: 32 -> 31, of which waited for: 19 -> 13; matrix products, arithmetic and copies ran while one was open for 12% -> 17% of each run, Pallas kernels for 0% -> 0%
where the time goes in v5:
time: 217 us
  starting transfers between devices  71.2 us (33%)
  waiting for transfers between devices  63.2 us (29%)
  matrix products  21.8 us (10%)
  local copies, waits for them, and re-layouts  18.3 us (8%)
  blocking collectives  17.3 us (8%)
  between operations  14.6 us (7%)
  other arithmetic  10.2 us (5%)
    ppermute x26, starting transfers between devices, shift(): return lax.ppermute(value, axis, [(i, (i + step) % n) for i in range(n)])  41.9 us
    ppermute x26, waiting for transfers between devices, shift(): return lax.ppermute(value, axis, [(i, (i + step) % n) for i in range(n)])  25.8 us
    all_to_all x1, waiting for transfers between devices, body(): second = lax.all_to_all(leave(second, Z), WALL, 0, 0, tiled=True)  17.8 us
    all_to_all x1, blocking collectives, body(): back = lax.all_to_all(back, PLANE, 0, 0, tiled=True)  17.3 us
    dynamic_update_slice x16, local copies, waits for them, and re-layouts, ring_gather(): total = lax.dynamic_update_slice(total, block, ((k * Z + place) * rows, 0))  14.1 us
    all_to_all x1, waiting for transfers between devices, body(): lax.all_to_all(wide.reshape(Y * cols, own, dev_feat + LANES), PLANE, 0, 0...  14 us
    all_to_all x1, starting transfers between devices, body(): second = lax.all_to_all(leave(second, Z), WALL, 0, 0, tiled=True)  12.5 us
    dot_general x1, matrix products, body(): jnp.dot(every[:, :model], weights[:, skip:], preferred_element_type=F32)  9.16 us
  transfers between devices with their start and end apart: 31, of which 13 were waited for; matrix products, arithmetic and copies ran while one was open for 17% of the time, Pallas kernels for 0%

profile of v5, /device:TPU:1, one launch (start us, length us, event | category | flops | bytes accessed | tf_op | source)
XLA Modules:
  0.0 216.6 jit_solution(14278470281109420412)
XLA Ops:
  9.9 2.7 %pad_maximum_fusion = bf16[640,1296]{0,1:T(8,128)(2,1)} fusion(bf16[640,432]{0,1:T(8,128)(2,1)} %param.10, bf16[640,432]{0,1:T(8,128)(2,1)} %param.9, bf16[640,432]{0,1:T(8,128)(2,1)} %bitcast.102), kind=kLoop, calls=%fused_computation.15 | loop fusion | flops 4976640 | bytes 3317760 | tf_op jit(solution)/shard_map/concatenate | solution.py:100
  13.6 8.6 %all-to-all-start = ((bf16[32,16,768]{2,1,0:T(8,128)(2,1)}), bf16[32,16,768]{2,1,0:T(8,128)(2,1)S(1)}, u32[]{:S(2)}, u32[]{:S(2)}) async-start(bf16[32,16,768]{2,1,0:T(8,128)(2,1)} %bitcast.5), calls=%async_computation | async-start | bytes 1572864 | tf_op jit(solution)/shard_map/all_to_all | solution.py:114
  22.4 14.0 %all-to-all-done = bf16[32,16,768]{2,1,0:T(8,128)(2,1)S(1)} async-done(((bf16[32,16,768]{2,1,0:T(8,128)(2,1)}), bf16[32,16,768]{2,1,0:T(8,128)(2,1)S(1)}, u32[]{:S(2)}, u32[]{:S(2)}) %all-to-all-start) | async-done | bytes 786464 | tf_op jit(solution)/shard_map/all_to_all | solution.py:114
  38.8 5.4 %collective-permute-start.1 = (bf16[32,5248]{1,0:T(8,128)(2,1)S(1)}, bf16[32,5248]{1,0:T(8,128)(2,1)S(1)}, u32[]{:S(2)}, u32[]{:S(2)}) collective-permute-start(bf16[32,5248]{1,0:T(8,128)(2,1)S(1)} %bitcast.90), channel_id=1, source_target_pairs={{0,224},{32,0},{64,32},{96,64},{128,96},{160,128},{192,160},{224,1... | collective-permute-start | bytes 1007624 | tf_op jit(solution)/shard_map/ppermute | solution.py:27
  44.2 2.7 %collective-permute-start.3 = (bf16[32,5248]{1,0:T(8,128)(2,1)S(1)}, bf16[32,5248]{1,0:T(8,128)(2,1)S(1)}, u32[]{:S(2)}, u32[]{:S(2)}) collective-permute-start(bf16[32,5248]{1,0:T(8,128)(2,1)S(1)} %bitcast.93), channel_id=1, source_target_pairs={{0,224},{32,0},{64,32},{96,64},{128,96},{160,128},{192,160},{224,1... | collective-permute-start | bytes 1007624 | tf_op jit(solution)/shard_map/ppermute | solution.py:27
  46.9 2.7 %dynamic_update_slice.48 = bf16[512,5248]{1,0:T(8,128)(2,1)} pad(bf16[32,5248]{1,0:T(8,128)(2,1)S(1)} %bitcast.91, bf16[]{:T(256)} %constant.164.clone.1), padding=0_480x0_0 | pad | bytes 5709826 | tf_op jit(solution)/shard_map/dynamic_update_slice | solution.py:45
  51.1 4.8 %all-to-all-start.1 = ((bf16[32,8,640]{2,1,0:T(8,128)(2,1)}), bf16[32,8,640]{2,1,0:T(8,128)(2,1)S(1)}, u32[]{:S(2)}, u32[]{:S(2)}) async-start(bf16[32,8,640]{2,1,0:T(8,128)(2,1)} %bitcast.12), calls=%async_computation.1 | async-start | bytes 655360 | tf_op jit(solution)/shard_map/all_to_all | solution.py:119
  59.2 2.7 %collective-permute-start.7 = (bf16[32,5248]{1,0:T(8,128)(2,1)S(1)}, bf16[32,5248]{1,0:T(8,128)(2,1)S(1)}, u32[]{:S(2)}, u32[]{:S(2)}) collective-permute-start(bf16[32,5248]{1,0:T(8,128)(2,1)S(1)} %collective-permute-done.3), channel_id=1, source_target_pairs={{0,224},{32,0},{64,32},{96,64},{128,96},{160,128},{192,160},{224,1... | collective-permute-start | bytes 1007624 | tf_op jit(solution)/shard_map/ppermute | solution.py:27
  66.5 2.7 %collective-permute-start.9 = (bf16[32,5248]{1,0:T(8,128)(2,1)S(1)}, bf16[32,5248]{1,0:T(8,128)(2,1)S(1)}, u32[]{:S(2)}, u32[]{:S(2)}) collective-permute-start(bf16[32,5248]{1,0:T(8,128)(2,1)S(1)} %collective-permute-done.5), channel_id=1, source_target_pairs={{0,224},{32,0},{64,32},{96,64},{128,96},{160,128},{192,160},{224,1... | collective-permute-start | bytes 1007624 | tf_op jit(solution)/shard_map/ppermute | solution.py:27
  69.1 4.5 %collective-permute-done.6 = bf16[32,5248]{1,0:T(8,128)(2,1)S(1)} collective-permute-done((bf16[32,5248]{1,0:T(8,128)(2,1)S(1)}, bf16[32,5248]{1,0:T(8,128)(2,1)S(1)}, u32[]{:S(2)}, u32[]{:S(2)}) %collective-permute-start.6) | collective-permute-done | bytes 335904 | tf_op jit(solution)/shard_map/ppermute | solution.py:27
  73.7 2.7 %collective-permute-start.11 = (bf16[32,5248]{1,0:T(8,128)(2,1)S(1)}, bf16[32,5248]{1,0:T(8,128)(2,1)S(1)}, u32[]{:S(2)}, u32[]{:S(2)}) collective-permute-start(bf16[32,5248]{1,0:T(8,128)(2,1)S(1)} %collective-permute-done.7), channel_id=1, source_target_pairs={{0,224},{32,0},{64,32},{96,64},{128,96},{160,128},{192,160},{224,1... | collective-permute-start | bytes 1007624 | tf_op jit(solution)/shard_map/ppermute | solution.py:27
  81.6 5.3 %collective-permute-done.11 = bf16[32,5248]{1,0:T(8,128)(2,1)S(1)} collective-permute-done((bf16[32,5248]{1,0:T(8,128)(2,1)S(1)}, bf16[32,5248]{1,0:T(8,128)(2,1)S(1)}, u32[]{:S(2)}, u32[]{:S(2)}) %collective-permute-start.11) | collective-permute-done | bytes 335904 | tf_op jit(solution)/shard_map/ppermute | solution.py:27
  86.9 3.5 %collective-permute-start.13 = (bf16[32,5248]{1,0:T(8,128)(2,1)S(1)}, bf16[32,5248]{1,0:T(8,128)(2,1)S(1)}, u32[]{:S(2)}, u32[]{:S(2)}) collective-permute-start(bf16[32,5248]{1,0:T(8,128)(2,1)S(1)} %collective-permute-done.11), channel_id=1, source_target_pairs={{0,224},{32,0},{64,32},{96,64},{128,96},{160,128},{192,160},{224,1... | collective-permute-start | bytes 1007624 | tf_op jit(solution)/shard_map/ppermute | solution.py:27
  97.0 9.2 %fusion = f32[512,912]{0,1:T(8,128)S(1)} fusion(bf16[5120,1296]{0,1:T(8,128)(2,1)} %all-gather.2.cloned.1.call-done, bf16[512,5248]{1,0:T(8,128)(2,1)} %constant_dynamic-update-slice_fusion.2), kind=kOutput, calls=%fused_computation | convolution fusion | flops 4781506560 | bytes 16449536 | tf_op jit(solution)/shard_map/dot_general | solution.py:150
  108.5 3.8 %fusion.5 = f32[256,5120]{1,0:T(8,128)S(1)} fusion(bf16[256,432]{1,0:T(8,128)(2,1)S(1)} %bitcast.99, bf16[5120,1296]{0,1:T(8,128)(2,1)} %all-gather.2.cloned.1.call-done), kind=kOutput, calls=%fused_computation.5 | convolution fusion | flops 1132462080 | bytes 9887744 | tf_op jit(solution)/shard_map/dot_general | solution.py:164
  112.8 3.2 %collective-permute-start.15 = (bf16[32,2560]{1,0:T(8,128)(2,1)S(1)}, bf16[32,2560]{1,0:T(8,128)(2,1)S(1)}, u32[]{:S(2)}, u32[]{:S(2)}) collective-permute-start(bf16[32,2560]{1,0:T(8,128)(2,1)S(1)} %get-tuple-element.27), channel_id=1, source_target_pairs={{0,224},{32,0},{64,32},{96,64},{128,96},{160,128},{192,160},{224,1... | collective-permute-start | bytes 491528 | tf_op jit(solution)/shard_map/ppermute | solution.py:27
  116.3 3.8 %fusion.3 = f32[256,5120]{1,0:T(8,128)S(1)} fusion(bf16[256,432]{1,0:T(8,128)(2,1)S(1)} %bitcast.98, bf16[5120,1296]{0,1:T(8,128)(2,1)} %all-gather.2.cloned.1.call-done), kind=kOutput, calls=%fused_computation.3 | convolution fusion | flops 1132462080 | bytes 9887744 | tf_op jit(solution)/shard_map/dot_general | solution.py:164
  128.4 2.7 %collective-permute-start.19 = (bf16[32,5120]{1,0:T(8,128)(2,1)S(1)}, bf16[32,5120]{1,0:T(8,128)(2,1)S(1)}, u32[]{:S(2)}, u32[]{:S(2)}) collective-permute-start(bf16[32,5120]{1,0:T(8,128)(2,1)S(1)} %get-tuple-element.31), channel_id=1, source_target_pairs={{0,224},{32,0},{64,32},{96,64},{128,96},{160,128},{192,160},{224,1... | collective-permute-start | bytes 983048 | tf_op jit(solution)/shard_map/ppermute | solution.py:27
  138.5 6.3 %collective-permute-done.24 = bf16[64,5120]{1,0:T(8,128)(2,1)S(1)} collective-permute-done((bf16[64,5120]{1,0:T(8,128)(2,1)S(1)}, bf16[64,5120]{1,0:T(8,128)(2,1)S(1)}, u32[]{:S(2)}, u32[]{:S(2)}) %collective-permute-start.24) | collective-permute-done | bytes 655392 | tf_op jit(solution)/shard_map/ppermute | solution.py:27
  145.9 12.5 %all-to-all-start.2 = ((bf16[64,8,640]{2,1,0:T(8,128)(2,1)}), bf16[64,8,640]{2,1,0:T(8,128)(2,1)S(1)}, u32[]{:S(2)}, u32[]{:S(2)}) async-start(bf16[64,8,640]{2,1,0:T(8,128)(2,1)} %bitcast.31), calls=%async_computation.2 | async-start | bytes 1310720 | tf_op jit(solution)/shard_map/all_to_all | solution.py:171
  160.9 17.8 %all-to-all-done.2 = bf16[64,8,640]{2,1,0:T(8,128)(2,1)S(1)} async-done(((bf16[64,8,640]{2,1,0:T(8,128)(2,1)}), bf16[64,8,640]{2,1,0:T(8,128)(2,1)S(1)}, u32[]{:S(2)}, u32[]{:S(2)}) %all-to-all-start.2) | async-done | bytes 655392 | tf_op jit(solution)/shard_map/all_to_all | solution.py:171
  179.4 17.3 %all_to_all.25 = bf16[32,8,768]{2,1,0:T(8,128)(2,1)S(1)} all-to-all(bf16[32,8,768]{2,1,0:T(8,128)(2,1)S(1)} %pad_maximum_fusion.1), channel_id=1, replica_groups=mesh['z'=8,'y'=4,'x'=4,'core'=2] {'y','x','core'}, dimensions={0} | all-to-all | bytes 786432 | tf_op jit(solution)/shard_map/all_to_all | solution.py:182
  198.1 3.3 %all-to-all-start.4 = ((f32[8,1,128]{2,1,0:T(1,128)}), f32[8,1,128]{2,1,0:T(1,128)S(1)}, u32[]{:S(2)}, u32[]{:S(2)}) async-start(f32[8,1,128]{2,1,0:T(1,128)} %broadcast_in_dim.30), calls=%async_computation.4 | async-start | bytes 8192 | tf_op jit(solution)/shard_map/all_to_all | solution.py:192
  202.2 5.6 %all-to-all-done.4 = f32[8,1,128]{2,1,0:T(1,128)S(1)} async-done(((f32[8,1,128]{2,1,0:T(1,128)}), f32[8,1,128]{2,1,0:T(1,128)S(1)}, u32[]{:S(2)}, u32[]{:S(2)}) %all-to-all-start.4) | async-done | bytes 4128 | tf_op jit(solution)/shard_map/all_to_all | solution.py:192
  (153 shorter events, 54.2 us)
Async XLA Ops:
  7.2 89.8 %all-gather.2.cloned.1.call-start = ((), (), s32[]{:S(2)}) async-start(), calls=%async_computation.5 | async-start | bytes 14929920 | tf_op jit(solution)/shard_map/all_gather | solution.py:113
  13.6 22.8 %all-to-all-start = ((bf16[32,16,768]{2,1,0:T(8,128)(2,1)}), bf16[32,16,768]{2,1,0:T(8,128)(2,1)S(1)}, u32[]{:S(2)}, u32[]{:S(2)}) async-start(bf16[32,16,768]{2,1,0:T(8,128)(2,1)} %bitcast.5), calls=%async_computation | async-start | bytes 1572864 | tf_op jit(solution)/shard_map/all_to_all | solution.py:114
  37.1 18.9 %collective-permute-start = (bf16[32,5248]{1,0:T(8,128)(2,1)S(1)}, bf16[32,5248]{1,0:T(8,128)(2,1)S(1)}, u32[]{:S(2)}, u32[]{:S(2)}) collective-permute-start(bf16[32,5248]{1,0:T(8,128)(2,1)S(1)} %bitcast.89), channel_id=1, source_target_pairs={{0,32},{32,64},{64,96},{96,128},{128,160},{160,192},{192,224},{224... | collective-permute-start | bytes 1007624 | tf_op jit(solution)/shard_map/ppermute | solution.py:27
  38.8 17.3 %collective-permute-start.1 = (bf16[32,5248]{1,0:T(8,128)(2,1)S(1)}, bf16[32,5248]{1,0:T(8,128)(2,1)S(1)}, u32[]{:S(2)}, u32[]{:S(2)}) collective-permute-start(bf16[32,5248]{1,0:T(8,128)(2,1)S(1)} %bitcast.90), channel_id=1, source_target_pairs={{0,224},{32,0},{64,32},{96,64},{128,96},{160,128},{192,160},{224,1... | collective-permute-start | bytes 1007624 | tf_op jit(solution)/shard_map/ppermute | solution.py:27
  44.2 15.1 %collective-permute-start.2 = (bf16[32,5248]{1,0:T(8,128)(2,1)S(1)}, bf16[32,5248]{1,0:T(8,128)(2,1)S(1)}, u32[]{:S(2)}, u32[]{:S(2)}) collective-permute-start(bf16[32,5248]{1,0:T(8,128)(2,1)S(1)} %bitcast.92), channel_id=1, source_target_pairs={{0,32},{32,64},{64,96},{96,128},{128,160},{160,192},{192,224},{224... | collective-permute-start | bytes 1007624 | tf_op jit(solution)/shard_map/ppermute | solution.py:27
  44.2 15.1 %collective-permute-start.3 = (bf16[32,5248]{1,0:T(8,128)(2,1)S(1)}, bf16[32,5248]{1,0:T(8,128)(2,1)S(1)}, u32[]{:S(2)}, u32[]{:S(2)}) collective-permute-start(bf16[32,5248]{1,0:T(8,128)(2,1)S(1)} %bitcast.93), channel_id=1, source_target_pairs={{0,224},{32,0},{64,32},{96,64},{128,96},{160,128},{192,160},{224,1... | collective-permute-start | bytes 1007624 | tf_op jit(solution)/shard_map/ppermute | solution.py:27
  51.1 57.2 %all-to-all-start.1 = ((bf16[32,8,640]{2,1,0:T(8,128)(2,1)}), bf16[32,8,640]{2,1,0:T(8,128)(2,1)S(1)}, u32[]{:S(2)}, u32[]{:S(2)}) async-start(bf16[32,8,640]{2,1,0:T(8,128)(2,1)} %bitcast.12), calls=%async_computation.1 | async-start | bytes 655360 | tf_op jit(solution)/shard_map/all_to_all | solution.py:119
  55.9 10.5 %collective-permute-start.4 = (bf16[32,5248]{1,0:T(8,128)(2,1)S(1)}, bf16[32,5248]{1,0:T(8,128)(2,1)S(1)}, u32[]{:S(2)}, u32[]{:S(2)}) collective-permute-start(bf16[32,5248]{1,0:T(8,128)(2,1)S(1)} %collective-permute-done), channel_id=1, source_target_pairs={{0,32},{32,64},{64,96},{96,128},{128,160},{160,192},{192,224},{224... | collective-permute-start | bytes 1007624 | tf_op jit(solution)/shard_map/ppermute | solution.py:27
  56.0 10.4 %collective-permute-start.5 = (bf16[32,5248]{1,0:T(8,128)(2,1)S(1)}, bf16[32,5248]{1,0:T(8,128)(2,1)S(1)}, u32[]{:S(2)}, u32[]{:S(2)}) collective-permute-start(bf16[32,5248]{1,0:T(8,128)(2,1)S(1)} %collective-permute-done.1), channel_id=1, source_target_pairs={{0,224},{32,0},{64,32},{96,64},{128,96},{160,128},{192,160},{224,1... | collective-permute-start | bytes 1007624 | tf_op jit(solution)/shard_map/ppermute | solution.py:27
  59.2 14.4 %collective-permute-start.6 = (bf16[32,5248]{1,0:T(8,128)(2,1)S(1)}, bf16[32,5248]{1,0:T(8,128)(2,1)S(1)}, u32[]{:S(2)}, u32[]{:S(2)}) collective-permute-start(bf16[32,5248]{1,0:T(8,128)(2,1)S(1)} %collective-permute-done.2), channel_id=1, source_target_pairs={{0,32},{32,64},{64,96},{96,128},{128,160},{160,192},{192,224},{224... | collective-permute-start | bytes 1007624 | tf_op jit(solution)/shard_map/ppermute | solution.py:27
  59.2 14.4 %collective-permute-start.7 = (bf16[32,5248]{1,0:T(8,128)(2,1)S(1)}, bf16[32,5248]{1,0:T(8,128)(2,1)S(1)}, u32[]{:S(2)}, u32[]{:S(2)}) collective-permute-start(bf16[32,5248]{1,0:T(8,128)(2,1)S(1)} %collective-permute-done.3), channel_id=1, source_target_pairs={{0,224},{32,0},{64,32},{96,64},{128,96},{160,128},{192,160},{224,1... | collective-permute-start | bytes 1007624 | tf_op jit(solution)/shard_map/ppermute | solution.py:27
  66.5 14.4 %collective-permute-start.8 = (bf16[32,5248]{1,0:T(8,128)(2,1)S(1)}, bf16[32,5248]{1,0:T(8,128)(2,1)S(1)}, u32[]{:S(2)}, u32[]{:S(2)}) collective-permute-start(bf16[32,5248]{1,0:T(8,128)(2,1)S(1)} %collective-permute-done.4), channel_id=1, source_target_pairs={{0,32},{32,64},{64,96},{96,128},{128,160},{160,192},{192,224},{224... | collective-permute-start | bytes 1007624 | tf_op jit(solution)/shard_map/ppermute | solution.py:27
  66.5 24.0 %collective-permute-start.9 = (bf16[32,5248]{1,0:T(8,128)(2,1)S(1)}, bf16[32,5248]{1,0:T(8,128)(2,1)S(1)}, u32[]{:S(2)}, u32[]{:S(2)}) collective-permute-start(bf16[32,5248]{1,0:T(8,128)(2,1)S(1)} %collective-permute-done.5), channel_id=1, source_target_pairs={{0,224},{32,0},{64,32},{96,64},{128,96},{160,128},{192,160},{224,1... | collective-permute-start | bytes 1007624 | tf_op jit(solution)/shard_map/ppermute | solution.py:27
  73.6 17.5 %collective-permute-start.10 = (bf16[32,5248]{1,0:T(8,128)(2,1)S(1)}, bf16[32,5248]{1,0:T(8,128)(2,1)S(1)}, u32[]{:S(2)}, u32[]{:S(2)}) collective-permute-start(bf16[32,5248]{1,0:T(8,128)(2,1)S(1)} %collective-permute-done.6), channel_id=1, source_target_pairs={{0,32},{32,64},{64,96},{96,128},{128,160},{160,192},{192,224},{224... | collective-permute-start | bytes 1007624 | tf_op jit(solution)/shard_map/ppermute | solution.py:27
  73.7 13.3 %collective-permute-start.11 = (bf16[32,5248]{1,0:T(8,128)(2,1)S(1)}, bf16[32,5248]{1,0:T(8,128)(2,1)S(1)}, u32[]{:S(2)}, u32[]{:S(2)}) collective-permute-start(bf16[32,5248]{1,0:T(8,128)(2,1)S(1)} %collective-permute-done.7), channel_id=1, source_target_pairs={{0,224},{32,0},{64,32},{96,64},{128,96},{160,128},{192,160},{224,1... | collective-permute-start | bytes 1007624 | tf_op jit(solution)/shard_map/ppermute | solution.py:27
  80.8 14.3 %collective-permute-start.12 = (bf16[32,5248]{1,0:T(8,128)(2,1)S(1)}, bf16[32,5248]{1,0:T(8,128)(2,1)S(1)}, u32[]{:S(2)}, u32[]{:S(2)}) collective-permute-start(bf16[32,5248]{1,0:T(8,128)(2,1)S(1)} %collective-permute-done.8), channel_id=1, source_target_pairs={{0,32},{32,64},{64,96},{96,128},{128,160},{160,192},{192,224},{224... | collective-permute-start | bytes 1007624 | tf_op jit(solution)/shard_map/ppermute | solution.py:27
  86.9 9.3 %collective-permute-start.13 = (bf16[32,5248]{1,0:T(8,128)(2,1)S(1)}, bf16[32,5248]{1,0:T(8,128)(2,1)S(1)}, u32[]{:S(2)}, u32[]{:S(2)}) collective-permute-start(bf16[32,5248]{1,0:T(8,128)(2,1)S(1)} %collective-permute-done.11), channel_id=1, source_target_pairs={{0,224},{32,0},{64,32},{96,64},{128,96},{160,128},{192,160},{224,1... | collective-permute-start | bytes 1007624 | tf_op jit(solution)/shard_map/ppermute | solution.py:27
  123.1 8.0 %collective-permute-start.22 = (bf16[64,2560]{1,0:T(8,128)(2,1)S(1)}, bf16[64,2560]{1,0:T(8,128)(2,1)S(1)}, u32[]{:S(2)}, u32[]{:S(2)}) collective-permute-start(bf16[64,2560]{1,0:T(8,128)(2,1)S(1)} %get-tuple-element.35), channel_id=1, source_target_pairs={{0,8},{8,16},{16,24},{24,0},{1,9},{9,17},{17,25},{25,1},{2,10},{10... | collective-permute-start | bytes 983048 | tf_op jit(solution)/shard_map/ppermute | solution.py:27
  131.3 13.5 %collective-permute-start.24 = (bf16[64,5120]{1,0:T(8,128)(2,1)S(1)}, bf16[64,5120]{1,0:T(8,128)(2,1)S(1)}, u32[]{:S(2)}, u32[]{:S(2)}) collective-permute-start(bf16[64,5120]{1,0:T(8,128)(2,1)S(1)} %get-tuple-element.37), channel_id=1, source_target_pairs={{0,8},{8,16},{16,24},{24,0},{1,9},{9,17},{17,25},{25,1},{2,10},{10... | collective-permute-start | bytes 1966088 | tf_op jit(solution)/shard_map/ppermute | solution.py:27
  132.8 12.1 %collective-permute-start.25 = (bf16[64,5120]{1,0:T(8,128)(2,1)S(1)}, bf16[64,5120]{1,0:T(8,128)(2,1)S(1)}, u32[]{:S(2)}, u32[]{:S(2)}) collective-permute-start(bf16[64,5120]{1,0:T(8,128)(2,1)S(1)} %get-tuple-element.38), channel_id=1, source_target_pairs={{0,24},{8,0},{16,8},{24,16},{1,25},{9,1},{17,9},{25,17},{2,26},{10... | collective-permute-start | bytes 1966088 | tf_op jit(solution)/shard_map/ppermute | solution.py:27
  135.7 22.7 %collective-permute-start.20 = (bf16[32,5120]{1,0:T(8,128)(2,1)S(1)}, bf16[32,5120]{1,0:T(8,128)(2,1)S(1)}, u32[]{:S(2)}, u32[]{:S(2)}) collective-permute-start(bf16[32,5120]{1,0:T(8,128)(2,1)S(1)} %get-tuple-element.32), channel_id=1, source_target_pairs={{0,32},{32,64},{64,96},{96,128},{128,160},{160,192},{192,224},{224... | collective-permute-start | bytes 983048 | tf_op jit(solution)/shard_map/ppermute | solution.py:27
  137.1 21.3 %collective-permute-start.21 = (bf16[32,5120]{1,0:T(8,128)(2,1)S(1)}, bf16[32,5120]{1,0:T(8,128)(2,1)S(1)}, u32[]{:S(2)}, u32[]{:S(2)}) collective-permute-start(bf16[32,5120]{1,0:T(8,128)(2,1)S(1)} %get-tuple-element.33), channel_id=1, source_target_pairs={{0,224},{32,0},{64,32},{96,64},{128,96},{160,128},{192,160},{224,1... | collective-permute-start | bytes 983048 | tf_op jit(solution)/shard_map/ppermute | solution.py:27
  145.9 32.8 %all-to-all-start.2 = ((bf16[64,8,640]{2,1,0:T(8,128)(2,1)}), bf16[64,8,640]{2,1,0:T(8,128)(2,1)S(1)}, u32[]{:S(2)}, u32[]{:S(2)}) async-start(bf16[64,8,640]{2,1,0:T(8,128)(2,1)} %bitcast.31), calls=%async_computation.2 | async-start | bytes 1310720 | tf_op jit(solution)/shard_map/all_to_all | solution.py:171
  198.1 9.7 %all-to-all-start.4 = ((f32[8,1,128]{2,1,0:T(1,128)}), f32[8,1,128]{2,1,0:T(1,128)S(1)}, u32[]{:S(2)}, u32[]{:S(2)}) async-start(f32[8,1,128]{2,1,0:T(1,128)} %broadcast_in_dim.30), calls=%async_computation.4 | async-start | bytes 8192 | tf_op jit(solution)/shard_map/all_to_all | solution.py:192
  (13 other events, 225.2 us)
Sparse Core Ops, SparseCore 0:
  13.7 80.3 all-gather.1

commit v6 on v5

--- a/solution.py
+++ b/solution.py
@@ -27,22 +27,20 @@
     return lax.ppermute(value, axis, [(i, (i + step) % n) for i in range(n)])
 
 
-def ring_gather(chunks):
+def ring_gather(value):
     half = Z // 2
-    rows, width = chunks[0].shape
-    total = jnp.zeros((len(chunks) * Z * rows, width), chunks[0].dtype)
-    ends = [[chunk, chunk] for chunk in chunks]
-    landed = [(k, 0, chunk) for k, chunk in enumerate(chunks)]
-    for step in range(1, half + 1):
-        for k, end in enumerate(ends):
-            if step < half or k % 2 == 0:
-                end[0] = shift(end[0], 1)
-                landed.append((k, Z - step, end[0]))
-            if step < half or k % 2 == 1:
-                end[1] = shift(end[1], -1)
-                landed.append((k, step, end[1]))
-    for k, place, block in landed:
-        total = lax.dynamic_update_slice(total, block, ((k * Z + place) * rows, 0))
+    rows, width = value.shape
+    mid = width // LANES // 2 * LANES
+    total = jnp.zeros((Z * rows, width), value.dtype)
+    ahead = behind = value
+    landed = [(0, 0, value)]
+    for step in range(1, half):
+        ahead, behind = shift(ahead, 1), shift(behind, -1)
+        landed += [(Z - step, 0, ahead), (step, 0, behind)]
+    landed.append((half, 0, shift(ahead[:, :mid], 1)))
+    landed.append((half, mid, shift(behind[:, mid:], -1)))
+    for place, column, block in landed:
+        total = lax.dynamic_update_slice(total, block, (place * rows, column))
     return total
 
 
@@ -126,14 +124,13 @@
     rows = jnp.swapaxes(moved[..., :dev_feat], 1, 2).reshape(Y, own, model)
     rows = jnp.concatenate([rows, extra], axis=2).reshape(Y * own, model + LANES)
     plane = Y * own
-    mid = plane // 2
-
-    every = ring_gather([rows[:mid], rows[mid:]])
+
+    every = ring_gather(rows)
 
     row = lax.broadcasted_iota(jnp.int32, (Z * plane, members * RANK * 2), 0)
     column = lax.broadcasted_iota(jnp.int32, (Z * plane, members * RANK * 2), 1)
-    row_y = row // (Z * mid) * (Y // 2) + row % mid // own
-    row_z = (z + row // mid) % Z
+    row_y = row % plane // own
+    row_z = (z + row // plane) % Z
     member = (row_z * Y + row_y) * local + (x * C + core) * own // SEQ
     spread_row = lax.broadcasted_iota(jnp.int32, (LANES, members * RANK * 2), 0)
     spread_col = lax.broadcasted_iota(jnp.int32, (LANES, members * RANK * 2), 1)
@@ -153,9 +150,9 @@
     hidden = (jax.nn.silu(gate) * up).astype(BF16)
     hidden, goal = lax.optimization_barrier((hidden, goal))
 
-    hidden = hidden.reshape(2, Z, Y // 2, 2, part, units)
-    first = jnp.transpose(hidden[:, :, :, 0], (1, 0, 2, 3, 4)).reshape(Z * Y * part, units)
-    second = jnp.transpose(hidden[:, :, :, 1], (1, 0, 2, 3, 4)).reshape(Z, Y, part, units)
+    hidden = hidden.reshape(Z, Y, 2, part, units)
+    first = hidden[:, :, 0].reshape(Z * Y * part, units)
+    second = hidden[:, :, 1]
     second = jnp.swapaxes(turn(second, (Z - z) % Z), 0, 1)
     second = turn(second, y).reshape(Y * Z * part, units)
     down = weights[:, :units]

time: 217 us -> 223 us (1.028)
  waiting for transfers between devices: 63.2 us -> 82.6 us
  starting transfers between devices: 71.2 us -> 62.3 us
  local copies, waits for them, and re-layouts: 18.3 us -> 14 us
    ppermute x26 -> x20, waiting for transfers between devices: 25.8 us -> 45.1 us  [shift(): return lax.ppermute(value, axis, [(i, (i + step) % n) for i in range(n)])]
    ppermute x26 -> x20, starting transfers between devices: 41.9 us -> 33.8 us  [shift(): return lax.ppermute(value, axis, [(i, (i + step) % n) for i in range(n)])]
    dynamic_update_slice x16 -> x9, local copies, waits for them, and re-layouts: 14.1 us -> 9.62 us  [ring_gather(): total = lax.dynamic_update_slice(total, block, (place * rows, column))]
  transfers between devices with their start and end apart: 31 -> 25, of which waited for: 13 -> 12; matrix products, arithmetic and copies ran while one was open for 17% -> 14% of each run, Pallas kernels for 0% -> 0%
where the time goes in v6:
time: 223 us
  waiting for transfers between devices  82.6 us (37%)
  starting transfers between devices  62.3 us (28%)
  matrix products  21.5 us (10%)
  blocking collectives  17.3 us (8%)
  between operations  14.6 us (7%)
  local copies, waits for them, and re-layouts  14 us (6%)
  other arithmetic  10.2 us (5%)
    ppermute x20, waiting for transfers between devices, shift(): return lax.ppermute(value, axis, [(i, (i + step) % n) for i in range(n)])  45.1 us
    ppermute x20, starting transfers between devices, shift(): return lax.ppermute(value, axis, [(i, (i + step) % n) for i in range(n)])  33.8 us
    all_to_all x1, waiting for transfers between devices, body(): second = lax.all_to_all(leave(second, Z), WALL, 0, 0, tiled=True)  17.8 us
    all_to_all x1, blocking collectives, body(): back = lax.all_to_all(back, PLANE, 0, 0, tiled=True)  17.3 us
    all_to_all x1, waiting for transfers between devices, body(): lax.all_to_all(wide.reshape(Y * cols, own, dev_feat + LANES), PLANE, 0, 0...  14.1 us
    all_to_all x1, starting transfers between devices, body(): second = lax.all_to_all(leave(second, Z), WALL, 0, 0, tiled=True)  12.2 us
    dynamic_update_slice x9, local copies, waits for them, and re-layouts, ring_gather(): total = lax.dynamic_update_slice(total, block, (place * rows, column))  9.62 us
    dot_general x1, matrix products, body(): jnp.dot(every[:, :model], weights[:, skip:], preferred_element_type=F32)  9.16 us
  transfers between devices with their start and end apart: 25, of which 12 were waited for; matrix products, arithmetic and copies ran while one was open for 14% of the time, Pallas kernels for 0%

profile of v6, /device:TPU:1, one launch (start us, length us, event | category | flops | bytes accessed | tf_op | source)
XLA Modules:
  0.0 222.5 jit_solution(17536726637706660541)
XLA Ops:
  9.9 2.7 %pad_maximum_fusion = bf16[640,1296]{0,1:T(8,128)(2,1)} fusion(bf16[640,432]{0,1:T(8,128)(2,1)} %param.10, bf16[640,432]{0,1:T(8,128)(2,1)} %param.9, bf16[640,432]{0,1:T(8,128)(2,1)} %bitcast.89), kind=kLoop, calls=%fused_computation.15 | loop fusion | flops 4976640 | bytes 3317760 | tf_op jit(solution)/shard_map/concatenate | solution.py:98
  13.6 8.6 %all-to-all-start = ((bf16[32,16,768]{2,1,0:T(8,128)(2,1)}), bf16[32,16,768]{2,1,0:T(8,128)(2,1)S(1)}, u32[]{:S(2)}, u32[]{:S(2)}) async-start(bf16[32,16,768]{2,1,0:T(8,128)(2,1)} %bitcast.5), calls=%async_computation | async-start | bytes 1572864 | tf_op jit(solution)/shard_map/all_to_all | solution.py:112
  22.3 14.1 %all-to-all-done = bf16[32,16,768]{2,1,0:T(8,128)(2,1)S(1)} async-done(((bf16[32,16,768]{2,1,0:T(8,128)(2,1)}), bf16[32,16,768]{2,1,0:T(8,128)(2,1)S(1)}, u32[]{:S(2)}, u32[]{:S(2)}) %all-to-all-start) | async-done | bytes 786464 | tf_op jit(solution)/shard_map/all_to_all | solution.py:112
  38.8 5.4 %collective-permute-start.1 = (bf16[64,5248]{1,0:T(8,128)(2,1)S(1)}, bf16[64,5248]{1,0:T(8,128)(2,1)S(1)}, u32[]{:S(2)}, u32[]{:S(2)}) collective-permute-start(bf16[64,5248]{1,0:T(8,128)(2,1)S(1)} %pad_maximum_fusion.1), channel_id=1, source_target_pairs={{0,224},{32,0},{64,32},{96,64},{128,96},{160,128},{192,160},{224,1... | collective-permute-start | bytes 2015240 | tf_op jit(solution)/shard_map/ppermute | solution.py:27
  44.3 2.7 %dynamic_update_slice.27 = bf16[512,5248]{1,0:T(8,128)(2,1)} pad(bf16[64,5248]{1,0:T(8,128)(2,1)S(1)} %pad_maximum_fusion.1, bf16[]{:T(256)} %constant.147.clone.1), padding=0_448x0_0 | pad | bytes 6045698 | tf_op jit(solution)/shard_map/dynamic_update_slice | solution.py:43
  47.8 4.3 %all-to-all-start.1 = ((bf16[32,8,640]{2,1,0:T(8,128)(2,1)}), bf16[32,8,640]{2,1,0:T(8,128)(2,1)S(1)}, u32[]{:S(2)}, u32[]{:S(2)}) async-start(bf16[32,8,640]{2,1,0:T(8,128)(2,1)} %bitcast.11), calls=%async_computation.1 | async-start | bytes 655360 | tf_op jit(solution)/shard_map/all_to_all | solution.py:117
  52.1 7.2 %collective-permute-done = bf16[64,5248]{1,0:T(8,128)(2,1)S(1)} collective-permute-done((bf16[64,5248]{1,0:T(8,128)(2,1)S(1)}, bf16[64,5248]{1,0:T(8,128)(2,1)S(1)}, u32[]{:S(2)}, u32[]{:S(2)}) %collective-permute-start) | collective-permute-done | bytes 671776 | tf_op jit(solution)/shard_map/ppermute | solution.py:27
  59.3 2.7 %collective-permute-start.3 = (bf16[64,5248]{1,0:T(8,128)(2,1)S(1)}, bf16[64,5248]{1,0:T(8,128)(2,1)S(1)}, u32[]{:S(2)}, u32[]{:S(2)}) collective-permute-start(bf16[64,5248]{1,0:T(8,128)(2,1)S(1)} %collective-permute-done.1), channel_id=1, source_target_pairs={{0,224},{32,0},{64,32},{96,64},{128,96},{160,128},{192,160},{224,1... | collective-permute-start | bytes 2015240 | tf_op jit(solution)/shard_map/ppermute | solution.py:27
  63.8 12.5 %collective-permute-done.2 = bf16[64,5248]{1,0:T(8,128)(2,1)S(1)} collective-permute-done((bf16[64,5248]{1,0:T(8,128)(2,1)S(1)}, bf16[64,5248]{1,0:T(8,128)(2,1)S(1)}, u32[]{:S(2)}, u32[]{:S(2)}) %collective-permute-start.2) | collective-permute-done | bytes 671776 | tf_op jit(solution)/shard_map/ppermute | solution.py:27
  76.3 2.7 %collective-permute-start.5 = (bf16[64,5248]{1,0:T(8,128)(2,1)S(1)}, bf16[64,5248]{1,0:T(8,128)(2,1)S(1)}, u32[]{:S(2)}, u32[]{:S(2)}) collective-permute-start(bf16[64,5248]{1,0:T(8,128)(2,1)S(1)} %collective-permute-done.3), channel_id=1, source_target_pairs={{0,224},{32,0},{64,32},{96,64},{128,96},{160,128},{192,160},{224,1... | collective-permute-start | bytes 2015240 | tf_op jit(solution)/shard_map/ppermute | solution.py:27
  80.8 11.6 %collective-permute-done.4 = bf16[64,5248]{1,0:T(8,128)(2,1)S(1)} collective-permute-done((bf16[64,5248]{1,0:T(8,128)(2,1)S(1)}, bf16[64,5248]{1,0:T(8,128)(2,1)S(1)}, u32[]{:S(2)}, u32[]{:S(2)}) %collective-permute-start.4) | collective-permute-done | bytes 671776 | tf_op jit(solution)/shard_map/ppermute | solution.py:27
  92.6 2.9 %collective-permute-start.7 = (bf16[64,2688]{1,0:T(8,128)(2,1)S(1)}, bf16[64,2688]{1,0:T(8,128)(2,1)S(1)}, u32[]{:S(2)}, u32[]{:S(2)}) collective-permute-start(bf16[64,2688]{1,0:T(8,128)(2,1)S(1)} %slice.175), channel_id=1, source_target_pairs={{0,224},{32,0},{64,32},{96,64},{128,96},{160,128},{192,160},{224,1... | collective-permute-start | bytes 1032200 | tf_op jit(solution)/shard_map/ppermute | solution.py:27
  97.3 3.0 %collective-permute-done.6 = bf16[64,2560]{1,0:T(8,128)(2,1)S(1)} collective-permute-done((bf16[64,2560]{1,0:T(8,128)(2,1)S(1)}, bf16[64,2560]{1,0:T(8,128)(2,1)S(1)}, u32[]{:S(2)}, u32[]{:S(2)}) %collective-permute-start.6) | collective-permute-done | bytes 327712 | tf_op jit(solution)/shard_map/ppermute | solution.py:27
  101.9 9.2 %fusion = f32[512,912]{0,1:T(8,128)S(1)} fusion(bf16[5120,1296]{0,1:T(8,128)(2,1)} %all-gather.2.cloned.1.call-done, bf16[512,5248]{1,0:T(8,128)(2,1)} %constant_dynamic-update-slice_fusion.9), kind=kOutput, calls=%fused_computation | convolution fusion | flops 4781506560 | bytes 16449536 | tf_op jit(solution)/shard_map/dot_general | solution.py:147
  113.2 3.8 %fusion.5 = f32[256,5120]{1,0:T(8,128)S(1)} fusion(bf16[256,432]{1,0:T(8,128)(2,1)S(1)} %bitcast.87, bf16[5120,1296]{0,1:T(8,128)(2,1)} %all-gather.2.cloned.1.call-done), kind=kOutput, calls=%fused_computation.5 | convolution fusion | flops 1132462080 | bytes 9887744 | tf_op jit(solution)/shard_map/dot_general | solution.py:161
  120.2 3.8 %fusion.3 = f32[256,5120]{1,0:T(8,128)S(1)} fusion(bf16[256,432]{1,0:T(8,128)(2,1)S(1)} %bitcast.86, bf16[5120,1296]{0,1:T(8,128)(2,1)} %all-gather.2.cloned.1.call-done), kind=kOutput, calls=%fused_computation.3 | convolution fusion | flops 1132462080 | bytes 9887744 | tf_op jit(solution)/shard_map/dot_general | solution.py:161
  126.9 4.3 %collective-permute-start.16 = (bf16[64,2560]{1,0:T(8,128)(2,1)S(1)}, bf16[64,2560]{1,0:T(8,128)(2,1)S(1)}, u32[]{:S(2)}, u32[]{:S(2)}) collective-permute-start(bf16[64,2560]{1,0:T(8,128)(2,1)S(1)} %get-tuple-element.35), channel_id=1, source_target_pairs={{0,8},{8,16},{16,24},{24,0},{1,9},{9,17},{17,25},{25,1},{2,10},{10... | collective-permute-start | bytes 983048 | tf_op jit(solution)/shard_map/ppermute | solution.py:27
  131.6 3.0 %collective-permute-start.13 = (bf16[32,5120]{1,0:T(8,128)(2,1)S(1)}, bf16[32,5120]{1,0:T(8,128)(2,1)S(1)}, u32[]{:S(2)}, u32[]{:S(2)}) collective-permute-start(bf16[32,5120]{1,0:T(8,128)(2,1)S(1)} %get-tuple-element.31), channel_id=1, source_target_pairs={{0,224},{32,0},{64,32},{96,64},{128,96},{160,128},{192,160},{224,1... | collective-permute-start | bytes 983048 | tf_op jit(solution)/shard_map/ppermute | solution.py:27
  143.3 7.4 %collective-permute-done.18 = bf16[64,5120]{1,0:T(8,128)(2,1)S(1)} collective-permute-done((bf16[64,5120]{1,0:T(8,128)(2,1)S(1)}, bf16[64,5120]{1,0:T(8,128)(2,1)S(1)}, u32[]{:S(2)}, u32[]{:S(2)}) %collective-permute-start.18) | collective-permute-done | bytes 655392 | tf_op jit(solution)/shard_map/ppermute | solution.py:27
  152.0 12.2 %all-to-all-start.2 = ((bf16[64,8,640]{2,1,0:T(8,128)(2,1)}), bf16[64,8,640]{2,1,0:T(8,128)(2,1)S(1)}, u32[]{:S(2)}, u32[]{:S(2)}) async-start(bf16[64,8,640]{2,1,0:T(8,128)(2,1)} %bitcast.26), calls=%async_computation.2 | async-start | bytes 1310720 | tf_op jit(solution)/shard_map/all_to_all | solution.py:168
  166.8 17.8 %all-to-all-done.2 = bf16[64,8,640]{2,1,0:T(8,128)(2,1)S(1)} async-done(((bf16[64,8,640]{2,1,0:T(8,128)(2,1)}), bf16[64,8,640]{2,1,0:T(8,128)(2,1)S(1)}, u32[]{:S(2)}, u32[]{:S(2)}) %all-to-all-start.2) | async-done | bytes 655392 | tf_op jit(solution)/shard_map/all_to_all | solution.py:168
  185.4 17.3 %all_to_all.25 = bf16[32,8,768]{2,1,0:T(8,128)(2,1)S(1)} all-to-all(bf16[32,8,768]{2,1,0:T(8,128)(2,1)S(1)} %pad_maximum_fusion.2), channel_id=1, replica_groups=mesh['z'=8,'y'=4,'x'=4,'core'=2] {'y','x','core'}, dimensions={0} | all-to-all | bytes 786432 | tf_op jit(solution)/shard_map/all_to_all | solution.py:179
  204.0 3.3 %all-to-all-start.4 = ((f32[8,1,128]{2,1,0:T(1,128)}), f32[8,1,128]{2,1,0:T(1,128)S(1)}, u32[]{:S(2)}, u32[]{:S(2)}) async-start(f32[8,1,128]{2,1,0:T(1,128)} %broadcast_in_dim.30), calls=%async_computation.4 | async-start | bytes 8192 | tf_op jit(solution)/shard_map/all_to_all | solution.py:189
  208.1 5.6 %all-to-all-done.4 = f32[8,1,128]{2,1,0:T(1,128)S(1)} async-done(((f32[8,1,128]{2,1,0:T(1,128)}), f32[8,1,128]{2,1,0:T(1,128)S(1)}, u32[]{:S(2)}, u32[]{:S(2)}) %all-to-all-start.4) | async-done | bytes 4128 | tf_op jit(solution)/shard_map/all_to_all | solution.py:189
  (135 shorter events, 39.7 us)
Async XLA Ops:
  7.2 94.7 %all-gather.2.cloned.1.call-start = ((), (), s32[]{:S(2)}) async-start(), calls=%async_computation.5 | async-start | bytes 14929920 | tf_op jit(solution)/shard_map/all_gather | solution.py:111
  13.6 22.8 %all-to-all-start = ((bf16[32,16,768]{2,1,0:T(8,128)(2,1)}), bf16[32,16,768]{2,1,0:T(8,128)(2,1)S(1)}, u32[]{:S(2)}, u32[]{:S(2)}) async-start(bf16[32,16,768]{2,1,0:T(8,128)(2,1)} %bitcast.5), calls=%async_computation | async-start | bytes 1572864 | tf_op jit(solution)/shard_map/all_to_all | solution.py:112
  37.1 22.2 %collective-permute-start = (bf16[64,5248]{1,0:T(8,128)(2,1)S(1)}, bf16[64,5248]{1,0:T(8,128)(2,1)S(1)}, u32[]{:S(2)}, u32[]{:S(2)}) collective-permute-start(bf16[64,5248]{1,0:T(8,128)(2,1)S(1)} %pad_maximum_fusion.1), channel_id=1, source_target_pairs={{0,32},{32,64},{64,96},{96,128},{128,160},{160,192},{192,224},{224... | collective-permute-start | bytes 2015240 | tf_op jit(solution)/shard_map/ppermute | solution.py:27
  38.8 20.5 %collective-permute-start.1 = (bf16[64,5248]{1,0:T(8,128)(2,1)S(1)}, bf16[64,5248]{1,0:T(8,128)(2,1)S(1)}, u32[]{:S(2)}, u32[]{:S(2)}) collective-permute-start(bf16[64,5248]{1,0:T(8,128)(2,1)S(1)} %pad_maximum_fusion.1), channel_id=1, source_target_pairs={{0,224},{32,0},{64,32},{96,64},{128,96},{160,128},{192,160},{224,1... | collective-permute-start | bytes 2015240 | tf_op jit(solution)/shard_map/ppermute | solution.py:27
  47.8 65.2 %all-to-all-start.1 = ((bf16[32,8,640]{2,1,0:T(8,128)(2,1)}), bf16[32,8,640]{2,1,0:T(8,128)(2,1)S(1)}, u32[]{:S(2)}, u32[]{:S(2)}) async-start(bf16[32,8,640]{2,1,0:T(8,128)(2,1)} %bitcast.11), calls=%async_computation.1 | async-start | bytes 655360 | tf_op jit(solution)/shard_map/all_to_all | solution.py:117
  59.3 17.0 %collective-permute-start.2 = (bf16[64,5248]{1,0:T(8,128)(2,1)S(1)}, bf16[64,5248]{1,0:T(8,128)(2,1)S(1)}, u32[]{:S(2)}, u32[]{:S(2)}) collective-permute-start(bf16[64,5248]{1,0:T(8,128)(2,1)S(1)} %collective-permute-done), channel_id=1, source_target_pairs={{0,32},{32,64},{64,96},{96,128},{128,160},{160,192},{192,224},{224... | collective-permute-start | bytes 2015240 | tf_op jit(solution)/shard_map/ppermute | solution.py:27
  59.3 17.0 %collective-permute-start.3 = (bf16[64,5248]{1,0:T(8,128)(2,1)S(1)}, bf16[64,5248]{1,0:T(8,128)(2,1)S(1)}, u32[]{:S(2)}, u32[]{:S(2)}) collective-permute-start(bf16[64,5248]{1,0:T(8,128)(2,1)S(1)} %collective-permute-done.1), channel_id=1, source_target_pairs={{0,224},{32,0},{64,32},{96,64},{128,96},{160,128},{192,160},{224,1... | collective-permute-start | bytes 2015240 | tf_op jit(solution)/shard_map/ppermute | solution.py:27
  76.3 16.1 %collective-permute-start.4 = (bf16[64,5248]{1,0:T(8,128)(2,1)S(1)}, bf16[64,5248]{1,0:T(8,128)(2,1)S(1)}, u32[]{:S(2)}, u32[]{:S(2)}) collective-permute-start(bf16[64,5248]{1,0:T(8,128)(2,1)S(1)} %collective-permute-done.2), channel_id=1, source_target_pairs={{0,32},{32,64},{64,96},{96,128},{128,160},{160,192},{192,224},{224... | collective-permute-start | bytes 2015240 | tf_op jit(solution)/shard_map/ppermute | solution.py:27
  76.3 16.2 %collective-permute-start.5 = (bf16[64,5248]{1,0:T(8,128)(2,1)S(1)}, bf16[64,5248]{1,0:T(8,128)(2,1)S(1)}, u32[]{:S(2)}, u32[]{:S(2)}) collective-permute-start(bf16[64,5248]{1,0:T(8,128)(2,1)S(1)} %collective-permute-done.3), channel_id=1, source_target_pairs={{0,224},{32,0},{64,32},{96,64},{128,96},{160,128},{192,160},{224,1... | collective-permute-start | bytes 2015240 | tf_op jit(solution)/shard_map/ppermute | solution.py:27
  92.4 7.9 %collective-permute-start.6 = (bf16[64,2560]{1,0:T(8,128)(2,1)S(1)}, bf16[64,2560]{1,0:T(8,128)(2,1)S(1)}, u32[]{:S(2)}, u32[]{:S(2)}) collective-permute-start(bf16[64,2560]{1,0:T(8,128)(2,1)S(1)} %slice.174), channel_id=1, source_target_pairs={{0,32},{32,64},{64,96},{96,128},{128,160},{160,192},{192,224},{224... | collective-permute-start | bytes 983048 | tf_op jit(solution)/shard_map/ppermute | solution.py:27
  92.6 8.5 %collective-permute-start.7 = (bf16[64,2688]{1,0:T(8,128)(2,1)S(1)}, bf16[64,2688]{1,0:T(8,128)(2,1)S(1)}, u32[]{:S(2)}, u32[]{:S(2)}) collective-permute-start(bf16[64,2688]{1,0:T(8,128)(2,1)S(1)} %slice.175), channel_id=1, source_target_pairs={{0,224},{32,0},{64,32},{96,64},{128,96},{160,128},{192,160},{224,1... | collective-permute-start | bytes 1032200 | tf_op jit(solution)/shard_map/ppermute | solution.py:27
  117.1 6.9 %collective-permute-start.8 = (bf16[32,2560]{1,0:T(8,128)(2,1)S(1)}, bf16[32,2560]{1,0:T(8,128)(2,1)S(1)}, u32[]{:S(2)}, u32[]{:S(2)}) collective-permute-start(bf16[32,2560]{1,0:T(8,128)(2,1)S(1)} %get-tuple-element.26), channel_id=1, source_target_pairs={{0,32},{32,64},{64,96},{96,128},{128,160},{160,192},{192,224},{224... | collective-permute-start | bytes 491528 | tf_op jit(solution)/shard_map/ppermute | solution.py:27
  117.2 6.8 %collective-permute-start.9 = (bf16[32,2560]{1,0:T(8,128)(2,1)S(1)}, bf16[32,2560]{1,0:T(8,128)(2,1)S(1)}, u32[]{:S(2)}, u32[]{:S(2)}) collective-permute-start(bf16[32,2560]{1,0:T(8,128)(2,1)S(1)} %get-tuple-element.27), channel_id=1, source_target_pairs={{0,224},{32,0},{64,32},{96,64},{128,96},{160,128},{192,160},{224,1... | collective-permute-start | bytes 491528 | tf_op jit(solution)/shard_map/ppermute | solution.py:27
  124.1 7.2 %collective-permute-start.10 = (bf16[32,5120]{1,0:T(8,128)(2,1)S(1)}, bf16[32,5120]{1,0:T(8,128)(2,1)S(1)}, u32[]{:S(2)}, u32[]{:S(2)}) collective-permute-start(bf16[32,5120]{1,0:T(8,128)(2,1)S(1)} %get-tuple-element.28), channel_id=1, source_target_pairs={{0,32},{32,64},{64,96},{96,128},{128,160},{160,192},{192,224},{224... | collective-permute-start | bytes 983048 | tf_op jit(solution)/shard_map/ppermute | solution.py:27
  124.2 7.1 %collective-permute-start.11 = (bf16[32,5120]{1,0:T(8,128)(2,1)S(1)}, bf16[32,5120]{1,0:T(8,128)(2,1)S(1)}, u32[]{:S(2)}, u32[]{:S(2)}) collective-permute-start(bf16[32,5120]{1,0:T(8,128)(2,1)S(1)} %get-tuple-element.29), channel_id=1, source_target_pairs={{0,224},{32,0},{64,32},{96,64},{128,96},{160,128},{192,160},{224,1... | collective-permute-start | bytes 983048 | tf_op jit(solution)/shard_map/ppermute | solution.py:27
  126.9 8.3 %collective-permute-start.16 = (bf16[64,2560]{1,0:T(8,128)(2,1)S(1)}, bf16[64,2560]{1,0:T(8,128)(2,1)S(1)}, u32[]{:S(2)}, u32[]{:S(2)}) collective-permute-start(bf16[64,2560]{1,0:T(8,128)(2,1)S(1)} %get-tuple-element.35), channel_id=1, source_target_pairs={{0,8},{8,16},{16,24},{24,0},{1,9},{9,17},{17,25},{25,1},{2,10},{10... | collective-permute-start | bytes 983048 | tf_op jit(solution)/shard_map/ppermute | solution.py:27
  131.5 8.9 %collective-permute-start.12 = (bf16[32,5120]{1,0:T(8,128)(2,1)S(1)}, bf16[32,5120]{1,0:T(8,128)(2,1)S(1)}, u32[]{:S(2)}, u32[]{:S(2)}) collective-permute-start(bf16[32,5120]{1,0:T(8,128)(2,1)S(1)} %get-tuple-element.30), channel_id=1, source_target_pairs={{0,32},{32,64},{64,96},{96,128},{128,160},{160,192},{192,224},{224... | collective-permute-start | bytes 983048 | tf_op jit(solution)/shard_map/ppermute | solution.py:27
  131.6 8.8 %collective-permute-start.13 = (bf16[32,5120]{1,0:T(8,128)(2,1)S(1)}, bf16[32,5120]{1,0:T(8,128)(2,1)S(1)}, u32[]{:S(2)}, u32[]{:S(2)}) collective-permute-start(bf16[32,5120]{1,0:T(8,128)(2,1)S(1)} %get-tuple-element.31), channel_id=1, source_target_pairs={{0,224},{32,0},{64,32},{96,64},{128,96},{160,128},{192,160},{224,1... | collective-permute-start | bytes 983048 | tf_op jit(solution)/shard_map/ppermute | solution.py:27
  137.7 13.1 %collective-permute-start.18 = (bf16[64,5120]{1,0:T(8,128)(2,1)S(1)}, bf16[64,5120]{1,0:T(8,128)(2,1)S(1)}, u32[]{:S(2)}, u32[]{:S(2)}) collective-permute-start(bf16[64,5120]{1,0:T(8,128)(2,1)S(1)} %get-tuple-element.37), channel_id=1, source_target_pairs={{0,8},{8,16},{16,24},{24,0},{1,9},{9,17},{17,25},{25,1},{2,10},{10... | collective-permute-start | bytes 1966088 | tf_op jit(solution)/shard_map/ppermute | solution.py:27
  139.3 11.7 %collective-permute-start.19 = (bf16[64,5120]{1,0:T(8,128)(2,1)S(1)}, bf16[64,5120]{1,0:T(8,128)(2,1)S(1)}, u32[]{:S(2)}, u32[]{:S(2)}) collective-permute-start(bf16[64,5120]{1,0:T(8,128)(2,1)S(1)} %get-tuple-element.38), channel_id=1, source_target_pairs={{0,24},{8,0},{16,8},{24,16},{1,25},{9,1},{17,9},{25,17},{2,26},{10... | collective-permute-start | bytes 1966088 | tf_op jit(solution)/shard_map/ppermute | solution.py:27
  140.6 23.7 %collective-permute-start.14 = (bf16[32,5120]{1,0:T(8,128)(2,1)S(1)}, bf16[32,5120]{1,0:T(8,128)(2,1)S(1)}, u32[]{:S(2)}, u32[]{:S(2)}) collective-permute-start(bf16[32,5120]{1,0:T(8,128)(2,1)S(1)} %get-tuple-element.32), channel_id=1, source_target_pairs={{0,32},{32,64},{64,96},{96,128},{128,160},{160,192},{192,224},{224... | collective-permute-start | bytes 983048 | tf_op jit(solution)/shard_map/ppermute | solution.py:27
  140.7 23.6 %collective-permute-start.15 = (bf16[32,5120]{1,0:T(8,128)(2,1)S(1)}, bf16[32,5120]{1,0:T(8,128)(2,1)S(1)}, u32[]{:S(2)}, u32[]{:S(2)}) collective-permute-start(bf16[32,5120]{1,0:T(8,128)(2,1)S(1)} %get-tuple-element.33), channel_id=1, source_target_pairs={{0,224},{32,0},{64,32},{96,64},{128,96},{160,128},{192,160},{224,1... | collective-permute-start | bytes 983048 | tf_op jit(solution)/shard_map/ppermute | solution.py:27
  152.0 32.6 %all-to-all-start.2 = ((bf16[64,8,640]{2,1,0:T(8,128)(2,1)}), bf16[64,8,640]{2,1,0:T(8,128)(2,1)S(1)}, u32[]{:S(2)}, u32[]{:S(2)}) async-start(bf16[64,8,640]{2,1,0:T(8,128)(2,1)} %bitcast.26), calls=%async_computation.2 | async-start | bytes 1310720 | tf_op jit(solution)/shard_map/all_to_all | solution.py:168
  204.0 9.7 %all-to-all-start.4 = ((f32[8,1,128]{2,1,0:T(1,128)}), f32[8,1,128]{2,1,0:T(1,128)S(1)}, u32[]{:S(2)}, u32[]{:S(2)}) async-start(f32[8,1,128]{2,1,0:T(1,128)} %broadcast_in_dim.30), calls=%async_computation.4 | async-start | bytes 8192 | tf_op jit(solution)/shard_map/all_to_all | solution.py:189
  (7 other events, 182.3 us)
Sparse Core Ops, SparseCore 0:
  13.7 80.3 all-gather.1
